TPU v7x, 32 devices: a whole 2x2x4 slice. The times are simulated.
32 devices in a mesh: groups: 2 (over y), mp: 4 (over x, core), dp: 4 (over z).
Axes of the slice: x: 2, y: 2, z: 4, core: 2. Of those that a mesh axis runs over, the one named last changes fastest.
Arguments:
- inputs: bfloat16 [1024, 6144], P(('groups', 'dp'), 'mp'), parts along dimension 0, may hold values from -6 to 6
- out_grad: bfloat16 [1024, 6144], P(('groups', 'dp'), 'mp'), parts along dimension 0, may hold values from -6 to 6
- up_weight: bfloat16 [4, 1536, 6144], P('mp'), may hold values from -0.15625 to 0.15625
- mix_weight: bfloat16 [4, 96, 256, 256], P(None, 'mp'), may hold values from -0.1875 to 0.1875
- output_factor_matrix: bfloat16 [4, 6144, 1536], P('mp'), may hold values from -0.078125 to 0.078125
- partner: int32 [2, 96], replicated, may hold values from 0 to 95, as said below
- local_perm: int32 [96], replicated, may hold values from 0 to 95, as said below
Outputs:
- outputs: bfloat16 [1024, 6144], P(('groups', 'dp'), 'mp'), parts along dimension 0
- input_grad: bfloat16 [1024, 6144], P(('groups', 'dp'), 'mp'), parts along dimension 0
- up_grad: float32 [8, 1536, 6144], P(('groups', 'mp'), None, 'dp'), parts along dimension 0
- mix_grad: float32 [8, 96, 256, 256], P('groups', 'mp', 'dp'), parts along dimension 0
- down_grad: float32 [8, 6144, 1536], P(('groups', 'mp'), 'dp'), parts along dimension 0
There are 2 independent parts, one for each index of `groups`. A program takes and returns all parts, laid end to end along the dimension named above; an argument that names none is the same for every part. Nothing has to cross between parts.
Inputs may be any that keep to these rules, and one draw needn't show every extreme that they name: partner[l, b] // 24 equals b // 24 with bit l flipped; each row of partner is a permutation of the blocks. local_perm[b] // 24 equals b // 24; local_perm is a permutation of the blocks.
All inputs are finite; a program needn't handle non-finite values.
Results may differ from a plain program's by a relative error of at most 0.01.
Values may be sent and summed in bfloat16 or wider, within the bound.
No kernel may reach another device: no remote copies, remote signals or barrier semaphores. Data moves between devices by JAX's collectives and lax.ppermute only.
A program may use at most 320 MiB of HBM per device.

v0:
```python
import jax
import jax.numpy as jnp
from jax import lax
from jax.sharding import PartitionSpec as P


def from_partner(value, axis, apart):
    mask = 2**apart
    pairs = [(source, source ^ mask) for source in range(lax.axis_size(axis))]
    return lax.ppermute(value, axis, pairs)


def gelu_tanh(values):
    inner = 0.7978845608028654 * (values + 0.044715 * values * values * values)
    return 0.5 * values * (1.0 + jnp.tanh(inner))


def gelu_slope(values):
    inner = 0.7978845608028654 * (values + 0.044715 * values * values * values)
    tangent = jnp.tanh(inner)
    return 0.5 * (1.0 + tangent) + 0.5 * values * (1.0 - tangent * tangent) * 0.7978845608028654 * (
        1.0 + 3.0 * 0.044715 * values * values
    )


def body(inputs, out_grad, up_weight, mix_weight, output_factor_matrix, partner, local_perm):
    row_count = inputs.shape[0]
    block_count = mix_weight.shape[1]
    block_size = mix_weight.shape[2]
    level_count = partner.shape[0]
    my_index = lax.axis_index("mp")
    my_base = my_index * block_count
    own_partner = lax.dynamic_slice_in_dim(partner, my_base, block_count, 1)
    perm_here = lax.dynamic_slice_in_dim(local_perm, my_base, block_count, 0) - my_base
    grad_scale = (row_count * lax.axis_size("dp")) ** (-0.5)
    hidden = jnp.dot(inputs, up_weight[0], preferred_element_type=jnp.float32).astype(jnp.bfloat16)
    diagonal_pieces = hidden.reshape(row_count, block_count, block_size)
    sources = [diagonal_pieces, jnp.take(diagonal_pieces, perm_here, axis=1)]
    for bit_level in range(level_count):
        received = from_partner(diagonal_pieces, "mp", bit_level)
        far_base = jnp.bitwise_xor(my_index, 1 << bit_level) * block_count
        sources.append(jnp.take(received, own_partner[bit_level] - far_base, axis=1))
    mixed_sum = jnp.zeros((row_count, block_count, block_size), jnp.float32)
    for level_pos in range(len(sources)):
        mixed_sum = mixed_sum + jnp.einsum(
            "tsk,skn->tsn",
            sources[level_pos],
            mix_weight[level_pos],
            preferred_element_type=jnp.float32,
        )
    activated = gelu_tanh(mixed_sum).astype(jnp.bfloat16)
    act_flat = activated.reshape(row_count, -1)
    outputs = (
        inputs.astype(jnp.float32)
        + jnp.dot(act_flat, output_factor_matrix[0], preferred_element_type=jnp.float32)
    ).astype(jnp.bfloat16)
    activation_grad = lax.dot_general(
        out_grad,
        output_factor_matrix[0],
        (((1,), (1,)), ((), ())),
        preferred_element_type=jnp.float32,
    )
    delta_mixed = (activation_grad * gelu_slope(mixed_sum.reshape(row_count, -1))).astype(
        jnp.bfloat16
    )
    delta_blocks = delta_mixed.reshape(row_count, block_count, block_size)
    down_part = (
        lax.dot_general(
            act_flat, out_grad, (((0,), (0,)), ((), ())), preferred_element_type=jnp.float32
        )
        * grad_scale
    )
    mix_part = (
        jnp.stack(
            [
                jnp.einsum(
                    "tsk,tsn->skn",
                    sources[level_pos],
                    delta_blocks,
                    preferred_element_type=jnp.float32,
                )
                for level_pos in range(len(sources))
            ]
        )
        * grad_scale
    )
    reverse_total = jnp.einsum(
        "tsn,skn->tsk", delta_blocks, mix_weight[0], preferred_element_type=jnp.float32
    )
    near_term = jnp.einsum(
        "tsn,skn->tsk", delta_blocks, mix_weight[1], preferred_element_type=jnp.float32
    )
    reverse_total = reverse_total + jnp.take(near_term, jnp.argsort(perm_here), axis=1)
    for bit_level in range(level_count):
        far_term = jnp.einsum(
            "tsn,skn->tsk",
            delta_blocks,
            mix_weight[2 + bit_level],
            preferred_element_type=jnp.float32,
        ).astype(jnp.bfloat16)
        received_term = from_partner(far_term, "mp", bit_level)
        far_base = jnp.bitwise_xor(my_index, 1 << bit_level) * block_count
        far_rows = lax.dynamic_slice_in_dim(partner[bit_level], far_base, block_count, 0) - my_base
        reverse_total = reverse_total + jnp.take(
            received_term, jnp.argsort(far_rows), axis=1
        ).astype(jnp.float32)
    hidden_grad = reverse_total.astype(jnp.bfloat16).reshape(row_count, -1)
    input_grad = (
        out_grad.astype(jnp.float32)
        + lax.dot_general(
            hidden_grad, up_weight[0], (((1,), (1,)), ((), ())), preferred_element_type=jnp.float32
        )
    ).astype(jnp.bfloat16)
    up_part = (
        lax.dot_general(
            inputs, hidden_grad, (((0,), (0,)), ((), ())), preferred_element_type=jnp.float32
        )
        * grad_scale
    )
    up_total, mix_total, down_total = (
        lax.psum_scatter(
            up_part[None].astype(jnp.bfloat16), "dp", scatter_dimension=2, tiled=True
        ).astype(jnp.float32),
        lax.psum_scatter(
            mix_part.astype(jnp.bfloat16), "dp", scatter_dimension=2, tiled=True
        ).astype(jnp.float32),
        lax.psum_scatter(
            down_part[None].astype(jnp.bfloat16), "dp", scatter_dimension=1, tiled=True
        ).astype(jnp.float32),
    )
    return (outputs, input_grad, up_total, mix_total, down_total)


def solution(mesh):
    return jax.shard_map(
        body,
        mesh=mesh,
        in_specs=(
            P(("groups", "dp"), "mp"),
            P(("groups", "dp"), "mp"),
            P("mp", None, None),
            P(None, "mp", None, None),
            P("mp", None, None),
            P(),
            P(),
        ),
        out_specs=(
            P(("groups", "dp"), "mp"),
            P(("groups", "dp"), "mp"),
            P(("groups", "mp"), None, "dp"),
            P("groups", "mp", "dp", None),
            P(("groups", "mp"), "dp", None),
        ),
        check_vma=False,
    )
```

profile of v0, /device:TPU:0, one launch (start us, length us, event | category | flops | bytes accessed | tf_op | source)
XLA Modules:
  0.0 960.0 jit_solution(14918395994631052281)
XLA Ops:
  7.2 9.1 fusion.17
  16.4 1.3 copy.93
  17.7 0.5 collective-permute-start
  18.2 2.5 collective-permute-start.1
  20.7 1.6 sort.45
  22.4 0.5 compare_select_fusion.4
  23.0 2.1 gather_fusion.1
  25.1 4.7 fusion.46
  29.8 4.2 fusion.42
  34.0 2.1 gather_fusion.2
  36.1 4.8 fusion.38
  40.9 15.2 %collective-permute-done.1 = bf16[128,24,256]{2,0,1:T(8,128)(2,1)} collective-permute-done((bf16[128,24,256]{2,0,1:T(8,128)(2,1)}, bf16[128,24,256]{2,0,1:T(8,128)(2,1)}, u32[]{:S(2)}, u32[]{:S(2)}) %collective-permute-start.1) | collective-permute-done | bytes 1572896 | tf_op jit(solution)/shard_map/ppermute | solution.py:10
  56.0 2.1 gather_fusion.3
  58.1 9.0 fusion.24
  67.1 3.5 copy.31
  70.6 3.6 copy.35
  74.2 10.8 %fusion.14 = bf16[128,6144]{1,0:T(8,128)(2,1)S(1)} fusion(bf16[128,1536]{1,0:T(8,128)(2,1)S(1)} %copy-done.10, bf16[1,6144,1536]{2,1,0:T(8,128)(2,1)} %param.13, f32[128,6144]{1,0:T(8,128)} %copy.35), kind=kOutput, calls=%fused_computation.21 | convolution fusion | flops 2430861312 | bytes 23986176 | tf_op jit(solution)/shard_map/dot_general | solution.py:57
  85.1 1.8 convolution_bitcast_fusion.1
  86.9 1.8 convolution_bitcast_fusion
  88.8 1.8 convolution_bitcast_fusion.2
  90.6 1.0 convolution_bitcast_fusion.3
  91.6 6.3 fusion
  98.0 1.9 copy.30
  100.0 9.8 %fusion.2 = bf16[1,6144,1536]{2,1,0:T(8,128)(2,1)} fusion(bf16[128,6144]{0,1:T(8,128)(2,1)S(1)} %bitcast.168, bf16[128,1536]{1,0:T(8,128)(2,1)S(1)} %copy-done.10), kind=kOutput, calls=%fused_computation.11 | convolution fusion | flops 2434793472 | bytes 20840448 | tf_op jit(solution)/shard_map/dot_general | solution.py:68
  109.8 0.3 reduce-scatter.4.cloned.1.call-start
  110.1 1.6 sort.47
  111.8 1.6 sort.46
  113.4 4.2 fusion.93
  117.6 1.7 collective-permute-start.3
  119.4 4.2 fusion.98
  123.7 4.7 fusion.70
  128.4 4.3 gather_fusion
  132.7 4.7 fusion.44
  137.4 16.8 %collective-permute-done.3 = bf16[128,24,256]{2,0,1:T(8,128)(2,1)} collective-permute-done((bf16[128,24,256]{2,0,1:T(8,128)(2,1)}, bf16[128,24,256]{2,0,1:T(8,128)(2,1)}, u32[]{:S(2)}, u32[]{:S(2)}) %collective-permute-start.3) | collective-permute-done | bytes 1572896 | tf_op jit(solution)/shard_map/ppermute | solution.py:10
  154.2 3.3 gather_fusion.5
  157.5 3.2 gather_fusion.4
  160.7 5.5 fusion.31
  166.2 2.0 copy.43
  168.1 9.2 fusion.1
  177.4 1.4 copy-done.8
  178.8 9.8 %fusion.62 = bf16[128,1536]{1,0:T(8,128)(2,1)} fusion(bf16[128,6144]{0,1:T(8,128)(2,1)S(1)} %bitcast.169, bf16[1,6144,1536]{2,1,0:T(8,128)(2,1)} %param.13, bf16[128,1536]{1,0:T(8,128)(2,1)S(1)} %copy-done.9), kind=kOutput, calls=%fused_computation.70 | convolution fusion | flops 2416508928 | bytes 21233664 | tf_op jit(solution)/shard_map/dot_general | solution.py:55
  188.5 13.9 %fusion.65 = bf16[128,1536]{1,0:T(8,128)(2,1)} fusion(bf16[128,6144]{0,1:T(8,128)(2,1)S(1)} %bitcast.171, bf16[1,1536,6144]{2,1,0:T(8,128)(2,1)} %param.11, bf16[128,1536]{1,0:T(8,128)(2,1)} %param.10), kind=kOutput, calls=%fused_computation.71 | convolution fusion | flops 2416508928 | bytes 21233664 | tf_op jit(solution)/shard_map/dot_general | solution.py:110
  202.4 109.1 %reduce-scatter.6.cloned.1.call-done = bf16[4,24,64,256]{3,2,1,0:T(8,128)(2,1)} async-done(((bf16[4,24,256,256]{3,2,1,0:T(8,128)(2,1)}), bf16[4,24,64,256]{3,2,1,0:T(8,128)(2,1)}) %reduce-scatter.6.cloned.1.call-update) | async-done | bytes 3145744 | tf_op jit(solution)/shard_map/reduce_scatter | solution.py:124
  311.5 5.5 convert_element_type.88
  317.0 311.7 %reduce-scatter.8.cloned.1.call-done = bf16[1,1536,1536]{2,1,0:T(8,128)(2,1)} async-done(((bf16[1,6144,1536]{2,1,0:T(8,128)(2,1)}), bf16[1,1536,1536]{2,1,0:T(8,128)(2,1)}) %reduce-scatter.8.cloned.1.call-update) | async-done | bytes 4718608 | tf_op jit(solution)/shard_map/reduce_scatter | solution.py:127
  628.7 7.4 convert_element_type.91
  636.1 310.0 %reduce-scatter.4.cloned.1.call-done = bf16[1,1536,1536]{1,2,0:T(8,128)(2,1)} async-done(((bf16[1,1536,6144]{1,2,0:T(8,128)(2,1)}), bf16[1,1536,1536]{1,2,0:T(8,128)(2,1)}) %reduce-scatter.4.cloned.1.call-update) | async-done | bytes 4718608 | tf_op jit(solution)/shard_map/reduce_scatter | solution.py:121
  946.1 7.4 copy.52
  (58 shorter events, 0.6 us)
Async XLA Ops:
  7.2 304.3 %reduce-scatter.6.cloned.1.call-start = ((), (), s32[]{:S(2)}) async-start(), calls=%async_computation.4 | async-start | bytes 15728640 | tf_op jit(solution)/shard_map/reduce_scatter | solution.py:124
  16.4 4.3 copy-start.13
  16.4 6.6 copy-start.11
  17.7 16.3 %collective-permute-start = (bf16[128,24,256]{2,0,1:T(8,128)(2,1)}, bf16[128,24,256]{2,0,1:T(8,128)(2,1)}, u32[]{:S(2)}, u32[]{:S(2)}) collective-permute-start(bf16[128,24,256]{2,0,1:T(8,128)(2,1)} %bitcast.155), channel_id=1, source_target_pairs={{0,4},{4,0},{8,12},{12,8},{1,5},{5,1},{9,13},{13,9},{2,6},{6,2},{1... | collective-permute-start | bytes 4718600 | tf_op jit(solution)/shard_map/ppermute | solution.py:10
  18.2 37.9 %collective-permute-start.1 = (bf16[128,24,256]{2,0,1:T(8,128)(2,1)}, bf16[128,24,256]{2,0,1:T(8,128)(2,1)}, u32[]{:S(2)}, u32[]{:S(2)}) collective-permute-start(bf16[128,24,256]{2,0,1:T(8,128)(2,1)} %bitcast.155), channel_id=1, source_target_pairs={{0,8},{4,12},{8,0},{12,4},{1,9},{5,13},{9,1},{13,5},{2,10},{6,14},... | collective-permute-start | bytes 4718600 | tf_op jit(solution)/shard_map/ppermute | solution.py:10
  22.4 0.6 copy-start.14
  25.1 4.7 copy-start
  36.1 4.8 copy-start.2
  58.1 9.0 copy-start.4
  70.6 3.6 copy-start.10
  74.2 10.8 %copy-start.3 = (bf16[24,128,256]{2,1,0:T(8,128)(2,1)S(1)}, bf16[24,128,256]{2,1,0:T(8,128)(2,1)}, u32[]{:S(2)}) copy-start(bf16[24,128,256]{2,1,0:T(8,128)(2,1)} %copy-done.2) | copy-start | bytes 4718596
  85.1 1.8 copy-start.5
  86.9 1.8 copy-start.1
  98.0 530.7 %reduce-scatter.8.cloned.1.call-start = ((), (), s32[]{:S(2)}) async-start(), calls=%async_computation.5 | async-start | bytes 23592960 | tf_op jit(solution)/shard_map/reduce_scatter | solution.py:127
  100.0 9.8 %copy-start.7 = (bf16[128,24,256]{0,2,1:T(8,128)(2,1)}, bf16[128,24,256]{0,2,1:T(8,128)(2,1)S(1)}, u32[]{:S(2)}) copy-start(bf16[128,24,256]{0,2,1:T(8,128)(2,1)S(1)} %copy.30) | copy-start | bytes 4718596
  109.8 836.3 %reduce-scatter.4.cloned.1.call-start = ((), (), s32[]{:S(2)}) async-start(), calls=%async_computation.3 | async-start | bytes 23592960 | tf_op jit(solution)/shard_map/reduce_scatter | solution.py:121
  117.6 6.0 copy-start.12
  117.6 6.0 copy-start.15
  117.6 36.5 %collective-permute-start.3 = (bf16[128,24,256]{2,0,1:T(8,128)(2,1)}, bf16[128,24,256]{2,0,1:T(8,128)(2,1)}, u32[]{:S(2)}, u32[]{:S(2)}) collective-permute-start(bf16[128,24,256]{2,0,1:T(8,128)(2,1)} %fusion.93), channel_id=1, source_target_pairs={{0,8},{4,12},{8,0},{12,4},{1,9},{5,13},{9,1},{13,5},{2,10},{6,14},... | collective-permute-start | bytes 4718600 | tf_op jit(solution)/shard_map/ppermute | solution.py:10
  123.6 33.8 %collective-permute-start.2 = (bf16[128,24,256]{2,0,1:T(8,128)(2,1)}, bf16[128,24,256]{2,0,1:T(8,128)(2,1)}, u32[]{:S(2)}, u32[]{:S(2)}) collective-permute-start(bf16[128,24,256]{2,0,1:T(8,128)(2,1)} %fusion.98), channel_id=1, source_target_pairs={{0,4},{4,0},{8,12},{12,8},{1,5},{5,1},{9,13},{13,9},{2,6},{6,2},{1... | collective-permute-start | bytes 4718600 | tf_op jit(solution)/shard_map/ppermute | solution.py:10
  137.4 23.3 %copy-start.6 = (f32[24,128,256]{2,1,0:T(8,128)S(1)}, f32[24,128,256]{2,1,0:T(8,128)}, u32[]{:S(2)}) copy-start(f32[24,128,256]{2,1,0:T(8,128)} %gather_fusion) | copy-start | bytes 9437188
  166.2 2.0 copy-start.9
  177.3 1.4 copy-start.8
Sparse Core Ops, SparseCore 0:
  98.1 213.3 reduce-scatter.5
  313.9 314.8 reduce-scatter.7
  631.2 314.8 reduce-scatter.3
where the time goes:
time: 961 us; the launch traced here: 960 us
  waiting for transfers between devices  763 us (79%)
  matrix products  110 us (11%)
  local copies, waits for them, and re-layouts  38.3 us (4%)
  other arithmetic  30.3 us (3%)
  between operations  14 us (1%)
    reduce_scatter x1, waiting for transfers between devices, body(): lax.psum_scatter(down_part[None].astype(jnp.bfloat16), 'dp', scatter_dime...  312 us
    reduce_scatter x1, waiting for transfers between devices, body(): lax.psum_scatter(up_part[None].astype(jnp.bfloat16), 'dp', scatter_dimens...  310 us
    reduce_scatter x1, waiting for transfers between devices, body(): lax.psum_scatter(mix_part.astype(jnp.bfloat16), 'dp', scatter_dimension=2...  109 us
    ppermute x4, waiting for transfers between devices, from_partner(): return lax.ppermute(value, axis, pairs)  31.9 us
    dot_general x4, matrix products, body(): jnp.einsum('tsk,skn->tsn', sources[level_pos], mix_weight[level_pos], pre...  22.6 us
  transfers between devices with their start and end apart: 7, of which 5 were waited for; matrix products, arithmetic and copies ran while one was open for 12% of the time, Pallas kernels for 0%

commit v1 on v0

v1 whole, which is shorter than its diff:
```python
import functools

import jax
import jax.numpy as jnp
from jax import lax
from jax.experimental import pallas as pl
from jax.experimental.pallas import tpu as pltpu
from jax.sharding import PartitionSpec as P

F32 = jnp.float32
BF16 = jnp.bfloat16
VMEM_BYTES = 56 * 1024 * 1024


def from_partner(value, axis, apart):
    mask = 2**apart
    pairs = [(source, source ^ mask) for source in range(lax.axis_size(axis))]
    return lax.ppermute(value, axis, pairs)


def rotated(value, axis, shift):
    size = lax.axis_size(axis)
    return lax.ppermute(value, axis, [(i, (i + shift) % size) for i in range(size)])


def gelu_tanh(values):
    inner = 0.7978845608028654 * (values + 0.044715 * values * values * values)
    return 0.5 * values * (1.0 + jnp.tanh(inner))


def gelu_slope(values):
    inner = 0.7978845608028654 * (values + 0.044715 * values * values * values)
    tangent = jnp.tanh(inner)
    return 0.5 * (1.0 + tangent) + 0.5 * values * (1.0 - tangent * tangent) * 0.7978845608028654 * (
        1.0 + 3.0 * 0.044715 * values * values
    )


def dot(a, b):
    return jnp.dot(a, b, preferred_element_type=F32)


def dot_nt(a, b):
    return lax.dot_general(a, b, (((1,), (1,)), ((), ())), preferred_element_type=F32)


def dot_tn(a, b):
    return lax.dot_general(a, b, (((0,), (0,)), ((), ())), preferred_element_type=F32)


def params():
    return pltpu.CompilerParams(vmem_limit_bytes=VMEM_BYTES)


def chunk_of(block_count, most):
    return max(c for c in range(1, most + 1) if block_count % c == 0)


def lanes(index, size):
    return pl.ds(pl.multiple_of(index * size, size), size)


def whole(shape):
    return pl.BlockSpec(shape, lambda i, *_: (0,) * len(shape))


def weight_specs(levels, chunk, size):
    return [
        pl.BlockSpec((1, chunk, size, size), functools.partial(lambda lv, i, *_: (lv, i, 0, 0), lv))
        for lv in levels
    ]


def mixed_near(sources, which, index, levels, mix_weight):
    rows, width = sources[0].shape
    blocks, size = mix_weight.shape[1], mix_weight.shape[2]
    chunk = chunk_of(blocks, 4)
    count = len(levels)

    def kernel(index_ref, *refs):
        source_refs, weight_refs, out_ref = refs[: len(sources)], refs[len(sources) : -1], refs[-1]
        step = pl.program_id(0)
        for c in range(chunk):
            total = None
            for k in range(count):
                picked = source_refs[which[k]][:, lanes(index_ref[k, step * chunk + c], size)]
                term = dot(picked, weight_refs[k][0, c])
                total = term if total is None else total + term
            out_ref[:, c * size : (c + 1) * size] = total

    return pl.pallas_call(
        kernel,
        grid_spec=pltpu.PrefetchScalarGridSpec(
            num_scalar_prefetch=1,
            grid=(blocks // chunk,),
            in_specs=[whole((rows, width)) for _ in sources] + weight_specs(levels, chunk, size),
            out_specs=pl.BlockSpec((rows, chunk * size), lambda i, *_: (0, i)),
        ),
        out_shape=jax.ShapeDtypeStruct((rows, width), F32),
        compiler_params=params(),
        name="mixed_near",
    )(index, *sources, *([mix_weight] * count))


def mixed_last(source, index, level, mix_weight, near, act_grad):
    rows, width = source.shape
    blocks, size = mix_weight.shape[1], mix_weight.shape[2]
    chunk = chunk_of(blocks, 4)

    def kernel(index_ref, source_ref, weight_ref, near_ref, grad_ref, mixed_ref, act_ref, delta_ref):
        step = pl.program_id(0)
        for c in range(chunk):
            here = slice(c * size, (c + 1) * size)
            picked = source_ref[:, lanes(index_ref[step * chunk + c], size)]
            total = near_ref[:, here] + dot(picked, weight_ref[0, c])
            mixed_ref[:, here] = total.astype(BF16)
            act_ref[:, here] = gelu_tanh(total).astype(BF16)
            delta_ref[:, here] = (grad_ref[:, here] * gelu_slope(total)).astype(BF16)

    columns = pl.BlockSpec((rows, chunk * size), lambda i, *_: (0, i))
    return pl.pallas_call(
        kernel,
        grid_spec=pltpu.PrefetchScalarGridSpec(
            num_scalar_prefetch=1,
            grid=(blocks // chunk,),
            in_specs=[whole((rows, width))] + weight_specs([level], chunk, size) + [columns, columns],
            out_specs=[columns] * 3,
        ),
        out_shape=[jax.ShapeDtypeStruct((rows, width), BF16)] * 3,
        compiler_params=params(),
        name="mixed_last",
    )(index, source, mix_weight, near, act_grad)


def far_terms(delta, targets, levels, mix_weight):
    rows, width = delta.shape
    blocks, size = mix_weight.shape[1], mix_weight.shape[2]
    chunk = chunk_of(blocks, 4)
    count = len(levels)

    def kernel(target_ref, delta_ref, *refs):
        step = pl.program_id(0)
        for c in range(chunk):
            here = delta_ref[:, c * size : (c + 1) * size]
            for k in range(count):
                place = lanes(target_ref[k, step * chunk + c], size)
                refs[count + k][:, place] = dot_nt(here, refs[k][0, c]).astype(BF16)

    return pl.pallas_call(
        kernel,
        grid_spec=pltpu.PrefetchScalarGridSpec(
            num_scalar_prefetch=1,
            grid=(blocks // chunk,),
            in_specs=[pl.BlockSpec((rows, chunk * size), lambda i, *_: (0, i))]
            + weight_specs(levels, chunk, size),
            out_specs=[whole((rows, width))] * count,
        ),
        out_shape=[jax.ShapeDtypeStruct((rows, width), BF16)] * count,
        compiler_params=params(),
        name="far_terms",
    )(targets, delta, *([mix_weight] * count))


def near_terms(delta, perm, mix_weight):
    rows, width = delta.shape
    blocks, size = mix_weight.shape[1], mix_weight.shape[2]
    chunk = chunk_of(blocks, 4)

    def kernel(perm_ref, delta_ref, own_ref, perm_weight_ref, out_ref):
        step = pl.program_id(0)

        @pl.when(step == 0)
        def _():
            out_ref[...] = jnp.zeros_like(out_ref)

        for c in range(chunk):
            here = delta_ref[:, c * size : (c + 1) * size]
            out_ref[:, lanes(step * chunk + c, size)] += dot_nt(here, own_ref[0, c])
            out_ref[:, lanes(perm_ref[step * chunk + c], size)] += dot_nt(here, perm_weight_ref[0, c])

    return pl.pallas_call(
        kernel,
        grid_spec=pltpu.PrefetchScalarGridSpec(
            num_scalar_prefetch=1,
            grid=(blocks // chunk,),
            in_specs=[pl.BlockSpec((rows, chunk * size), lambda i, *_: (0, i))]
            + weight_specs([0, 1], chunk, size),
            out_specs=whole((rows, width)),
        ),
        out_shape=jax.ShapeDtypeStruct((rows, width), F32),
        compiler_params=params(),
        name="near_terms",
    )(perm, delta, mix_weight, mix_weight)


def mix_gradient(mixed_all, out_grad_all, down, sources, which, index, scale):
    tokens, width = mixed_all.shape
    blocks, part, _ = sources[0].shape
    size = width // blocks
    chunk = chunk_of(blocks, 2)
    features = out_grad_all.shape[1]
    count = len(which)

    def kernel(index_ref, mixed_ref, grad_ref, down_ref, *refs):
        source_refs, out_ref = refs[:-1], refs[-1]
        step = pl.program_id(0)
        for c in range(chunk):
            here = slice(c * size, (c + 1) * size)
            act_grad = dot_nt(grad_ref[...], down_ref[here, :])
            slope = gelu_slope(mixed_ref[:, here].astype(F32))
            delta = (act_grad * slope).astype(BF16)
            picked = jnp.concatenate(
                [source_refs[which[k]][index_ref[k, step * chunk + c]] for k in range(count)], axis=0
            )
            result = dot(picked, delta) * scale
            for k in range(count):
                out_ref[k, c] = result[k * part : (k + 1) * part]

    return pl.pallas_call(
        kernel,
        grid_spec=pltpu.PrefetchScalarGridSpec(
            num_scalar_prefetch=1,
            grid=(blocks // chunk,),
            in_specs=[
                pl.BlockSpec((tokens, chunk * size), lambda i, *_: (0, i)),
                whole((tokens, features)),
                pl.BlockSpec((chunk * size, features), lambda i, *_: (i, 0)),
            ]
            + [whole((blocks, part, tokens)) for _ in sources],
            out_specs=pl.BlockSpec((count, chunk, part, size), lambda i, *_: (0, i, 0, 0)),
        ),
        out_shape=jax.ShapeDtypeStruct((count, blocks, part, size), F32),
        compiler_params=params(),
        name="mix_gradient",
    )(index, mixed_all, out_grad_all, down, *sources)


def gathered(value, axis):
    size = lax.axis_size(axis)
    me = lax.axis_index(axis)
    pieces = jnp.stack([value] + [rotated(value, axis, s) for s in range(1, size)])
    order = (me - jnp.arange(size, dtype=jnp.int32)) % size
    return jnp.take(pieces, order, axis=0, mode="clip").reshape(size * value.shape[0], value.shape[1])


def exchanged(value, axis):
    size = lax.axis_size(axis)
    me = lax.axis_index(axis)
    rows = value.shape[0]
    share = value.shape[1] // size
    pieces = []
    for s in range(size):
        piece = lax.dynamic_slice_in_dim(value, ((me + s) % size) * share, share, 1)
        pieces.append(rotated(piece, axis, s) if s else piece)
    order = (me - jnp.arange(size, dtype=jnp.int32)) % size
    return jnp.take(jnp.stack(pieces), order, axis=0, mode="clip").reshape(size * rows, share)


def body(inputs, out_grad, up_weight, mix_weight, output_factor_matrix, partner, local_perm):
    rows = inputs.shape[0]
    blocks, size = mix_weight.shape[1], mix_weight.shape[2]
    levels = partner.shape[0]
    up, down = up_weight[0], output_factor_matrix[0]
    width = up.shape[1]
    runs = lax.axis_size("dp")
    me, run = lax.axis_index("mp"), lax.axis_index("dp")
    base = me * blocks
    scale = (rows * runs) ** (-0.5)
    perm_here = lax.dynamic_slice_in_dim(local_perm, base, blocks, 0) - base
    far_here = lax.dynamic_slice_in_dim(partner, base, blocks, 1)
    far_base = jnp.stack([jnp.bitwise_xor(me, 1 << lv) * blocks for lv in range(levels)])
    far_index = far_here - far_base[:, None]
    index = jnp.concatenate(
        [jnp.arange(blocks, dtype=jnp.int32)[None], perm_here[None], far_index], axis=0
    )
    which = [0, 0] + list(range(1, levels + 1))
    last = levels + 1

    hidden = dot(inputs, up).astype(BF16)
    received = [from_partner(hidden, "mp", lv) for lv in range(levels)]
    inputs_all = gathered(inputs, "dp")
    out_grad_all = gathered(out_grad, "dp")
    act_grad = dot_nt(out_grad, down)
    near = mixed_near(
        [hidden] + received[:-1], which[:-1], index[:-1], list(range(last)), mix_weight
    )
    mixed, activated, delta = mixed_last(
        received[-1], index[-1], last, mix_weight, near, act_grad
    )
    mixed_all = lax.all_gather(mixed, "dp", axis=0, tiled=True)

    far = far_terms(delta, far_index, list(range(2, levels + 2)), mix_weight)
    far_received = [from_partner(far[lv], "mp", lv) for lv in range(levels)]
    back = near_terms(delta, perm_here, mix_weight)

    hidden_part = (
        lax.dot_general(up, inputs_all, (((0,), (1,)), ((), ())), preferred_element_type=F32)
        .astype(BF16)
        .reshape(blocks, size, runs * rows)
    )
    part = size // runs
    hidden_part = lax.dynamic_slice_in_dim(hidden_part, run * part, part, 1)
    part_received = [from_partner(hidden_part, "mp", lv) for lv in range(levels)]

    outputs = (inputs.astype(F32) + dot(activated, down)).astype(BF16)
    for term in far_received:
        back = back + term.astype(F32)
    hidden_grad = back.astype(BF16)
    hidden_grad_part = exchanged(hidden_grad, "dp")
    input_grad = (out_grad.astype(F32) + dot_nt(hidden_grad, up)).astype(BF16)
    up_grad = dot_tn(inputs_all, hidden_grad_part) * scale

    mix_grad = mix_gradient(
        mixed_all, out_grad_all, down, [hidden_part] + part_received, which, index, scale
    )
    share = width // runs
    mixed_part = lax.dynamic_slice_in_dim(mixed_all, run * share, share, 1)
    activated_part = gelu_tanh(mixed_part.astype(F32)).astype(BF16)
    down_grad = dot_tn(activated_part, out_grad_all) * scale
    return (outputs, input_grad, up_grad[None], mix_grad, down_grad[None])


def solution(mesh):
    return jax.shard_map(
        body,
        mesh=mesh,
        in_specs=(
            P(("groups", "dp"), "mp"),
            P(("groups", "dp"), "mp"),
            P("mp", None, None),
            P(None, "mp", None, None),
            P("mp", None, None),
            P(),
            P(),
        ),
        out_specs=(
            P(("groups", "dp"), "mp"),
            P(("groups", "dp"), "mp"),
            P(("groups", "mp"), None, "dp"),
            P("groups", "mp", "dp", None),
            P(("groups", "mp"), "dp", None),
        ),
        check_vma=False,
    )
```

time: 961 us -> 337 us (0.35)
  waiting for transfers between devices: 763 us -> 114 us
  Pallas kernels: 0 us -> 70.9 us
  matrix products: 110 us -> 77.8 us
  starting transfers between devices: 5.03 us -> 30.3 us
  other arithmetic: 30.3 us -> 7.1 us
  local copies, waits for them, and re-layouts: 38.3 us -> 18.3 us
    reduce_scatter x3 -> x0, waiting for transfers between devices: 731 us -> none  [the longest x1 312 us: body(): lax.psum_scatter(down_part[None].astype(jnp.bfloat16), 'dp', scatter_dime...]
    ppermute x0 -> x9, waiting for transfers between devices: none -> 105 us  [rotated(): lax.ppermute(value, axis, [(i, (i + shift) % size) for i in range(size)])]
    pallas_call x0 -> x5, Pallas kernels: none -> 70.9 us  [the longest x1 34.9 us: mix_gradient(): pl.pallas_call(kernel, grid_spec=pltpu.PrefetchScalarGridSpec(num_scalar_...]
    dot_general x18 -> x7, matrix products: 110 us -> 77.8 us  [the longest x2 27.5 us: dot_nt(): lax.dot_general(a, b, (((1,), (1,)), ((), ())), preferred_element_type=F32)]
    ppermute x0 -> x9, starting transfers between devices: none -> 25.1 us  [rotated(): lax.ppermute(value, axis, [(i, (i + shift) % size) for i in range(size)])]
    ppermute x4 -> x6, waiting for transfers between devices: 31.9 us -> 9.3 us  [from_partner(): return lax.ppermute(value, axis, pairs)]
    convert_element_type x4 -> x1, other arithmetic: 24.7 us -> 2.52 us  [body(): hidden_grad = back.astype(BF16)]
    gather x6 -> x3, local copies, waits for them, and re-layouts: 17 us -> 4.26 us  [the longest x2 2.47 us: gathered(): jnp.take(pieces, order, axis=0, mode='clip')]
  transfers between devices with their start and end apart: 7 -> 16, of which waited for: 5 -> 6; matrix products, arithmetic and copies ran while one was open for 12% -> 28% of each run, Pallas kernels for 0% -> 8%
where the time goes in v1:
time: 337 us; the launch traced here: 333 us
  waiting for transfers between devices  114 us (34%)
  matrix products  77.8 us (23%)
  Pallas kernels  70.9 us (21%)
  starting transfers between devices  30.3 us (9%)
  local copies, waits for them, and re-layouts  18.3 us (5%)
  between operations  14.2 us (4%)
  other arithmetic  7.1 us (2%)
    ppermute x9, waiting for transfers between devices, rotated(): lax.ppermute(value, axis, [(i, (i + shift) % size) for i in range(size)])  105 us
    pallas_call x1, Pallas kernels, mix_gradient(): pl.pallas_call(kernel, grid_spec=pltpu.PrefetchScalarGridSpec(num_scalar_...  34.9 us
    dot_general x2, matrix products, dot_nt(): lax.dot_general(a, b, (((1,), (1,)), ((), ())), preferred_element_type=F32)  27.5 us
    ppermute x9, starting transfers between devices, rotated(): lax.ppermute(value, axis, [(i, (i + shift) % size) for i in range(size)])  25.1 us
    dot_general x2, matrix products, dot(): return jnp.dot(a, b, preferred_element_type=F32)  19 us
    dot_general x2, matrix products, dot_tn(): lax.dot_general(a, b, (((0,), (0,)), ((), ())), preferred_element_type=F32)  15.9 us
    dot_general x1, matrix products, body(): lax.dot_general(up, inputs_all, (((0,), (1,)), ((), ())), preferred_eleme...  15.4 us
    pallas_call x1, Pallas kernels, mixed_last(): pl.pallas_call(kernel, grid_spec=pltpu.PrefetchScalarGridSpec(num_scalar_...  9.76 us
  transfers between devices with their start and end apart: 16, of which 6 were waited for; matrix products, arithmetic and copies ran while one was open for 28% of the time, Pallas kernels for 8%

profile of v1, /device:TPU:0, one launch (start us, length us, event | category | flops | bytes accessed | tf_op | source)
XLA Modules:
  0.0 333.0 jit_solution(2407341672371224359)
XLA Ops:
  7.2 0.0 all-gather.2.cloned.1.call-start
  7.2 9.2 %fusion.14.refs_0_ = bf16[128,6144]{1,0:T(8,128)(2,1)S(1)} fusion(bf16[128,1536]{1,0:T(8,128)(2,1)} %param.7, bf16[1,1536,6144]{2,1,0:T(8,128)(2,1)} %param.9), kind=kOutput, calls=%fused_computation.15 | convolution fusion | flops 2416705536 | bytes 20840448 | tf_op jit(solution)/shard_map/dot_general | solution.py:40
  16.4 0.5 collective-permute-start.1
  16.9 2.6 collective-permute-start
  19.5 0.1 pad_add_fusion.1
  19.6 0.1 fusion.36.target_ref
  19.7 0.5 slice_bitcast_fusion.index_ref
  20.2 0.1 fusion.54
  20.3 0.6 pad_add_fusion.index_ref
  20.8 14.0 %fusion.40.grad_ref = f32[128,6144]{1,0:T(8,128)} fusion(bf16[128,1536]{1,0:T(8,128)(2,1)S(1)} %copy-done.4, bf16[1,6144,1536]{2,1,0:T(8,128)(2,1)} %param.11), kind=kOutput, calls=%fused_computation.58 | convolution fusion | flops 2415919104 | bytes 22413312 | tf_op jit(solution)/shard_map/dot_general | solution.py:44
  34.9 1.1 copy-done.8
  36.0 9.3 %mixed_near.1.near_ref = f32[128,6144]{1,0:T(8,128)} custom-call(s32[3,24]{1,0:T(4,128)} %bitcast.75, bf16[128,6144]{1,0:T(8,128)(2,1)} %copy-done.1, bf16[128,6144]{1,0:T(8,128)(2,1)} %copy-done.8, bf16[4,24,256,256]{3,2,1,0:T(8,128)(2,1)} %refs_1_.1, bf16[4,24,256,256]{3,2,1,0:T(8,128)(2,1)} %refs_1_.1, bf16[4,24,256,256]{3,2,1,0:T(8,128)(2,1)} %refs_1_.1), custom_call_target="tpu_custom_call" | custom-call | tf_op jit(solution)/shard_map/mixed_near/pallas_call | solution.py:91
  45.3 9.3 %collective-permute-done.source_ref = bf16[128,6144]{1,0:T(8,128)(2,1)} collective-permute-done((bf16[128,6144]{1,0:T(8,128)(2,1)S(1)}, bf16[128,6144]{1,0:T(8,128)(2,1)}, u32[]{:S(2)}, u32[]{:S(2)}) %collective-permute-start) | collective-permute-done | bytes 1572896 | tf_op jit(solution)/shard_map/ppermute | solution.py:18
  54.6 9.8 %mixed_last.1 = (bf16[128,6144]{1,0:T(8,128)(2,1)}, bf16[128,6144]{1,0:T(8,128)(2,1)}, bf16[128,6144]{1,0:T(8,128)(2,1)}) custom-call(s32[24]{0:T(128)} %slice_bitcast_fusion.index_ref, bf16[128,6144]{1,0:T(8,128)(2,1)} %collective-permute-done.source_ref, bf16[4,24,256,256]{3,2,1,0:T(8,128)(2,1)} %refs_1_.1, f32[128,6144]{1,0:T(8,128)} %mixed_near.1.near_ref, ...), custom_call_target="tpu_custom_call" | custom-call | tf_op jit(solution)/shard_map/mixed_last/pallas_call | solution.py:121
  64.4 1.0 copy-done.5
  65.4 1.8 collective-permute-start.4
  67.2 2.0 collective-permute-start.6
  69.2 1.0 collective-permute-start.5
  70.2 1.6 collective-permute-start.10
  71.8 2.2 collective-permute-start.12
  74.1 0.6 dynamic-slice_subtract_fusion.perm_ref
  74.7 4.6 %collective-permute-done.4 = bf16[128,1536]{1,0:T(8,128)(2,1)S(1)} collective-permute-done((bf16[128,1536]{1,0:T(8,128)(2,1)S(1)}, bf16[128,1536]{1,0:T(8,128)(2,1)S(1)}, u32[]{:S(2)}, u32[]{:S(2)}) %collective-permute-start.4) | collective-permute-done | bytes 393248 | tf_op jit(solution)/shard_map/ppermute | solution.py:23
  79.2 14.4 %collective-permute-start.11 = (bf16[128,1536]{1,0:T(8,128)(2,1)S(1)}, bf16[128,1536]{1,0:T(8,128)(2,1)}, u32[]{:S(2)}, u32[]{:S(2)}) collective-permute-start(bf16[128,1536]{1,0:T(8,128)(2,1)S(1)} %copy-done.4), channel_id=1, source_target_pairs={{0,2},{1,3},{2,0},{3,1},{4,6},{5,7},{6,4},{7,5},{8,10},{9,11},{10,... | collective-permute-start | bytes 1179656 | tf_op jit(solution)/shard_map/ppermute | solution.py:23
  93.6 7.1 %collective-permute-done.6 = bf16[128,1536]{1,0:T(8,128)(2,1)S(1)} collective-permute-done((bf16[128,1536]{1,0:T(8,128)(2,1)S(1)}, bf16[128,1536]{1,0:T(8,128)(2,1)S(1)}, u32[]{:S(2)}, u32[]{:S(2)}) %collective-permute-start.6) | collective-permute-done | bytes 393248 | tf_op jit(solution)/shard_map/ppermute | solution.py:23
  100.7 44.3 %collective-permute-done.5 = bf16[128,1536]{1,0:T(8,128)(2,1)S(1)} collective-permute-done((bf16[128,1536]{1,0:T(8,128)(2,1)S(1)}, bf16[128,1536]{1,0:T(8,128)(2,1)S(1)}, u32[]{:S(2)}, u32[]{:S(2)}) %collective-permute-start.5) | collective-permute-done | bytes 393248 | tf_op jit(solution)/shard_map/ppermute | solution.py:23
  145.0 0.2 pad_maximum_fusion
  145.2 0.6 gather_fusion
  145.9 8.3 %far_terms.1 = (bf16[128,6144]{1,0:T(8,128)(2,1)}, bf16[128,6144]{1,0:T(8,128)(2,1)}) custom-call(s32[2,24]{1,0:T(2,128)} %copy-done.10, bf16[128,6144]{1,0:T(8,128)(2,1)} %get-tuple-element.11.delta_ref, bf16[4,24,256,256]{3,2,1,0:T(8,128)(2,1)} %refs_1_.1, bf16[4,24,256,256]{3,2,1,0:T(8,128)(2,1)} %refs_1_.1), custom_call_target="tpu_custom_call" | custom-call | tf_op jit(solution)/shard_map/far_terms/pallas_call | solution.py:149
  154.2 1.6 collective-permute-start.3
  155.9 15.4 %fusion.11 = bf16[6144,512]{0,1:T(8,128)(2,1)} fusion(bf16[512,1536]{1,0:T(8,128)(2,1)S(1)} %bitcast.71, bf16[1,1536,6144]{2,1,0:T(8,128)(2,1)} %param.9), kind=kOutput, calls=%fused_computation.14 | convolution fusion | flops 9666822144 | bytes 26738688 | tf_op jit(solution)/shard_map/dot_general | solution.py:297
  171.3 8.6 %copy.13 = bf16[6144,512]{1,0:T(8,128)(2,1)} copy(bf16[6144,512]{0,1:T(8,128)(2,1)} %fusion.11) | data formatting | bytes 12582912 | tf_op jit(solution)/shard_map/convert_element_type | solution.py:298
  179.9 1.5 constant_dynamic-slice_fusion.refs_0_
  181.5 0.4 collective-permute-start.14
  182.0 34.0 %collective-permute-done.11 = bf16[128,1536]{1,0:T(8,128)(2,1)} collective-permute-done((bf16[128,1536]{1,0:T(8,128)(2,1)S(1)}, bf16[128,1536]{1,0:T(8,128)(2,1)}, u32[]{:S(2)}, u32[]{:S(2)}) %collective-permute-start.11) | collective-permute-done | bytes 393248 | tf_op jit(solution)/shard_map/ppermute | solution.py:23
  216.0 1.4 pad_maximum_fusion.2
  217.4 1.8 gather_fusion.2
  219.2 8.7 %near_terms.1 = f32[128,6144]{1,0:T(8,128)} custom-call(s32[24]{0:T(128)} %dynamic-slice_subtract_fusion.perm_ref, bf16[128,6144]{1,0:T(8,128)(2,1)} %get-tuple-element.11.delta_ref, bf16[4,24,256,256]{3,2,1,0:T(8,128)(2,1)} %refs_1_.1, bf16[4,24,256,256]{3,2,1,0:T(8,128)(2,1)} %refs_1_.1), custom_call_target="tpu_custom_call" | custom-call | tf_op jit(solution)/shard_map/near_terms/pallas_call | solution.py:181
  227.9 9.9 %fusion.25 = bf16[128,1536]{1,0:T(8,128)(2,1)} fusion(bf16[128,6144]{1,0:T(8,128)(2,1)S(1)} %copy-done.7, bf16[128,1536]{1,0:T(8,128)(2,1)S(1)} %copy-done.6, bf16[1,6144,1536]{2,1,0:T(8,128)(2,1)} %param.11), kind=kOutput, calls=%fused_computation.29 | convolution fusion | flops 2416508928 | bytes 21233664 | tf_op jit(solution)/shard_map/dot_general | solution.py:40
  237.8 2.5 add_convert_fusion
  240.4 1.2 dynamic-slice_bitcast_fusion
  241.5 2.0 collective-permute-start.7
  243.6 13.4 %fusion.26 = bf16[128,1536]{1,0:T(8,128)(2,1)} fusion(bf16[128,6144]{1,0:T(8,128)(2,1)S(1)} %add_convert_fusion, bf16[1,1536,6144]{2,1,0:T(8,128)(2,1)} %param.9, bf16[128,1536]{1,0:T(8,128)(2,1)S(1)} %copy-done.4), kind=kOutput, calls=%fused_computation.30 | convolution fusion | flops 2416508928 | bytes 21233664 | tf_op jit(solution)/shard_map/dot_general | solution.py:44
  257.0 15.1 %collective-permute-done.8 = bf16[128,1536]{1,0:T(8,128)(2,1)} collective-permute-done((bf16[128,1536]{1,0:T(8,128)(2,1)}, bf16[128,1536]{1,0:T(8,128)(2,1)}, u32[]{:S(2)}, u32[]{:S(2)}) %collective-permute-start.8) | collective-permute-done | bytes 393248 | tf_op jit(solution)/shard_map/ppermute | solution.py:23
  272.1 1.5 pad_maximum_fusion.1
  273.6 1.8 gather_fusion.1
  275.4 8.4 %fusion.6 = f32[1,1536,1536]{2,1,0:T(8,128)} fusion(bf16[4,128,1536]{2,1,0:T(8,128)(2,1)} %copy-done.9, bf16[4,128,1536]{2,1,0:T(8,128)(2,1)} %gather_fusion.1), kind=kOutput, calls=%fused_computation.11 | convolution fusion | flops 2418278400 | bytes 12582912 | tf_op jit(solution)/shard_map/dot_general | solution.py:48
  283.8 7.5 %fusion.10 = f32[1,1536,1536]{2,1,0:T(8,128)} fusion(bf16[512,1536]{1,0:T(8,128)(2,1)S(1)} %bitcast.68, bf16[512,6144]{1,0:T(8,128)(2,1)} %all-gather.2.cloned.1.call-done.mixed_ref, s32[]{:T(128)S(6)} %select_n.69), kind=kOutput, calls=%fused_computation.13 | convolution fusion | flops 2426142720 | bytes 12582916 | tf_op jit(solution)/shard_map/dot_general | solution.py:48
  291.3 34.9 %mix_gradient.1 = f32[4,24,64,256]{3,2,1,0:T(8,128)} custom-call(s32[4,24]{1,0:T(4,128)} %pad_add_fusion.index_ref, bf16[512,6144]{1,0:T(8,128)(2,1)} %all-gather.2.cloned.1.call-done.mixed_ref, bf16[512,1536]{1,0:T(8,128)(2,1)} %bitcast.67, bf16[6144,1536]{1,0:T(8,128)(2,1)} %bitcast.65, bf16[24,64,512]{2,1,0:T(8,128)(2,1)} %copy-done.2, ...), custom_call_target="tpu_custom_call" | custom-call | tf_op jit(solution)/shard_map/mix_gradient/pallas_call | solution.py:219
  (42 shorter events, 0.1 us)
Async XLA Ops:
  7.2 12.4 %copy-start.12 = (s32[2,96]{1,0:T(2,128)S(1)}, s32[2,96]{1,0:T(2,128)}, u32[]{:S(2)}) copy-start(s32[2,96]{1,0:T(2,128)} %param.12) | copy-start | bytes 2308
  7.2 13.0 %copy-start.11 = (s32[96]{0:T(128)S(1)}, s32[96]{0:T(128)}, u32[]{:S(2)}) copy-start(s32[96]{0:T(128)} %param.13) | copy-start | bytes 1156
  7.2 13.7 %copy-start.4 = (bf16[128,1536]{1,0:T(8,128)(2,1)S(1)}, bf16[128,1536]{1,0:T(8,128)(2,1)}, u32[]{:S(2)}) copy-start(bf16[128,1536]{1,0:T(8,128)(2,1)} %param.8) | copy-start | bytes 1179652
  7.2 276.6 %all-gather.2.cloned.1.call-start = ((), (), s32[]{:S(2)}) async-start(), calls=%async_computation | async-start | bytes 7864320 | tf_op jit(solution)/shard_map/all_gather | solution.py:290
  16.4 18.5 %copy-start.1 = (bf16[128,6144]{1,0:T(8,128)(2,1)}, bf16[128,6144]{1,0:T(8,128)(2,1)S(1)}, u32[]{:S(2)}) copy-start(bf16[128,6144]{1,0:T(8,128)(2,1)S(1)} %fusion.14.refs_0_) | copy-start | bytes 4718596
  16.4 18.5 %collective-permute-start.1 = (bf16[128,6144]{1,0:T(8,128)(2,1)S(1)}, bf16[128,6144]{1,0:T(8,128)(2,1)S(1)}, u32[]{:S(2)}, u32[]{:S(2)}) collective-permute-start(bf16[128,6144]{1,0:T(8,128)(2,1)S(1)} %fusion.14.refs_0_), channel_id=1, source_target_pairs={{0,4},{4,0},{8,12},{12,8},{1,5},{5,1},{9,13},{13,9},{2,6},{6,2},{1... | collective-permute-start | bytes 4718600 | tf_op jit(solution)/shard_map/ppermute | solution.py:18
  16.9 37.7 %collective-permute-start = (bf16[128,6144]{1,0:T(8,128)(2,1)S(1)}, bf16[128,6144]{1,0:T(8,128)(2,1)}, u32[]{:S(2)}, u32[]{:S(2)}) collective-permute-start(bf16[128,6144]{1,0:T(8,128)(2,1)S(1)} %fusion.14.refs_0_), channel_id=1, source_target_pairs={{0,8},{4,12},{8,0},{12,4},{1,9},{5,13},{9,1},{13,5},{2,10},{6,14},... | collective-permute-start | bytes 4718600 | tf_op jit(solution)/shard_map/ppermute | solution.py:18
  19.7 15.2 %copy-start.10 = (s32[2,24]{1,0:T(2,128)}, s32[2,24]{1,0:T(2,128)S(1)}, u32[]{:S(2)}) copy-start(s32[2,24]{1,0:T(2,128)S(1)} %fusion.36.target_ref) | copy-start | bytes 580
  34.9 1.1 copy-start.8
  64.4 1.0 copy-start.5
  65.4 13.9 %collective-permute-start.4 = (bf16[128,1536]{1,0:T(8,128)(2,1)S(1)}, bf16[128,1536]{1,0:T(8,128)(2,1)S(1)}, u32[]{:S(2)}, u32[]{:S(2)}) collective-permute-start(bf16[128,1536]{1,0:T(8,128)(2,1)S(1)} %copy-done.5), channel_id=1, source_target_pairs={{0,1},{1,2},{2,3},{3,0},{4,5},{5,6},{6,7},{7,4},{8,9},{9,10},{10,1... | collective-permute-start | bytes 1179656 | tf_op jit(solution)/shard_map/ppermute | solution.py:23
  67.2 33.5 %collective-permute-start.6 = (bf16[128,1536]{1,0:T(8,128)(2,1)S(1)}, bf16[128,1536]{1,0:T(8,128)(2,1)S(1)}, u32[]{:S(2)}, u32[]{:S(2)}) collective-permute-start(bf16[128,1536]{1,0:T(8,128)(2,1)S(1)} %copy-done.5), channel_id=1, source_target_pairs={{0,3},{1,0},{2,1},{3,2},{4,7},{5,4},{6,5},{7,6},{8,11},{9,8},{10,9... | collective-permute-start | bytes 1179656 | tf_op jit(solution)/shard_map/ppermute | solution.py:23
  69.2 75.8 %collective-permute-start.5 = (bf16[128,1536]{1,0:T(8,128)(2,1)S(1)}, bf16[128,1536]{1,0:T(8,128)(2,1)S(1)}, u32[]{:S(2)}, u32[]{:S(2)}) collective-permute-start(bf16[128,1536]{1,0:T(8,128)(2,1)S(1)} %copy-done.5), channel_id=1, source_target_pairs={{0,2},{1,3},{2,0},{3,1},{4,6},{5,7},{6,4},{7,5},{8,10},{9,11},{10,... | collective-permute-start | bytes 1179656 | tf_op jit(solution)/shard_map/ppermute | solution.py:23
  70.2 111.3 %collective-permute-start.10 = (bf16[128,1536]{1,0:T(8,128)(2,1)S(1)}, bf16[128,1536]{1,0:T(8,128)(2,1)}, u32[]{:S(2)}, u32[]{:S(2)}) collective-permute-start(bf16[128,1536]{1,0:T(8,128)(2,1)S(1)} %copy-done.4), channel_id=1, source_target_pairs={{0,1},{1,2},{2,3},{3,0},{4,5},{5,6},{6,7},{7,4},{8,9},{9,10},{10,1... | collective-permute-start | bytes 1179656 | tf_op jit(solution)/shard_map/ppermute | solution.py:23
  71.8 110.1 %collective-permute-start.12 = (bf16[128,1536]{1,0:T(8,128)(2,1)S(1)}, bf16[128,1536]{1,0:T(8,128)(2,1)}, u32[]{:S(2)}, u32[]{:S(2)}) collective-permute-start(bf16[128,1536]{1,0:T(8,128)(2,1)S(1)} %copy-done.4), channel_id=1, source_target_pairs={{0,3},{1,0},{2,1},{3,2},{4,7},{5,4},{6,5},{7,6},{8,11},{9,8},{10,9... | collective-permute-start | bytes 1179656 | tf_op jit(solution)/shard_map/ppermute | solution.py:23
  79.2 136.7 %collective-permute-start.11 = (bf16[128,1536]{1,0:T(8,128)(2,1)S(1)}, bf16[128,1536]{1,0:T(8,128)(2,1)}, u32[]{:S(2)}, u32[]{:S(2)}) collective-permute-start(bf16[128,1536]{1,0:T(8,128)(2,1)S(1)} %copy-done.4), channel_id=1, source_target_pairs={{0,2},{1,3},{2,0},{3,1},{4,6},{5,7},{6,4},{7,5},{8,10},{9,11},{10,... | collective-permute-start | bytes 1179656 | tf_op jit(solution)/shard_map/ppermute | solution.py:23
  145.9 9.9 %copy-start.9 = (bf16[4,128,1536]{2,1,0:T(8,128)(2,1)}, bf16[4,128,1536]{2,1,0:T(8,128)(2,1)S(1)}, u32[]{:S(2)}) copy-start(bf16[4,128,1536]{2,1,0:T(8,128)(2,1)S(1)} %gather_fusion) | copy-start | bytes 4718596
  154.2 83.6 %collective-permute-start.2 = (bf16[128,6144]{1,0:T(8,128)(2,1)}, bf16[128,6144]{1,0:T(8,128)(2,1)}, u32[]{:S(2)}, u32[]{:S(2)}) collective-permute-start(bf16[128,6144]{1,0:T(8,128)(2,1)} %get-tuple-element.12), channel_id=1, source_target_pairs={{0,4},{4,0},{8,12},{12,8},{1,5},{5,1},{9,13},{13,9},{2,6},{6,2},{1... | collective-permute-start | bytes 4718600 | tf_op jit(solution)/shard_map/ppermute | solution.py:18
  154.2 83.6 %collective-permute-start.3 = (bf16[128,6144]{1,0:T(8,128)(2,1)}, bf16[128,6144]{1,0:T(8,128)(2,1)}, u32[]{:S(2)}, u32[]{:S(2)}) collective-permute-start(bf16[128,6144]{1,0:T(8,128)(2,1)} %get-tuple-element.13), channel_id=1, source_target_pairs={{0,8},{4,12},{8,0},{12,4},{1,9},{5,13},{9,1},{13,5},{2,10},{6,14},... | collective-permute-start | bytes 4718600 | tf_op jit(solution)/shard_map/ppermute | solution.py:18
  181.5 35.9 %copy-start.2 = (bf16[24,64,512]{2,1,0:T(8,128)(2,1)}, bf16[24,64,512]{2,1,0:T(8,128)(2,1)S(1)}, u32[]{:S(2)}) copy-start(bf16[24,64,512]{2,1,0:T(8,128)(2,1)S(1)} %constant_dynamic-slice_fusion.refs_0_) | copy-start | bytes 4718596
  181.5 109.8 %collective-permute-start.14 = (bf16[24,64,512]{2,1,0:T(8,128)(2,1)S(1)}, bf16[24,64,512]{2,1,0:T(8,128)(2,1)}, u32[]{:S(2)}, u32[]{:S(2)}) collective-permute-start(bf16[24,64,512]{2,1,0:T(8,128)(2,1)S(1)} %constant_dynamic-slice_fusion.refs_0_), channel_id=1, source_target_pairs={{0,8},{4,12},{8,0},{12,4},{1,9},{5,13},{9,1},{13,5},{2,10},{6,14},... | collective-permute-start | bytes 4718600 | tf_op jit(solution)/shard_map/ppermute | solution.py:18
  181.9 109.4 %collective-permute-start.13 = (bf16[24,64,512]{2,1,0:T(8,128)(2,1)S(1)}, bf16[24,64,512]{2,1,0:T(8,128)(2,1)}, u32[]{:S(2)}, u32[]{:S(2)}) collective-permute-start(bf16[24,64,512]{2,1,0:T(8,128)(2,1)S(1)} %constant_dynamic-slice_fusion.refs_0_), channel_id=1, source_target_pairs={{0,4},{4,0},{8,12},{12,8},{1,5},{5,1},{9,13},{13,9},{2,6},{6,2},{1... | collective-permute-start | bytes 4718600 | tf_op jit(solution)/shard_map/ppermute | solution.py:18
  219.2 8.7 %copy-start.6 = (bf16[128,1536]{1,0:T(8,128)(2,1)S(1)}, bf16[128,1536]{1,0:T(8,128)(2,1)}, u32[]{:S(2)}) copy-start(bf16[128,1536]{1,0:T(8,128)(2,1)} %param.7) | copy-start | bytes 1179652
  219.2 8.7 %copy-start.7 = (bf16[128,6144]{1,0:T(8,128)(2,1)S(1)}, bf16[128,6144]{1,0:T(8,128)(2,1)}, u32[]{:S(2)}) copy-start(bf16[128,6144]{1,0:T(8,128)(2,1)} %get-tuple-element.10) | copy-start | bytes 4718596
  227.9 9.9 %copy-start = (f32[128,6144]{1,0:T(8,128)S(1)}, f32[128,6144]{1,0:T(8,128)}, u32[]{:S(2)}) copy-start(f32[128,6144]{1,0:T(8,128)} %near_terms.1) | copy-start | bytes 9437188
  241.5 15.5 %collective-permute-start.9 = (bf16[128,1536]{1,0:T(8,128)(2,1)}, bf16[128,1536]{1,0:T(8,128)(2,1)}, u32[]{:S(2)}, u32[]{:S(2)}) collective-permute-start(bf16[128,1536]{1,0:T(8,128)(2,1)} %get-tuple-element.16), channel_id=1, source_target_pairs={{0,3},{1,0},{2,1},{3,2},{4,7},{5,4},{6,5},{7,6},{8,11},{9,8},{10,9... | collective-permute-start | bytes 1179656 | tf_op jit(solution)/shard_map/ppermute | solution.py:23
  241.5 30.5 %collective-permute-start.8 = (bf16[128,1536]{1,0:T(8,128)(2,1)}, bf16[128,1536]{1,0:T(8,128)(2,1)}, u32[]{:S(2)}, u32[]{:S(2)}) collective-permute-start(bf16[128,1536]{1,0:T(8,128)(2,1)} %get-tuple-element.17), channel_id=1, source_target_pairs={{0,2},{1,3},{2,0},{3,1},{4,6},{5,7},{6,4},{7,5},{8,10},{9,11},{10,... | collective-permute-start | bytes 1179656 | tf_op jit(solution)/shard_map/ppermute | solution.py:23
  241.5 30.5 %collective-permute-start.7 = (bf16[128,1536]{1,0:T(8,128)(2,1)}, bf16[128,1536]{1,0:T(8,128)(2,1)}, u32[]{:S(2)}, u32[]{:S(2)}) collective-permute-start(bf16[128,1536]{1,0:T(8,128)(2,1)} %get-tuple-element.18), channel_id=1, source_target_pairs={{0,1},{1,2},{2,3},{3,0},{4,5},{5,6},{6,7},{7,4},{8,9},{9,10},{10,1... | collective-permute-start | bytes 1179656 | tf_op jit(solution)/shard_map/ppermute | solution.py:23
  275.4 8.4 %copy-start.3 = (bf16[4,128,1536]{2,1,0:T(8,128)(2,1)S(1)}, bf16[4,128,1536]{2,1,0:T(8,128)(2,1)}, u32[]{:S(2)}) copy-start(bf16[4,128,1536]{2,1,0:T(8,128)(2,1)} %gather_fusion.2) | copy-start | bytes 4718596
Sparse Core Ops, SparseCore 0:
  64.5 174.6 all-gather.1

commit v2 on v1

v2 whole, which is shorter than its diff:
```python
import functools
import math

import jax
import jax.numpy as jnp
from jax import lax
from jax.experimental import pallas as pl
from jax.experimental.pallas import tpu as pltpu
from jax.sharding import PartitionSpec as P

F32 = jnp.float32
BF16 = jnp.bfloat16
VMEM_BYTES = 56 * 1024 * 1024
ANY = pl.BlockSpec(memory_space=pl.ANY)


def from_partner(value, axis, apart):
    mask = 2**apart
    pairs = [(source, source ^ mask) for source in range(lax.axis_size(axis))]
    return lax.ppermute(value, axis, pairs)


def rotated(value, axis, shift):
    size = lax.axis_size(axis)
    return lax.ppermute(value, axis, [(i, (i + shift) % size) for i in range(size)])


def gelu_tanh(values):
    inner = 0.7978845608028654 * (values + 0.044715 * values * values * values)
    return 0.5 * values * (1.0 + jnp.tanh(inner))


def gelu_slope(values):
    inner = 0.7978845608028654 * (values + 0.044715 * values * values * values)
    tangent = jnp.tanh(inner)
    return 0.5 * (1.0 + tangent) + 0.5 * values * (1.0 - tangent * tangent) * 0.7978845608028654 * (
        1.0 + 3.0 * 0.044715 * values * values
    )


def dot(a, b):
    return jnp.dot(a, b, preferred_element_type=F32)


def dot_nt(a, b):
    return lax.dot_general(a, b, (((1,), (1,)), ((), ())), preferred_element_type=F32)


def dot_tn(a, b):
    return lax.dot_general(a, b, (((0,), (0,)), ((), ())), preferred_element_type=F32)


def params():
    return pltpu.CompilerParams(vmem_limit_bytes=VMEM_BYTES)


def cost(*arrays):
    moved = sum(math.prod(a.shape) * a.dtype.itemsize for a in arrays)
    return pl.CostEstimate(flops=0, bytes_accessed=int(2.2 * moved), transcendentals=0)


def level_shape(mix_weight):
    return jax.ShapeDtypeStruct(mix_weight.shape[1:], mix_weight.dtype)


def chunk_of(block_count, most):
    return max(c for c in range(1, most + 1) if block_count % c == 0)


def lanes(index, size):
    return pl.ds(pl.multiple_of(index * size, size), size)


def whole(shape):
    return pl.BlockSpec(shape, lambda i, *_: (0,) * len(shape))


def column_half(tokens, features, half):
    return pl.BlockSpec((tokens, features), lambda i, *_: (0, half))


def weight_specs(levels, chunk, size):
    return [
        pl.BlockSpec((1, chunk, size, size), functools.partial(lambda lv, i, *_: (lv, i, 0, 0), lv))
        for lv in levels
    ]


def mixed_near(sources, which, index, levels, mix_weight, after=()):
    rows, width = sources[0].shape
    blocks, size = mix_weight.shape[1], mix_weight.shape[2]
    chunk = chunk_of(blocks, 4)
    count = len(levels)
    near_shape = jax.ShapeDtypeStruct((rows, width), F32)

    def kernel(index_ref, *refs):
        source_refs, weight_refs, out_ref = refs[: len(sources)], refs[len(sources) :], refs[-1]
        step = pl.program_id(0)
        for c in range(chunk):
            total = None
            for k in range(count):
                picked = source_refs[which[k]][:, lanes(index_ref[k, step * chunk + c], size)]
                term = dot(picked, weight_refs[k][0, c])
                total = term if total is None else total + term
            out_ref[:, c * size : (c + 1) * size] = total

    return pl.pallas_call(
        kernel,
        grid_spec=pltpu.PrefetchScalarGridSpec(
            num_scalar_prefetch=1,
            grid=(blocks // chunk,),
            in_specs=[whole((rows, width)) for _ in sources]
            + weight_specs(levels, chunk, size)
            + [ANY] * len(after),
            out_specs=pl.BlockSpec((rows, chunk * size), lambda i, *_: (0, i)),
        ),
        out_shape=near_shape,
        compiler_params=params(),
        name="mixed_near",
        cost_estimate=cost(*sources, *[level_shape(mix_weight)] * count, near_shape),
    )(index, *sources, *([mix_weight] * count), *after)


def mixed_last(source, index, level, mix_weight, near, act_grad, kept, after=()):
    rows, width = source.shape
    blocks, size = mix_weight.shape[1], mix_weight.shape[2]
    chunk = chunk_of(math.gcd(blocks, kept), 4)

    def kernel(index_ref, source_ref, weight_ref, near_ref, grad_ref, *refs):
        mixed_ref, act_ref, delta_ref = refs[-3:]
        step = pl.program_id(0)
        for c in range(chunk):
            here = slice(c * size, (c + 1) * size)
            picked = source_ref[:, lanes(index_ref[step * chunk + c], size)]
            total = near_ref[:, here] + dot(picked, weight_ref[0, c])

            @pl.when(step < kept // chunk)
            def _(total=total, here=here):
                mixed_ref[:, here] = total.astype(BF16)

            act_ref[:, here] = gelu_tanh(total).astype(BF16)
            delta_ref[:, here] = (grad_ref[:, here] * gelu_slope(total)).astype(BF16)

    columns = pl.BlockSpec((rows, chunk * size), lambda i, *_: (0, i))
    return pl.pallas_call(
        kernel,
        grid_spec=pltpu.PrefetchScalarGridSpec(
            num_scalar_prefetch=1,
            grid=(blocks // chunk,),
            in_specs=[whole((rows, width))] + weight_specs([level], chunk, size)
            + [columns, columns]
            + [ANY] * len(after),
            out_specs=[
                pl.BlockSpec((rows, chunk * size), lambda i, *_: (0, jnp.minimum(i, kept // chunk - 1))),
                columns,
                columns,
            ],
        ),
        out_shape=[jax.ShapeDtypeStruct((rows, kept * size), BF16)]
        + [jax.ShapeDtypeStruct((rows, width), BF16)] * 2,
        compiler_params=params(),
        name="mixed_last",
        cost_estimate=cost(source, level_shape(mix_weight), near, act_grad, source, source),
    )(index, source, mix_weight, near, act_grad, *after)


def far_terms(delta, targets, levels, mix_weight):
    rows, width = delta.shape
    blocks, size = mix_weight.shape[1], mix_weight.shape[2]
    chunk = chunk_of(blocks, 4)
    count = len(levels)

    def kernel(target_ref, delta_ref, *refs):
        step = pl.program_id(0)
        for c in range(chunk):
            here = delta_ref[:, c * size : (c + 1) * size]
            for k in range(count):
                place = lanes(target_ref[k, step * chunk + c], size)
                refs[count + k][:, place] = dot_nt(here, refs[k][0, c]).astype(BF16)

    return pl.pallas_call(
        kernel,
        grid_spec=pltpu.PrefetchScalarGridSpec(
            num_scalar_prefetch=1,
            grid=(blocks // chunk,),
            in_specs=[pl.BlockSpec((rows, chunk * size), lambda i, *_: (0, i))]
            + weight_specs(levels, chunk, size),
            out_specs=[whole((rows, width))] * count,
        ),
        out_shape=[jax.ShapeDtypeStruct((rows, width), BF16)] * count,
        compiler_params=params(),
        name="far_terms",
        cost_estimate=cost(delta, *[level_shape(mix_weight), delta] * count),
    )(targets, delta, *([mix_weight] * count))


def near_terms(delta, perm, mix_weight, after=()):
    rows, width = delta.shape
    blocks, size = mix_weight.shape[1], mix_weight.shape[2]
    chunk = chunk_of(blocks, 4)

    def kernel(perm_ref, delta_ref, own_ref, perm_weight_ref, *refs):
        out_ref = refs[-1]
        step = pl.program_id(0)

        @pl.when(step == 0)
        def _():
            out_ref[...] = jnp.zeros_like(out_ref)

        for c in range(chunk):
            here = delta_ref[:, c * size : (c + 1) * size]
            out_ref[:, lanes(step * chunk + c, size)] += dot_nt(here, own_ref[0, c])
            out_ref[:, lanes(perm_ref[step * chunk + c], size)] += dot_nt(here, perm_weight_ref[0, c])

    return pl.pallas_call(
        kernel,
        grid_spec=pltpu.PrefetchScalarGridSpec(
            num_scalar_prefetch=1,
            grid=(blocks // chunk,),
            in_specs=[pl.BlockSpec((rows, chunk * size), lambda i, *_: (0, i))]
            + weight_specs([0, 1], chunk, size)
            + [ANY] * len(after),
            out_specs=whole((rows, width)),
        ),
        out_shape=jax.ShapeDtypeStruct((rows, width), F32),
        compiler_params=params(),
        name="near_terms",
        cost_estimate=cost(delta, delta, delta, *[level_shape(mix_weight)] * 2),
    )(perm, delta, mix_weight, mix_weight, *after)


def dense(left, right, out_type, right_transposed=False, after=()):
    rows, depth = left.shape
    width = right.shape[0] if right_transposed else right.shape[1]
    step = chunk_of(width // 128, 12) * 128
    out_shape = jax.ShapeDtypeStruct((rows, width), out_type)
    if right_transposed:
        right_spec = pl.BlockSpec((step, depth), lambda i: (i, 0))
    else:
        right_spec = pl.BlockSpec((depth, step), lambda i: (0, i))

    def kernel(left_ref, right_ref, *refs):
        product = (dot_nt if right_transposed else dot)(left_ref[...], right_ref[...])
        refs[-1][...] = product.astype(out_type)

    return pl.pallas_call(
        kernel,
        grid=(width // step,),
        in_specs=[whole((rows, depth)), right_spec] + [ANY] * len(after),
        out_specs=pl.BlockSpec((rows, step), lambda i: (0, i)),
        out_shape=out_shape,
        compiler_params=params(),
        name="dense_nt" if right_transposed else "dense",
        cost_estimate=cost(left, right, out_shape),
    )(left, right, *after)


def dense_added(left, right, base, right_transposed=False, after=()):
    rows, depth = left.shape
    width = base.shape[1]
    step = chunk_of(depth // 128, 12) * 128
    if right_transposed:
        right_spec = pl.BlockSpec((width, step), lambda i: (0, i))
    else:
        right_spec = pl.BlockSpec((step, width), lambda i: (i, 0))

    def kernel(left_ref, right_ref, base_ref, *refs):
        out_ref, total_ref = refs[-2], refs[-1]
        here = pl.program_id(0)

        @pl.when(here == 0)
        def _():
            total_ref[...] = base_ref[...].astype(F32)

        total_ref[...] += (dot_nt if right_transposed else dot)(left_ref[...], right_ref[...])

        @pl.when(here == depth // step - 1)
        def _():
            out_ref[...] = total_ref[...].astype(out_ref.dtype)

    return pl.pallas_call(
        kernel,
        grid=(depth // step,),
        in_specs=[pl.BlockSpec((rows, step), lambda i: (0, i)), right_spec, whole(base.shape)]
        + [ANY] * len(after),
        out_specs=whole(base.shape),
        out_shape=jax.ShapeDtypeStruct(base.shape, base.dtype),
        scratch_shapes=[pltpu.VMEM(base.shape, F32)],
        compiler_params=params(),
        name="added_nt" if right_transposed else "added",
        cost_estimate=cost(left, right, base),
    )(left, right, base, *after)


def hidden_rows(up, gathered, run, places, blocks, kept, part, after=()):
    depth, width = up.shape
    tokens = gathered.shape[0]
    size = width // blocks
    chunk = chunk_of(blocks, 4)
    levels = places.shape[0]
    again = blocks - kept
    sent = jax.ShapeDtypeStruct((again * size + kept * part, tokens), BF16)

    def kernel(run_ref, place_ref, up_ref, inputs_ref, *refs):
        whole_ref, out_ref = refs[-3 - levels : -1 - levels]
        sent_refs, full_ref = refs[-1 - levels : -1], refs[-1]
        full_ref[...] = lax.dot_general(
            up_ref[...], inputs_ref[...], (((0,), (1,)), ((), ())), preferred_element_type=F32
        )
        for c in range(chunk):
            first = pl.multiple_of(run_ref[0] * part, part) + c * size
            whole_ref[c] = full_ref[c * size : (c + 1) * size].astype(BF16)
            out_ref[c] = full_ref[pl.ds(first, part), :].astype(BF16)
            for lv in range(levels):
                place = place_ref[lv, pl.program_id(0) * chunk + c]

                if again:

                    @pl.when(place >= kept)
                    def _(place=place, lv=lv, c=c):
                        there = pl.multiple_of((place - kept) * size, size)
                        sent_refs[lv][pl.ds(there, size), :] = whole_ref[c]

                @pl.when(place < kept)
                def _(place=place, lv=lv, c=c):
                    there = pl.multiple_of(again * size + place * part, part)
                    sent_refs[lv][pl.ds(there, part), :] = out_ref[c]

    return pl.pallas_call(
        kernel,
        grid_spec=pltpu.PrefetchScalarGridSpec(
            num_scalar_prefetch=2,
            grid=(blocks // chunk,),
            in_specs=[
                pl.BlockSpec((depth, chunk * size), lambda i, *_: (0, i)),
                column_half(tokens, depth, 0),
            ]
            + [ANY] * len(after),
            out_specs=[
                pl.BlockSpec((chunk, size, tokens), lambda i, *_: (i, 0, 0)),
                pl.BlockSpec((chunk, part, tokens), lambda i, *_: (i, 0, 0)),
            ]
            + [whole(sent.shape)] * levels,
            scratch_shapes=[pltpu.VMEM((chunk * size, tokens), F32)],
        ),
        out_shape=[
            jax.ShapeDtypeStruct((blocks, size, tokens), BF16),
            jax.ShapeDtypeStruct((blocks, part, tokens), BF16),
        ]
        + [sent] * levels,
        compiler_params=params(),
        name="hidden_rows",
        cost_estimate=cost(up, jax.ShapeDtypeStruct((blocks, size, tokens), BF16)),
    )(run, places, up, gathered, *after)


def down_pass(activated, down, base, gathered, kept, after=()):
    rows, width = activated.shape
    features = down.shape[1]
    tokens = gathered.shape[0]
    step = chunk_of(math.gcd(width, kept) // 128, 8) * 128

    def kernel(act_ref, down_ref, base_ref, all_ref, *refs):
        out_ref, grad_ref, total_ref = refs[-3:]
        here = pl.program_id(0)

        @pl.when(here == 0)
        def _():
            total_ref[...] = base_ref[...].astype(F32)

        total_ref[...] += dot(act_ref[...], down_ref[...])

        @pl.when(here < kept // step)
        def _():
            grad_ref[...] = dot_nt(all_ref[...], down_ref[...])

        @pl.when(here == width // step - 1)
        def _():
            out_ref[...] = total_ref[...].astype(BF16)

    return pl.pallas_call(
        kernel,
        grid=(width // step,),
        in_specs=[
            pl.BlockSpec((rows, step), lambda i: (0, i)),
            pl.BlockSpec((step, features), lambda i: (i, 0)),
            whole((rows, features)),
            column_half(tokens, features, 1),
        ]
        + [ANY] * len(after),
        out_specs=[
            whole((rows, features)),
            pl.BlockSpec((tokens, step), lambda i: (0, jnp.minimum(i, kept // step - 1))),
        ],
        out_shape=[
            jax.ShapeDtypeStruct((rows, features), BF16),
            jax.ShapeDtypeStruct((tokens, kept), F32),
        ],
        scratch_shapes=[pltpu.VMEM((rows, features), F32)],
        compiler_params=params(),
        name="down_pass",
        cost_estimate=cost(activated, down, jax.ShapeDtypeStruct((tokens, kept), F32)),
    )(activated, down, base, gathered, *after)


def mix_gradient(mixed_all, act_grad_all, hidden_part, received, perm, scale, made=None):
    tokens, width = mixed_all.shape
    blocks, part, _ = hidden_part.shape
    size = part * lax.axis_size("dp")
    kept = width // size
    chunk = chunk_of(kept, 4)
    count = 2 + len(received)
    given = pl.BlockSpec(
        (kept * part, tokens), lambda i, *_: ((blocks - kept) * size // (kept * part), 0)
    )

    def kernel(perm_ref, mixed_ref, grad_ref, part_ref, *refs):
        given_refs, out_ref = refs[: len(received)], refs[-1]
        step = pl.program_id(0)
        for c in range(chunk):
            here = slice(c * size, (c + 1) * size)
            block = step * chunk + c
            slope = gelu_slope(mixed_ref[:, here].astype(F32))
            delta = (grad_ref[:, here] * slope).astype(BF16)
            rows = pl.ds(pl.multiple_of(block * part, part), part)
            picked = jnp.concatenate(
                [part_ref[block], part_ref[perm_ref[block]]] + [ref[rows, :] for ref in given_refs],
                axis=0,
            )
            result = dot(picked, delta) * scale
            for k in range(count):
                out_ref[k, c] = result[k * part : (k + 1) * part]

    columns = pl.BlockSpec((tokens, chunk * size), lambda i, *_: (0, i))
    return pl.pallas_call(
        kernel,
        grid_spec=pltpu.PrefetchScalarGridSpec(
            num_scalar_prefetch=1,
            grid=(kept // chunk,),
            in_specs=[columns, columns, whole(hidden_part.shape)]
            + [given] * len(received)
            + ([] if made is None else [ANY]),
            out_specs=pl.BlockSpec((count, chunk, part, size), lambda i, *_: (0, i, 0, 0)),
        ),
        out_shape=jax.ShapeDtypeStruct((count, blocks, part, size), F32),
        input_output_aliases={} if made is None else {4 + len(received): 0},
        compiler_params=params(),
        name="mix_gradient",
        cost_estimate=cost(mixed_all, act_grad_all),
    )(perm, mixed_all, act_grad_all, hidden_part, *received, *([] if made is None else [made]))


def recomputed(hidden_all, received, again, index, down, gathered, run, mix_weight, scale, after=()):
    blocks, size, tokens = hidden_all.shape
    count = mix_weight.shape[0]
    kept = blocks - again
    part = size // lax.axis_size("dp")
    features = down.shape[1]

    def kernel(index_ref, run_ref, *refs):
        source_refs, weight_refs = refs[:count], refs[count : 2 * count]
        down_ref, grad_ref = refs[2 * count : 2 * count + 2]
        out_ref, act_ref = refs[-2:]
        mixed = None
        sources = [ref.at[0] if k < 2 else ref for k, ref in enumerate(source_refs)]
        for k in range(count):
            term = dot_tn(weight_refs[k][0, 0], sources[k][...])
            mixed = term if mixed is None else mixed + term
        act_ref[0] = gelu_tanh(mixed).astype(BF16)
        act_grad = dot_nt(down_ref[...], grad_ref[...])
        delta = (act_grad * gelu_slope(mixed)).astype(BF16)
        first = pl.multiple_of(run_ref[0] * part, part)
        picked = jnp.concatenate(
            [sources[k][pl.ds(first, part), :] for k in range(count)], axis=0
        )
        result = dot_nt(picked, delta) * scale
        for k in range(count):
            out_ref[k, 0] = result[k * part : (k + 1) * part]

    source_specs = [
        pl.BlockSpec((1, size, tokens), lambda i, *_: (kept + i, 0, 0)),
        pl.BlockSpec((1, size, tokens), lambda i, index, run: (index[kept + i], 0, 0)),
    ] + [pl.BlockSpec((size, tokens), lambda i, *_: (i, 0))] * len(received)
    level_specs = [
        pl.BlockSpec(
            (1, 1, size, size), functools.partial(lambda k, i, *_: (k, kept + i, 0, 0), k)
        )
        for k in range(count)
    ]
    return pl.pallas_call(
        kernel,
        grid_spec=pltpu.PrefetchScalarGridSpec(
            num_scalar_prefetch=2,
            grid=(again,),
            in_specs=source_specs
            + level_specs
            + [
                pl.BlockSpec((size, features), lambda i, *_: (kept + i, 0)),
                column_half(tokens, features, 1),
            ]
            + [ANY] * len(after),
            out_specs=[
                pl.BlockSpec((count, 1, part, size), lambda i, *_: (0, kept + i, 0, 0)),
                pl.BlockSpec((1, size, tokens), lambda i, *_: (i, 0, 0)),
            ],
        ),
        out_shape=[
            jax.ShapeDtypeStruct((count, blocks, part, size), F32),
            jax.ShapeDtypeStruct((again, size, tokens), BF16),
        ],
        compiler_params=params(),
        name="recomputed",
        cost_estimate=cost(*received, *received, gathered, level_shape(mix_weight)),
    )(
        index, run, hidden_all, hidden_all, *received, *([mix_weight] * count), down, gathered,
        *after,
    )


def up_gradient(gathered, height, pieces, run_rows, scale, after=()):
    tokens = gathered.shape[0]
    rows, width = pieces[0].shape
    runs = len(pieces)
    step = chunk_of(height // 128, 4) * 128

    def kernel(run_ref, inputs_ref, *refs):
        out_ref, all_ref = refs[-2:]

        @pl.when(pl.program_id(0) == 0)
        def _():
            for s in range(runs):
                first = pl.multiple_of(run_ref[s] * rows, rows)
                all_ref[pl.ds(first, rows), :] = refs[s][...]

        out_ref[...] = dot_tn(inputs_ref[...], all_ref[...]) * scale

    return pl.pallas_call(
        kernel,
        grid_spec=pltpu.PrefetchScalarGridSpec(
            num_scalar_prefetch=1,
            grid=(height // step,),
            in_specs=[pl.BlockSpec((tokens, step), lambda i, *_: (0, i))]
            + [whole((rows, width))] * runs
            + [ANY] * len(after),
            out_specs=pl.BlockSpec((step, width), lambda i, *_: (i, 0)),
            scratch_shapes=[pltpu.VMEM((tokens, width), BF16)],
        ),
        out_shape=jax.ShapeDtypeStruct((height, width), F32),
        compiler_params=params(),
        name="up_gradient",
        cost_estimate=cost(gathered, jax.ShapeDtypeStruct((height, width), F32)),
    )(run_rows, gathered, *pieces, *after)


def down_gradient(mixed_all, gathered, run, share, scale, after=()):
    tokens, width = gathered.shape[0], gathered.shape[1] // 2
    if share % 128 == 0:
        step = chunk_of(share // 128, 4) * 128
        first = run * (share // step)
    else:
        mixed_all = lax.dynamic_slice_in_dim(mixed_all, run * share, share, 1)
        step, first = share, run * 0

    def kernel(first_ref, mixed_ref, right_ref, *refs):
        activated = gelu_tanh(mixed_ref[...].astype(F32)).astype(BF16)
        refs[-1][...] = dot_tn(activated, right_ref[...]) * scale

    return pl.pallas_call(
        kernel,
        grid_spec=pltpu.PrefetchScalarGridSpec(
            num_scalar_prefetch=1,
            grid=(share // step,),
            in_specs=[
                pl.BlockSpec((tokens, step), lambda i, first: (0, first[0] + i)),
                column_half(tokens, width, 1),
            ]
            + [ANY] * len(after),
            out_specs=pl.BlockSpec((step, width), lambda i, *_: (i, 0)),
        ),
        out_shape=jax.ShapeDtypeStruct((share, width), F32),
        compiler_params=params(),
        name="down_gradient",
        cost_estimate=cost(gathered, jax.ShapeDtypeStruct((share, width), F32)),
    )(first[None], mixed_all, gathered, *after)


def down_gradient_split(mixed_all, act_rest, gathered, run, share, scale, after=()):
    tokens, width = gathered.shape[0], gathered.shape[1] // 2
    again, size, _ = act_rest.shape
    kept = mixed_all.shape[1] // size
    count = share // size

    def kernel(run_ref, mixed_ref, act_ref, right_ref, *refs):
        out_ref = refs[-1]
        block = run_ref[0] * count + pl.program_id(0)

        @pl.when(block < kept)
        def _():
            activated = gelu_tanh(mixed_ref[...].astype(F32)).astype(BF16)
            out_ref[...] = dot_tn(activated, right_ref[...]) * scale

        @pl.when(block >= kept)
        def _():
            out_ref[...] = dot(act_ref[0], right_ref[...]) * scale

    return pl.pallas_call(
        kernel,
        grid_spec=pltpu.PrefetchScalarGridSpec(
            num_scalar_prefetch=1,
            grid=(count,),
            in_specs=[
                pl.BlockSpec(
                    (tokens, size), lambda i, run: (0, jnp.minimum(run[0] * count + i, kept - 1))
                ),
                pl.BlockSpec(
                    (1, size, tokens),
                    lambda i, run: (jnp.clip(run[0] * count + i - kept, 0, again - 1), 0, 0),
                ),
                column_half(tokens, width, 1),
            ]
            + [ANY] * len(after),
            out_specs=pl.BlockSpec((size, width), lambda i, *_: (i, 0)),
        ),
        out_shape=jax.ShapeDtypeStruct((share, width), F32),
        compiler_params=params(),
        name="down_gradient_split",
        cost_estimate=cost(gathered, jax.ShapeDtypeStruct((share, width), F32)),
    )(run, mixed_all, act_rest, gathered, *after)


def exchanged(value, axis):
    size = lax.axis_size(axis)
    me = lax.axis_index(axis)
    share = value.shape[1] // size
    pieces = []
    for s in range(size):
        piece = lax.dynamic_slice_in_dim(value, ((me + s) % size) * share, share, 1)
        pieces.append(rotated(piece, axis, s) if s else piece)
    return pieces


def body(inputs, out_grad, up_weight, mix_weight, output_factor_matrix, partner, local_perm):
    rows = inputs.shape[0]
    blocks, size = mix_weight.shape[1], mix_weight.shape[2]
    levels = partner.shape[0]
    up, down = up_weight[0], output_factor_matrix[0]
    width = up.shape[1]
    runs = lax.axis_size("dp")
    me, run = lax.axis_index("mp"), lax.axis_index("dp")
    base = me * blocks
    scale = (rows * runs) ** (-0.5)
    run_rows = ((run - jnp.arange(runs, dtype=jnp.int32)) % runs).astype(jnp.int32)
    perm_here = lax.dynamic_slice_in_dim(local_perm, base, blocks, 0) - base
    far_here = lax.dynamic_slice_in_dim(partner, base, blocks, 1)
    far_base = jnp.stack([jnp.bitwise_xor(me, 1 << lv) * blocks for lv in range(levels)])
    far_index = far_here - far_base[:, None]
    index = jnp.concatenate(
        [jnp.arange(blocks, dtype=jnp.int32)[None], perm_here[None], far_index], axis=0
    )
    which = [0, 0] + list(range(1, levels + 1))
    last = levels + 1
    part, share = size // runs, width // runs

    again = blocks // 3 if share % size == 0 else 0
    kept = blocks - again
    theirs = jnp.stack(
        [
            lax.dynamic_slice_in_dim(partner[lv], far_base[lv], blocks, 0) - base
            for lv in range(levels)
        ]
    )

    order = jnp.arange(blocks, dtype=jnp.int32)
    places = jnp.sum(
        jnp.where(theirs[:, None, :] == order[None, :, None], order[None, None, :], 0),
        axis=2,
        dtype=jnp.int32,
    )

    gathered = lax.all_gather(
        jnp.concatenate([inputs, out_grad], axis=1), "dp", axis=0, tiled=True
    )
    hidden = dense(inputs, up, BF16)
    received = [from_partner(hidden, "mp", lv) for lv in range(levels)]
    act_grad = dense(out_grad, down, F32, True, after=received[:-1])
    near = mixed_near(
        [hidden] + received[:-1], which[:-1], index[:-1], list(range(last)), mix_weight,
        after=(act_grad,),
    )
    mixed, activated, delta = mixed_last(
        received[-1], index[-1], last, mix_weight, near, act_grad, kept
    )
    mixed_all = lax.all_gather(mixed, "dp", axis=0, tiled=True)
    far = far_terms(delta, far_index, list(range(2, levels + 2)), mix_weight)
    far_received = [from_partner(far[lv], "mp", lv) for lv in range(levels)]
    hidden_all, hidden_part, *sent = hidden_rows(
        up, gathered, run[None], places, blocks, kept, part, after=far[:1]
    )
    sources = [from_partner(sent[lv], "mp", lv) for lv in range(levels)]
    back = near_terms(delta, perm_here, mix_weight, after=(hidden_part,))
    outputs, act_grad_all = down_pass(
        activated, down, inputs, gathered, kept * size, after=(back,)
    )

    for term in far_received:
        back = back + term.astype(F32)
    hidden_grad = back.astype(BF16)
    hidden_grad_pieces = exchanged(hidden_grad, "dp")
    input_grad = dense_added(hidden_grad, up, out_grad, True, after=(outputs,))
    made, act_rest = None, input_grad
    if again:
        made, act_rest = recomputed(
            hidden_all, sources, again, perm_here, down, gathered, run[None], mix_weight,
            scale, after=(input_grad,),
        )
    up_grad = up_gradient(
        gathered, up.shape[0], hidden_grad_pieces, run_rows, scale, after=(act_rest,)
    )
    if again:
        down_grad = down_gradient_split(
            mixed_all, act_rest, gathered, run[None], share, scale, after=(up_grad,)
        )
    else:
        down_grad = down_gradient(mixed_all, gathered, run, share, scale, after=(up_grad,))
    mix_grad = mix_gradient(
        mixed_all, act_grad_all, hidden_part, sources, perm_here, scale, made
    )
    return (outputs, input_grad, up_grad[None], mix_grad, down_grad[None])


def solution(mesh):
    return jax.shard_map(
        body,
        mesh=mesh,
        in_specs=(
            P(("groups", "dp"), "mp"),
            P(("groups", "dp"), "mp"),
            P("mp", None, None),
            P(None, "mp", None, None),
            P("mp", None, None),
            P(),
            P(),
        ),
        out_specs=(
            P(("groups", "dp"), "mp"),
            P(("groups", "dp"), "mp"),
            P(("groups", "mp"), None, "dp"),
            P("groups", "mp", "dp", None),
            P(("groups", "mp"), "dp", None),
        ),
        check_vma=False,
    )
```

time: 337 us -> 234 us (0.69)
  matrix products: 77.8 us -> 0 us
  Pallas kernels: 70.9 us -> 148 us
  waiting for transfers between devices: 114 us -> 46.5 us
  starting transfers between devices: 30.3 us -> 10.4 us
  local copies, waits for them, and re-layouts: 18.3 us -> 4.82 us
    ppermute x9 -> x3, waiting for transfers between devices: 105 us -> 0.01 us  [rotated(): lax.ppermute(value, axis, [(i, (i + shift) % size) for i in range(size)])]
    pallas_call x0 -> x8, Pallas kernels: none -> 99 us  [the longest x2 20.1 us: dense(): pl.pallas_call(kernel, grid=(width // step,), in_specs=[whole((rows, dept...]
    dot_general x7 -> x0, matrix products: 77.8 us -> none  [the longest x2 27.5 us: dot_nt(): lax.dot_general(a, b, (((1,), (1,)), ((), ())), preferred_element_type=F32)]
    ppermute x6, waiting for transfers between devices: 9.3 us -> 46.5 us  [from_partner(): return lax.ppermute(value, axis, pairs)]
    pallas_call x1, Pallas kernels: 34.9 us -> 12.1 us  [mix_gradient(): pl.pallas_call(kernel, grid_spec=pltpu.PrefetchScalarGridSpec(num_scalar_...]
    ppermute x9 -> x3, starting transfers between devices: 25.1 us -> 4.91 us  [rotated(): lax.ppermute(value, axis, [(i, (i + shift) % size) for i in range(size)])]
    convert_element_type x1 -> x0, local copies, waits for them, and re-layouts: 8.64 us -> none  [body(): hidden_part = lax.dot_general(up, inputs_all, (((0,), (1,)), ((), ())), p...]
    gather x3 -> x0, local copies, waits for them, and re-layouts: 4.26 us -> none  [the longest x2 2.47 us: gathered(): jnp.take(pieces, order, axis=0, mode='clip')]
  transfers between devices with their start and end apart: 16 -> 11, of which waited for: 6 -> 3; matrix products, arithmetic and copies ran while one was open for 28% -> 3% of each run, Pallas kernels for 8% -> 55%
where the time goes in v2:
time: 234 us; the launch traced here: 232 us
  Pallas kernels  148 us (63%)
  waiting for transfers between devices  46.5 us (20%)
  between operations  14.1 us (6%)
  starting transfers between devices  10.4 us (4%)
  other arithmetic  8.16 us (3%)
  local copies, waits for them, and re-layouts  4.82 us (2%)
    ppermute x6, waiting for transfers between devices, from_partner(): return lax.ppermute(value, axis, pairs)  46.5 us
    pallas_call x2, Pallas kernels, dense(): pl.pallas_call(kernel, grid=(width // step,), in_specs=[whole((rows, dept...  20.1 us
    pallas_call x1, Pallas kernels, hidden_rows(): pl.pallas_call(kernel, grid_spec=pltpu.PrefetchScalarGridSpec(num_scalar_...  19.7 us
    pallas_call x1, Pallas kernels, down_pass(): pl.pallas_call(kernel, grid=(width // step,), in_specs=[pl.BlockSpec((row...  16.9 us
    pallas_call x1, Pallas kernels, recomputed(): pl.pallas_call(kernel, grid_spec=pltpu.PrefetchScalarGridSpec(num_scalar_...  15.4 us
    pallas_call x1, Pallas kernels, mix_gradient(): pl.pallas_call(kernel, grid_spec=pltpu.PrefetchScalarGridSpec(num_scalar_...  12.1 us
    pallas_call x1, Pallas kernels, dense_added(): pl.pallas_call(kernel, grid=(depth // step,), in_specs=[pl.BlockSpec((row...  11 us
    pallas_call x1, Pallas kernels, mixed_last(): pl.pallas_call(kernel, grid_spec=pltpu.PrefetchScalarGridSpec(num_scalar_...  10.9 us
  transfers between devices with their start and end apart: 11, of which 3 were waited for; matrix products, arithmetic and copies ran while one was open for 3% of the time, Pallas kernels for 55%

profile of v2, /device:TPU:0, one launch (start us, length us, event | category | flops | bytes accessed | tf_op | source)
XLA Modules:
  0.0 232.4 jit_solution(17088008084792366452)
XLA Ops:
  7.2 0.0 all-gather.3.cloned.1.call-start
  7.2 2.1 pad_maximum_fusion
  9.3 0.0 all-gather.3.cloned.1.call-update
  9.3 0.0 all-gather.5.cloned.1.call-start
  9.3 0.0 copy-start.9
  9.4 0.0 copy-start.8
  9.4 9.0 %dense.1.refs_0_ = bf16[128,6144]{1,0:T(8,128)(2,1)} custom-call(bf16[128,1536]{1,0:T(8,128)(2,1)} %base_ref.2, bf16[1536,6144]{1,0:T(8,128)(2,1)} %bitcast.12), custom_call_target="tpu_custom_call" | custom-call | bytes 45848984 | tf_op jit(solution)/shard_map/dense/pallas_call | solution.py:246
  18.4 0.5 collective-permute-start.1
  18.8 2.5 %collective-permute-start = (bf16[128,6144]{1,0:T(8,128)(2,1)}, bf16[128,6144]{1,0:T(8,128)(2,1)S(1)}, u32[]{:S(2)}, u32[]{:S(2)}) collective-permute-start(bf16[128,6144]{1,0:T(8,128)(2,1)} %dense.1.refs_0_), channel_id=1, source_target_pairs={{0,8},{4,12},{8,0},{12,4},{1,9},{5,13},{9,1},{13,5},{2,10},{6,14},... | collective-permute-start | bytes 4718600 | tf_op jit(solution)/shard_map/ppermute | solution.py:20
  21.3 0.1 fusion.5
  21.4 0.1 pad_add_fusion.2
  21.5 0.1 fusion.target_ref
  21.5 0.6 pad_add_fusion
  22.1 0.5 slice_bitcast_fusion.index_ref
  22.6 0.0 collective-permute-done.1.refs_0_.refs_1_
  22.6 1.2 copy-done.2
  23.8 11.2 %dense_nt.1.refs_5_.grad_ref = f32[128,6144]{1,0:T(8,128)} custom-call(bf16[128,1536]{1,0:T(8,128)(2,1)} %base_ref.3, bf16[6144,1536]{1,0:T(8,128)(2,1)} %bitcast.15, bf16[128,6144]{1,0:T(8,128)(2,1)} %copy-done.2), custom_call_target="tpu_custom_call" | custom-call | bytes 49309288 | tf_op jit(solution)/shard_map/dense_nt/pallas_call | solution.py:246
  35.0 9.3 %mixed_near.1.near_ref = f32[128,6144]{1,0:T(8,128)} custom-call(s32[3,24]{1,0:T(4,128)} %bitcast.20, bf16[128,6144]{1,0:T(8,128)(2,1)} %dense.1.refs_0_, bf16[128,6144]{1,0:T(8,128)(2,1)} %copy-done.2, bf16[4,24,256,256]{3,2,1,0:T(8,128)(2,1)} %refs_7_.1, bf16[4,24,256,256]{3,2,1,0:T(8,128)(2,1)} %refs_7_.1, bf16[4,24,256,256]{3,2,1,0:T(8,128)(2,1)} %refs_7_.1, ...), custom_call_target="tpu_custom_call" | custom-call | bytes 34603008 | tf_op jit(solution)/shard_map/mixed_near/pallas_call | solution.py:107
  44.3 12.3 %collective-permute-done.source_ref = bf16[128,6144]{1,0:T(8,128)(2,1)S(1)} collective-permute-done((bf16[128,6144]{1,0:T(8,128)(2,1)}, bf16[128,6144]{1,0:T(8,128)(2,1)S(1)}, u32[]{:S(2)}, u32[]{:S(2)}) %collective-permute-start) | collective-permute-done | bytes 1572896 | tf_op jit(solution)/shard_map/ppermute | solution.py:20
  56.6 1.1 copy-done.3
  57.7 10.9 %mixed_last.1 = (bf16[128,4096]{1,0:T(8,128)(2,1)}, bf16[128,6144]{1,0:T(8,128)(2,1)}, bf16[128,6144]{1,0:T(8,128)(2,1)}) custom-call(s32[24]{0:T(128)} %slice_bitcast_fusion.index_ref, bf16[128,6144]{1,0:T(8,128)(2,1)} %copy-done.3, bf16[4,24,256,256]{3,2,1,0:T(8,128)(2,1)} %refs_7_.1, f32[128,6144]{1,0:T(8,128)} %mixed_near.1.near_ref, ...), custom_call_target="tpu_custom_call" | custom-call | bytes 31142708 | tf_op jit(solution)/shard_map/mixed_last/pallas_call | solution.py:145
  68.6 0.0 all-gather.5.cloned.1.call-update
  68.6 8.4 %far_terms.1 = (bf16[128,6144]{1,0:T(8,128)(2,1)}, bf16[128,6144]{1,0:T(8,128)(2,1)}) custom-call(s32[2,24]{1,0:T(2,128)} %copy-done.7, bf16[128,6144]{1,0:T(8,128)(2,1)} %get-tuple-element.19.delta_ref, bf16[4,24,256,256]{3,2,1,0:T(8,128)(2,1)} %refs_7_.1, bf16[4,24,256,256]{3,2,1,0:T(8,128)(2,1)} %refs_7_.1), custom_call_target="tpu_custom_call" | custom-call | bytes 24222104 | tf_op jit(solution)/shard_map/far_terms/pallas_call | solution.py:181
  77.0 1.8 collective-permute-start.3
  78.7 0.1 fusion.1
  78.8 0.7 select_reduce_fusion.place_ref
  79.5 19.7 %hidden_rows.1 = (bf16[24,256,512]{2,1,0:T(8,128)(2,1)}, bf16[24,64,512]{2,1,0:T(8,128)(2,1)}, bf16[3072,512]{1,0:T(8,128)(2,1)}, bf16[3072,512]{1,0:T(8,128)(2,1)}) custom-call(s32[1]{0:T(128)} %bitcast.6.run_ref, s32[2,24]{1,0:T(2,128)} %select_reduce_fusion.place_ref, bf16[1536,6144]{1,0:T(8,128)(2,1)} %bitcast.13, ...), custom_call_target="tpu_custom_call" | custom-call | bytes 55364812 | tf_op jit(solution)/shard_map/hidden_rows/pallas_call | solution.py:329
  99.2 0.5 collective-permute-start.7
  99.7 0.2 collective-permute-start.8
  99.9 0.6 dynamic-slice_subtract_fusion.perm_ref.index_ref
  100.5 8.6 %near_terms.1.refs_0_ = f32[128,6144]{1,0:T(8,128)} custom-call(s32[24]{0:T(128)} %dynamic-slice_subtract_fusion.perm_ref.index_ref, bf16[128,6144]{1,0:T(8,128)(2,1)} %get-tuple-element.19.delta_ref, bf16[4,24,256,256]{3,2,1,0:T(8,128)(2,1)} %refs_7_.1, bf16[4,24,256,256]{3,2,1,0:T(8,128)(2,1)} %refs_7_.1, ...), custom_call_target="tpu_custom_call" | custom-call | bytes 24222104 | tf_op jit(solution)/shard_map/near_terms/pallas_call | solution.py:215
  109.1 5.4 %collective-permute-done.3 = bf16[128,6144]{1,0:T(8,128)(2,1)} collective-permute-done((bf16[128,6144]{1,0:T(8,128)(2,1)}, bf16[128,6144]{1,0:T(8,128)(2,1)}, u32[]{:S(2)}, u32[]{:S(2)}) %collective-permute-start.3) | collective-permute-done | bytes 1572896 | tf_op jit(solution)/shard_map/ppermute | solution.py:20
  114.5 3.4 %add_convert_fusion.left_ref = bf16[128,6144]{1,0:T(8,128)(2,1)S(1)} fusion(bf16[128,6144]{1,0:T(8,128)(2,1)} %collective-permute-done.3, f32[128,6144]{1,0:T(8,128)} %near_terms.1.refs_0_, bf16[128,6144]{1,0:T(8,128)(2,1)} %collective-permute-done.2), kind=kLoop, calls=%fused_computation | loop fusion | flops 3932160 | bytes 7864320 | tf_op jit(solution)/shard_map/convert_element_type | solution.py:707
  117.9 1.0 constant_dynamic-slice_fusion
  118.9 4.0 %collective-permute-start.6 = (bf16[128,1536]{1,0:T(8,128)(2,1)S(1)}, bf16[128,1536]{1,0:T(8,128)(2,1)S(1)}, u32[]{:S(2)}, u32[]{:S(2)}) collective-permute-start(bf16[128,1536]{1,0:T(8,128)(2,1)S(1)} %get-tuple-element.31), channel_id=1, source_target_pairs={{0,3},{1,0},{2,1},{3,2},{4,7},{5,4},{6,5},{7,6},{8,11},{9,8},{10,9... | collective-permute-start | bytes 1179656 | tf_op jit(solution)/shard_map/ppermute | solution.py:25
  122.9 1.0 collective-permute-start.4
  123.8 0.5 and_select_fusion.run_ref
  124.4 16.9 %down_pass.1 = (bf16[128,1536]{1,0:T(8,128)(2,1)}, f32[512,4096]{1,0:T(8,128)}) custom-call(bf16[128,6144]{1,0:T(8,128)(2,1)} %get-tuple-element.18.act_ref, bf16[6144,1536]{1,0:T(8,128)(2,1)} %bitcast.16, bf16[128,1536]{1,0:T(8,128)(2,1)} %base_ref.2, bf16[512,3072]{1,0:T(8,128)(2,1)} %all-gather.3.cloned.1.call-done.inputs_ref.all_ref.refs_9_.right_ref, ...), custom_call_target="tpu_custom_call" | custom-call | bytes 63438848 | tf_op jit(solution)/shard_map/down_pass/pallas_call | solution.py:381
  141.2 11.0 %added_nt.1.refs_10_ = bf16[128,1536]{1,0:T(8,128)(2,1)} custom-call(bf16[128,6144]{1,0:T(8,128)(2,1)} %copy-done, bf16[1536,6144]{1,0:T(8,128)(2,1)} %bitcast.14, bf16[128,1536]{1,0:T(8,128)(2,1)} %base_ref.3, bf16[128,1536]{1,0:T(8,128)(2,1)} %get-tuple-element.13.refs_0_), custom_call_target="tpu_custom_call" | custom-call | bytes 45848984 | tf_op jit(solution)/shard_map/added_nt/pallas_call | solution.py:281
  152.3 28.8 %collective-permute-done.8.refs_3_.refs_1_ = bf16[3072,512]{1,0:T(8,128)(2,1)} collective-permute-done((bf16[3072,512]{1,0:T(8,128)(2,1)}, bf16[3072,512]{1,0:T(8,128)(2,1)}, u32[]{:S(2)}, u32[]{:S(2)}) %collective-permute-start.8) | collective-permute-done | bytes 3145760 | tf_op jit(solution)/shard_map/ppermute | solution.py:20
  181.1 15.4 %recomputed.1 = (f32[4,24,64,256]{3,2,1,0:T(8,128)}, bf16[8,256,512]{2,1,0:T(8,128)(2,1)}) custom-call(s32[24]{0:T(128)} %dynamic-slice_subtract_fusion.perm_ref.index_ref, s32[1]{0:T(128)} %bitcast.6.run_ref, bf16[24,256,512]{2,1,0:T(8,128)(2,1)} %get-tuple-element.24.refs_0_.refs_1_, bf16[24,256,512]{2,1,0:T(8,128)(2,1)} %get-tuple-element.24.refs_0_.refs_1_, ...), custom_call_target="tpu_custom_call" | custom-call | bytes 41523608 | tf_op jit(solution)/shard_map/recomputed/pallas_call | solution.py:490
  196.5 0.0 copy-start.6
  196.5 0.7 copy-done.4
  197.2 0.1 copy-done.5
  197.3 0.1 copy-done.6
  197.4 7.7 %up_gradient.1.refs_0_ = f32[1536,1536]{1,0:T(8,128)} custom-call(s32[4]{0:T(128)} %and_select_fusion.run_ref, bf16[512,3072]{1,0:T(8,128)(2,1)} %all-gather.3.cloned.1.call-done.inputs_ref.all_ref.refs_9_.right_ref, bf16[128,1536]{1,0:T(8,128)(2,1)} %get-tuple-element.34.refs_0_, bf16[128,1536]{1,0:T(8,128)(2,1)} %copy-done.6, bf16[128,1536]{1,0:T(8,128)(2,1)} %copy-done.5, ...), custom_call_target="tpu_custom_call" | custom-call | bytes 27682406 | tf_op jit(solution)/shard_map/up_gradient/pallas_call | solution.py:537
  205.1 8.3 %down_gradient_split.1 = f32[1536,1536]{1,0:T(8,128)} custom-call(s32[1]{0:T(128)} %bitcast.6.run_ref, bf16[512,4096]{1,0:T(8,128)(2,1)} %all-gather.5.cloned.1.call-done.mixed_ref, bf16[8,256,512]{2,1,0:T(8,128)(2,1)} %get-tuple-element.27.refs_4_.act_ref, bf16[512,3072]{1,0:T(8,128)(2,1)} %all-gather.3.cloned.1.call-done.inputs_ref.all_ref.refs_9_.right_ref, ...), custom_call_target="tpu_custom_call" | custom-call | bytes 27682406 | tf_op jit(solution)/shard_map/down_gradient_split/pallas_call | solution.py:606
  213.4 12.1 %mix_gradient.1 = f32[4,24,64,256]{3,2,1,0:T(8,128)} custom-call(s32[24]{0:T(128)} %dynamic-slice_subtract_fusion.perm_ref.index_ref, bf16[512,4096]{1,0:T(8,128)(2,1)} %all-gather.5.cloned.1.call-done.mixed_ref, f32[512,4096]{1,0:T(8,128)} %get-tuple-element.29.grad_ref, ...), custom_call_target="tpu_custom_call", output_to_operand_aliasing={{}: (6, {})} | custom-call | bytes 27682406 | tf_op jit(solution)/shard_map/mix_gradient/pallas_call | solution.py:435
  (24 shorter events, 0.1 us)
Async XLA Ops:
  7.2 72.3 %all-gather.3.cloned.1.call-start = ((), (), s32[]{:S(2)}) async-start(), calls=%async_computation | async-start | bytes 3932160 | tf_op jit(solution)/shard_map/all_gather | solution.py:680
  9.3 195.8 %all-gather.5.cloned.1.call-start = ((), (), s32[]{:S(2)}) async-start(), calls=%async_computation.1 | async-start | bytes 5242880 | tf_op jit(solution)/shard_map/all_gather | solution.py:693
  9.3 12.0 %copy-start.9 = (s32[96]{0:T(128)S(1)}, s32[96]{0:T(128)}, u32[]{:S(2)}) copy-start(s32[96]{0:T(128)} %param.13) | copy-start | bytes 1156
  9.4 12.1 %copy-start.8 = (s32[2,96]{1,0:T(2,128)S(1)}, s32[2,96]{1,0:T(2,128)}, u32[]{:S(2)}) copy-start(s32[2,96]{1,0:T(2,128)} %param.12) | copy-start | bytes 2308
  18.4 4.3 %collective-permute-start.1 = (bf16[128,6144]{1,0:T(8,128)(2,1)}, bf16[128,6144]{1,0:T(8,128)(2,1)S(1)}, u32[]{:S(2)}, u32[]{:S(2)}) collective-permute-start(bf16[128,6144]{1,0:T(8,128)(2,1)} %dense.1.refs_0_), channel_id=1, source_target_pairs={{0,4},{4,0},{8,12},{12,8},{1,5},{5,1},{9,13},{13,9},{2,6},{6,2},{1... | collective-permute-start | bytes 4718600 | tf_op jit(solution)/shard_map/ppermute | solution.py:20
  18.8 37.8 %collective-permute-start = (bf16[128,6144]{1,0:T(8,128)(2,1)}, bf16[128,6144]{1,0:T(8,128)(2,1)S(1)}, u32[]{:S(2)}, u32[]{:S(2)}) collective-permute-start(bf16[128,6144]{1,0:T(8,128)(2,1)} %dense.1.refs_0_), channel_id=1, source_target_pairs={{0,8},{4,12},{8,0},{12,4},{1,9},{5,13},{9,1},{13,5},{2,10},{6,14},... | collective-permute-start | bytes 4718600 | tf_op jit(solution)/shard_map/ppermute | solution.py:20
  21.5 13.5 %copy-start.7 = (s32[2,24]{1,0:T(2,128)}, s32[2,24]{1,0:T(2,128)S(1)}, u32[]{:S(2)}) copy-start(s32[2,24]{1,0:T(2,128)S(1)} %fusion.target_ref) | copy-start | bytes 580
  22.6 1.2 copy-start.2
  56.6 1.1 copy-start.3
  77.0 37.6 %collective-permute-start.3 = (bf16[128,6144]{1,0:T(8,128)(2,1)}, bf16[128,6144]{1,0:T(8,128)(2,1)}, u32[]{:S(2)}, u32[]{:S(2)}) collective-permute-start(bf16[128,6144]{1,0:T(8,128)(2,1)} %get-tuple-element.23), channel_id=1, source_target_pairs={{0,8},{4,12},{8,0},{12,4},{1,9},{5,13},{9,1},{13,5},{2,10},{6,14},... | collective-permute-start | bytes 4718600 | tf_op jit(solution)/shard_map/ppermute | solution.py:20
  78.7 35.8 %collective-permute-start.2 = (bf16[128,6144]{1,0:T(8,128)(2,1)}, bf16[128,6144]{1,0:T(8,128)(2,1)}, u32[]{:S(2)}, u32[]{:S(2)}) collective-permute-start(bf16[128,6144]{1,0:T(8,128)(2,1)} %get-tuple-element.20.refs_0_), channel_id=1, source_target_pairs={{0,4},{4,0},{8,12},{12,8},{1,5},{5,1},{9,13},{13,9},{2,6},{6,2},{1... | collective-permute-start | bytes 4718600 | tf_op jit(solution)/shard_map/ppermute | solution.py:20
  99.2 53.1 %collective-permute-start.7 = (bf16[3072,512]{1,0:T(8,128)(2,1)}, bf16[3072,512]{1,0:T(8,128)(2,1)S(1)}, u32[]{:S(2)}, u32[]{:S(2)}) collective-permute-start(bf16[3072,512]{1,0:T(8,128)(2,1)} %get-tuple-element.25), channel_id=1, source_target_pairs={{0,4},{4,0},{8,12},{12,8},{1,5},{5,1},{9,13},{13,9},{2,6},{6,2},{1... | collective-permute-start | bytes 9437192 | tf_op jit(solution)/shard_map/ppermute | solution.py:20
  99.7 81.4 %collective-permute-start.8 = (bf16[3072,512]{1,0:T(8,128)(2,1)}, bf16[3072,512]{1,0:T(8,128)(2,1)}, u32[]{:S(2)}, u32[]{:S(2)}) collective-permute-start(bf16[3072,512]{1,0:T(8,128)(2,1)} %get-tuple-element.26), channel_id=1, source_target_pairs={{0,8},{4,12},{8,0},{12,4},{1,9},{5,13},{9,1},{13,5},{2,10},{6,14},... | collective-permute-start | bytes 9437192 | tf_op jit(solution)/shard_map/ppermute | solution.py:20
  117.9 23.3 %copy-start = (bf16[128,6144]{1,0:T(8,128)(2,1)}, bf16[128,6144]{1,0:T(8,128)(2,1)S(1)}, u32[]{:S(2)}) copy-start(bf16[128,6144]{1,0:T(8,128)(2,1)S(1)} %add_convert_fusion.left_ref) | copy-start | bytes 4718596
  118.9 77.5 %collective-permute-start.6 = (bf16[128,1536]{1,0:T(8,128)(2,1)S(1)}, bf16[128,1536]{1,0:T(8,128)(2,1)S(1)}, u32[]{:S(2)}, u32[]{:S(2)}) collective-permute-start(bf16[128,1536]{1,0:T(8,128)(2,1)S(1)} %get-tuple-element.31), channel_id=1, source_target_pairs={{0,3},{1,0},{2,1},{3,2},{4,7},{5,4},{6,5},{7,6},{8,11},{9,8},{10,9... | collective-permute-start | bytes 1179656 | tf_op jit(solution)/shard_map/ppermute | solution.py:25
  122.9 73.6 %collective-permute-start.5 = (bf16[128,1536]{1,0:T(8,128)(2,1)S(1)}, bf16[128,1536]{1,0:T(8,128)(2,1)S(1)}, u32[]{:S(2)}, u32[]{:S(2)}) collective-permute-start(bf16[128,1536]{1,0:T(8,128)(2,1)S(1)} %get-tuple-element.32), channel_id=1, source_target_pairs={{0,2},{1,3},{2,0},{3,1},{4,6},{5,7},{6,4},{7,5},{8,10},{9,11},{10,... | collective-permute-start | bytes 1179656 | tf_op jit(solution)/shard_map/ppermute | solution.py:25
  122.9 73.6 %collective-permute-start.4 = (bf16[128,1536]{1,0:T(8,128)(2,1)S(1)}, bf16[128,1536]{1,0:T(8,128)(2,1)S(1)}, u32[]{:S(2)}, u32[]{:S(2)}) collective-permute-start(bf16[128,1536]{1,0:T(8,128)(2,1)S(1)} %get-tuple-element.33), channel_id=1, source_target_pairs={{0,1},{1,2},{2,3},{3,0},{4,5},{5,6},{6,7},{7,4},{8,9},{9,10},{10,1... | collective-permute-start | bytes 1179656 | tf_op jit(solution)/shard_map/ppermute | solution.py:25
  152.3 28.8 %copy-start.1 = (bf16[3072,512]{1,0:T(8,128)(2,1)}, bf16[3072,512]{1,0:T(8,128)(2,1)S(1)}, u32[]{:S(2)}) copy-start(bf16[3072,512]{1,0:T(8,128)(2,1)S(1)} %collective-permute-done.7.refs_2_.refs_0_) | copy-start | bytes 9437188
  196.4 0.8 copy-start.4
  196.5 0.9 copy-start.5
  196.5 1.0 copy-start.6
Sparse Core Ops, SparseCore 0:
  9.6 66.1 all-gather.2
  77.4 112.8 all-gather.4

commit v3 on v2

--- a/solution.py
+++ b/solution.py
@@ -164,7 +164,7 @@
     )(index, source, mix_weight, near, act_grad, *after)
 
 
-def far_terms(delta, targets, levels, mix_weight):
+def far_terms(delta, targets, levels, mix_weight, after=()):
     rows, width = delta.shape
     blocks, size = mix_weight.shape[1], mix_weight.shape[2]
     chunk = chunk_of(blocks, 4)
@@ -176,7 +176,7 @@
             here = delta_ref[:, c * size : (c + 1) * size]
             for k in range(count):
                 place = lanes(target_ref[k, step * chunk + c], size)
-                refs[count + k][:, place] = dot_nt(here, refs[k][0, c]).astype(BF16)
+                refs[count + len(after) + k][:, place] = dot_nt(here, refs[k][0, c]).astype(BF16)
 
     return pl.pallas_call(
         kernel,
@@ -184,49 +184,70 @@
             num_scalar_prefetch=1,
             grid=(blocks // chunk,),
             in_specs=[pl.BlockSpec((rows, chunk * size), lambda i, *_: (0, i))]
-            + weight_specs(levels, chunk, size),
+            + weight_specs(levels, chunk, size)
+            + [ANY] * len(after),
             out_specs=[whole((rows, width))] * count,
         ),
         out_shape=[jax.ShapeDtypeStruct((rows, width), BF16)] * count,
         compiler_params=params(),
         name="far_terms",
         cost_estimate=cost(delta, *[level_shape(mix_weight), delta] * count),
-    )(targets, delta, *([mix_weight] * count))
-
-
-def near_terms(delta, perm, mix_weight, after=()):
+    )(targets, delta, *([mix_weight] * count), *after)
+
+
+def back_pass(delta, perm, mix_weight, terms, run_next, after=()):
     rows, width = delta.shape
     blocks, size = mix_weight.shape[1], mix_weight.shape[2]
     chunk = chunk_of(blocks, 4)
-
-    def kernel(perm_ref, delta_ref, own_ref, perm_weight_ref, *refs):
-        out_ref = refs[-1]
+    runs = run_next.shape[0]
+    share = width // runs
+    split = share % 128 == 0
+
+    def kernel(perm_ref, run_ref, delta_ref, own_ref, perm_weight_ref, *refs):
+        out_ref, *piece_refs, total_ref = refs[len(terms) + len(after) :]
         step = pl.program_id(0)
 
         @pl.when(step == 0)
         def _():
-            out_ref[...] = jnp.zeros_like(out_ref)
+            total = refs[0][...].astype(F32)
+            for term_ref in refs[1 : len(terms)]:
+                total = total + term_ref[...].astype(F32)
+            total_ref[...] = total
 
         for c in range(chunk):
             here = delta_ref[:, c * size : (c + 1) * size]
-            out_ref[:, lanes(step * chunk + c, size)] += dot_nt(here, own_ref[0, c])
-            out_ref[:, lanes(perm_ref[step * chunk + c], size)] += dot_nt(here, perm_weight_ref[0, c])
-
-    return pl.pallas_call(
-        kernel,
-        grid_spec=pltpu.PrefetchScalarGridSpec(
-            num_scalar_prefetch=1,
+            total_ref[:, lanes(step * chunk + c, size)] += dot_nt(here, own_ref[0, c])
+            total_ref[:, lanes(perm_ref[step * chunk + c], size)] += dot_nt(here, perm_weight_ref[0, c])
+
+        @pl.when(step == blocks // chunk - 1)
+        def _():
+            out_ref[...] = total_ref[...].astype(BF16)
+            for s, piece_ref in enumerate(piece_refs):
+                piece_ref[...] = total_ref[:, lanes(run_ref[s], share)].astype(BF16)
+
+    results = pl.pallas_call(
+        kernel,
+        grid_spec=pltpu.PrefetchScalarGridSpec(
+            num_scalar_prefetch=2,
             grid=(blocks // chunk,),
             in_specs=[pl.BlockSpec((rows, chunk * size), lambda i, *_: (0, i))]
             + weight_specs([0, 1], chunk, size)
-            + [ANY] * len(after),
-            out_specs=whole((rows, width)),
-        ),
-        out_shape=jax.ShapeDtypeStruct((rows, width), F32),
-        compiler_params=params(),
-        name="near_terms",
-        cost_estimate=cost(delta, delta, delta, *[level_shape(mix_weight)] * 2),
-    )(perm, delta, mix_weight, mix_weight, *after)
+            + [whole((rows, width))] * len(terms)
+            + [ANY] * len(after),
+            out_specs=[whole((rows, width))] + [whole((rows, share))] * (runs if split else 0),
+            scratch_shapes=[pltpu.VMEM((rows, width), F32)],
+        ),
+        out_shape=[jax.ShapeDtypeStruct((rows, width), BF16)]
+        + [jax.ShapeDtypeStruct((rows, share), BF16)] * (runs if split else 0),
+        compiler_params=params(),
+        name="back_pass",
+        cost_estimate=cost(delta, *terms, *[level_shape(mix_weight)] * 2),
+    )(perm, run_next, delta, mix_weight, mix_weight, *terms, *after)
+    if split:
+        return results[0], results[1:]
+    return results[0], [
+        lax.dynamic_slice_in_dim(results[0], run_next[s] * share, share, 1) for s in range(runs)
+    ]
 
 
 def dense(left, right, out_type, right_transposed=False, after=()):
@@ -292,25 +313,28 @@
     )(left, right, base, *after)
 
 
-def hidden_rows(up, gathered, run, places, blocks, kept, part, after=()):
+def hidden_rows(up, gathered, run_rows, places, blocks, kept, part, rows, after=()):
     depth, width = up.shape
     tokens = gathered.shape[0]
     size = width // blocks
     chunk = chunk_of(blocks, 4)
     levels = places.shape[0]
     again = blocks - kept
-    sent = jax.ShapeDtypeStruct((again * size + kept * part, tokens), BF16)
+    others = tokens - rows
+    sent = [jax.ShapeDtypeStruct((kept * part, tokens), BF16)] * levels
+    if again:
+        sent += [jax.ShapeDtypeStruct((again * size, others), BF16)] * levels
 
     def kernel(run_ref, place_ref, up_ref, inputs_ref, *refs):
-        whole_ref, out_ref = refs[-3 - levels : -1 - levels]
-        sent_refs, full_ref = refs[-1 - levels : -1], refs[-1]
-        full_ref[...] = lax.dot_general(
-            up_ref[...], inputs_ref[...], (((0,), (1,)), ((), ())), preferred_element_type=F32
-        )
+        whole_ref, out_ref, *sent_refs, full_ref = refs[len(after) :]
+        full_ref[...] = dot(inputs_ref[...], up_ref[...]).astype(BF16).T
         for c in range(chunk):
             first = pl.multiple_of(run_ref[0] * part, part) + c * size
-            whole_ref[c] = full_ref[c * size : (c + 1) * size].astype(BF16)
-            out_ref[c] = full_ref[pl.ds(first, part), :].astype(BF16)
+            for s in range(1, tokens // rows):
+                there = pl.multiple_of(run_ref[s] * rows, rows)
+                piece = full_ref[c * size : (c + 1) * size, pl.ds(there, rows)]
+                whole_ref[c, :, (s - 1) * rows : s * rows] = piece
+            out_ref[c] = full_ref[pl.ds(first, part), :]
             for lv in range(levels):
                 place = place_ref[lv, pl.program_id(0) * chunk + c]
 
@@ -319,11 +343,11 @@
                     @pl.when(place >= kept)
                     def _(place=place, lv=lv, c=c):
                         there = pl.multiple_of((place - kept) * size, size)
-                        sent_refs[lv][pl.ds(there, size), :] = whole_ref[c]
+                        sent_refs[levels + lv][pl.ds(there, size), :] = whole_ref[c]
 
                 @pl.when(place < kept)
                 def _(place=place, lv=lv, c=c):
-                    there = pl.multiple_of(again * size + place * part, part)
+                    there = pl.multiple_of(place * part, part)
                     sent_refs[lv][pl.ds(there, part), :] = out_ref[c]
 
     return pl.pallas_call(
@@ -337,28 +361,29 @@
             ]
             + [ANY] * len(after),
             out_specs=[
-                pl.BlockSpec((chunk, size, tokens), lambda i, *_: (i, 0, 0)),
+                pl.BlockSpec((chunk, size, others), lambda i, *_: (i, 0, 0)),
                 pl.BlockSpec((chunk, part, tokens), lambda i, *_: (i, 0, 0)),
             ]
-            + [whole(sent.shape)] * levels,
-            scratch_shapes=[pltpu.VMEM((chunk * size, tokens), F32)],
+            + [whole(shape.shape) for shape in sent],
+            scratch_shapes=[pltpu.VMEM((chunk * size, tokens), BF16)],
         ),
         out_shape=[
-            jax.ShapeDtypeStruct((blocks, size, tokens), BF16),
+            jax.ShapeDtypeStruct((blocks, size, others), BF16),
             jax.ShapeDtypeStruct((blocks, part, tokens), BF16),
         ]
-        + [sent] * levels,
+        + sent,
         compiler_params=params(),
         name="hidden_rows",
         cost_estimate=cost(up, jax.ShapeDtypeStruct((blocks, size, tokens), BF16)),
-    )(run, places, up, gathered, *after)
-
-
-def down_pass(activated, down, base, gathered, kept, after=()):
+    )(run_rows, places, up, gathered, *after)
+
+
+def down_first(activated, down, base, gathered, kept, after=()):
     rows, width = activated.shape
     features = down.shape[1]
     tokens = gathered.shape[0]
     step = chunk_of(math.gcd(width, kept) // 128, 8) * 128
+    out_type = BF16 if kept == width else F32
 
     def kernel(act_ref, down_ref, base_ref, all_ref, *refs):
         out_ref, grad_ref, total_ref = refs[-3:]
@@ -369,18 +394,19 @@
             total_ref[...] = base_ref[...].astype(F32)
 
         total_ref[...] += dot(act_ref[...], down_ref[...])
-
-        @pl.when(here < kept // step)
-        def _():
-            grad_ref[...] = dot_nt(all_ref[...], down_ref[...])
-
-        @pl.when(here == width // step - 1)
-        def _():
-            out_ref[...] = total_ref[...].astype(BF16)
-
-    return pl.pallas_call(
-        kernel,
-        grid=(width // step,),
+        grad_ref[...] = dot_nt(all_ref[...], down_ref[...])
+
+        @pl.when(here == kept // step - 1)
+        def _():
+            out_ref[...] = total_ref[...].astype(out_type)
+
+    out_shape = [
+        jax.ShapeDtypeStruct((rows, features), out_type),
+        jax.ShapeDtypeStruct((tokens, kept), F32),
+    ]
+    return pl.pallas_call(
+        kernel,
+        grid=(kept // step,),
         in_specs=[
             pl.BlockSpec((rows, step), lambda i: (0, i)),
             pl.BlockSpec((step, features), lambda i: (i, 0)),
@@ -390,17 +416,71 @@
         + [ANY] * len(after),
         out_specs=[
             whole((rows, features)),
-            pl.BlockSpec((tokens, step), lambda i: (0, jnp.minimum(i, kept // step - 1))),
+            pl.BlockSpec((tokens, step), lambda i: (0, i)),
         ],
-        out_shape=[
-            jax.ShapeDtypeStruct((rows, features), BF16),
-            jax.ShapeDtypeStruct((tokens, kept), F32),
-        ],
+        out_shape=out_shape,
         scratch_shapes=[pltpu.VMEM((rows, features), F32)],
         compiler_params=params(),
-        name="down_pass",
-        cost_estimate=cost(activated, down, jax.ShapeDtypeStruct((tokens, kept), F32)),
+        name="down_first",
+        cost_estimate=cost(activated, down, out_shape[1]),
     )(activated, down, base, gathered, *after)
+
+
+def down_rest(activated, down, partial, gathered, run_rows, kept, after=()):
+    rows, width = activated.shape
+    features = down.shape[1]
+    tokens = gathered.shape[0]
+    others = tokens - rows
+    step = chunk_of(math.gcd(width, kept) // 128, 8) * 128
+    first = kept // step
+
+    def kernel(run_ref, act_ref, down_ref, partial_ref, all_ref, *refs):
+        out_ref, grad_ref, rest_ref, total_ref = refs[-4:]
+        here = pl.program_id(0)
+
+        @pl.when(here == 0)
+        def _():
+            total_ref[...] = partial_ref[...]
+            for s in range(1, tokens // rows):
+                there = pl.multiple_of(run_ref[s] * rows, rows)
+                rest_ref[(s - 1) * rows : s * rows, :] = all_ref[pl.ds(there, rows), :]
+
+        total_ref[...] += dot(act_ref[...], down_ref[...])
+        grad_ref[...] = dot_nt(down_ref[...], rest_ref[...])
+
+        @pl.when(here == width // step - first - 1)
+        def _():
+            out_ref[...] = total_ref[...].astype(BF16)
+
+    out_shape = [
+        jax.ShapeDtypeStruct((rows, features), BF16),
+        jax.ShapeDtypeStruct((width - kept, others), F32),
+        jax.ShapeDtypeStruct((others, features), BF16),
+    ]
+    return pl.pallas_call(
+        kernel,
+        grid_spec=pltpu.PrefetchScalarGridSpec(
+            num_scalar_prefetch=1,
+            grid=(width // step - first,),
+            in_specs=[
+                pl.BlockSpec((rows, step), lambda i, *_: (0, first + i)),
+                pl.BlockSpec((step, features), lambda i, *_: (first + i, 0)),
+                whole((rows, features)),
+                column_half(tokens, features, 1),
+            ]
+            + [ANY] * len(after),
+            out_specs=[
+                whole((rows, features)),
+                pl.BlockSpec((step, others), lambda i, *_: (i, 0)),
+                whole((others, features)),
+            ],
+            scratch_shapes=[pltpu.VMEM((rows, features), F32)],
+        ),
+        out_shape=out_shape,
+        compiler_params=params(),
+        name="down_rest",
+        cost_estimate=cost(out_shape[1], out_shape[1], partial, partial),
+    )(run_rows, activated, down, partial, gathered, *after)
 
 
 def mix_gradient(mixed_all, act_grad_all, hidden_part, received, perm, scale, made=None):
@@ -410,9 +490,7 @@
     kept = width // size
     chunk = chunk_of(kept, 4)
     count = 2 + len(received)
-    given = pl.BlockSpec(
-        (kept * part, tokens), lambda i, *_: ((blocks - kept) * size // (kept * part), 0)
-    )
+    given = whole((kept * part, tokens))
 
     def kernel(perm_ref, mixed_ref, grad_ref, part_ref, *refs):
         given_refs, out_ref = refs[: len(received)], refs[-1]
@@ -450,40 +528,68 @@
     )(perm, mixed_all, act_grad_all, hidden_part, *received, *([] if made is None else [made]))
 
 
-def recomputed(hidden_all, received, again, index, down, gathered, run, mix_weight, scale, after=()):
-    blocks, size, tokens = hidden_all.shape
+def recomputed(
+    own_sources, own_delta, others, received, index, act_grad_rest, run, mix_weight, scale, after=()
+):
+    blocks, size, tokens = others.shape
+    rows = own_delta.shape[0]
     count = mix_weight.shape[0]
+    again = act_grad_rest.shape[0] // size
     kept = blocks - again
     part = size // lax.axis_size("dp")
-    features = down.shape[1]
+    chunk = chunk_of(math.gcd(again, kept), 2)
 
     def kernel(index_ref, run_ref, *refs):
-        source_refs, weight_refs = refs[:count], refs[count : 2 * count]
-        down_ref, grad_ref = refs[2 * count : 2 * count + 2]
-        out_ref, act_ref = refs[-2:]
-        mixed = None
-        sources = [ref.at[0] if k < 2 else ref for k, ref in enumerate(source_refs)]
-        for k in range(count):
-            term = dot_tn(weight_refs[k][0, 0], sources[k][...])
-            mixed = term if mixed is None else mixed + term
-        act_ref[0] = gelu_tanh(mixed).astype(BF16)
-        act_grad = dot_nt(down_ref[...], grad_ref[...])
-        delta = (act_grad * gelu_slope(mixed)).astype(BF16)
+        straight_ref, *refs = refs
+        permuted_refs, refs = refs[:chunk], refs[chunk:]
+        received_refs, refs = refs[: len(received)], refs[len(received) :]
+        own_refs, refs = refs[: count * chunk], refs[count * chunk :]
+        weight_refs, refs = refs[:count], refs[count:]
+        grad_ref, delta_ref = refs[:2]
+        out_ref, act_ref, full_ref = refs[-3:]
         first = pl.multiple_of(run_ref[0] * part, part)
-        picked = jnp.concatenate(
-            [sources[k][pl.ds(first, part), :] for k in range(count)], axis=0
+        for c in range(chunk):
+            here = pl.ds(c * size, size)
+            sources = [straight_ref.at[c], permuted_refs[c].at[0]]
+            sources += [ref.at[here] for ref in received_refs]
+            mixed = None
+            for k in range(count):
+                term = dot_tn(weight_refs[k][0, c], sources[k][...])
+                mixed = term if mixed is None else mixed + term
+                full_ref[c * count + k] = dot_tn(own_refs[k * chunk + c][...], delta_ref[:, here])
+            act_ref[c] = gelu_tanh(mixed).astype(BF16)
+            delta = (grad_ref[here, :] * gelu_slope(mixed)).astype(BF16)
+            picked = jnp.concatenate([ref[pl.ds(first, part), :] for ref in sources], axis=0)
+            result = dot_nt(picked, delta)
+            for k in range(count):
+                own = full_ref[c * count + k, pl.ds(first, part), :]
+                out_ref[k, c] = (result[k * part : (k + 1) * part] + own) * scale
+
+    source_specs = [
+        pl.BlockSpec((chunk, size, tokens), lambda i, *_: (kept // chunk + i, 0, 0))
+    ]
+    for c in range(chunk):
+        source_specs.append(
+            pl.BlockSpec(
+                (1, size, tokens),
+                functools.partial(lambda c, i, index, run: (index[1, kept + i * chunk + c], 0, 0), c),
+            )
         )
-        result = dot_nt(picked, delta) * scale
-        for k in range(count):
-            out_ref[k, 0] = result[k * part : (k + 1) * part]
-
-    source_specs = [
-        pl.BlockSpec((1, size, tokens), lambda i, *_: (kept + i, 0, 0)),
-        pl.BlockSpec((1, size, tokens), lambda i, index, run: (index[kept + i], 0, 0)),
-    ] + [pl.BlockSpec((size, tokens), lambda i, *_: (i, 0))] * len(received)
+    source_specs += [pl.BlockSpec((chunk * size, tokens), lambda i, *_: (i, 0))] * len(received)
+    own_specs = [
+        pl.BlockSpec(
+            (rows, size),
+            functools.partial(
+                lambda k, c, i, index, run: (0, index[k, kept + i * chunk + c]), k, c
+            ),
+        )
+        for k in range(count)
+        for c in range(chunk)
+    ]
     level_specs = [
         pl.BlockSpec(
-            (1, 1, size, size), functools.partial(lambda k, i, *_: (k, kept + i, 0, 0), k)
+            (1, chunk, size, size),
+            functools.partial(lambda k, i, *_: (k, kept // chunk + i, 0, 0), k),
         )
         for k in range(count)
     ]
@@ -491,18 +597,20 @@
         kernel,
         grid_spec=pltpu.PrefetchScalarGridSpec(
             num_scalar_prefetch=2,
-            grid=(again,),
+            grid=(again // chunk,),
             in_specs=source_specs
+            + own_specs
             + level_specs
             + [
-                pl.BlockSpec((size, features), lambda i, *_: (kept + i, 0)),
-                column_half(tokens, features, 1),
+                pl.BlockSpec((chunk * size, tokens), lambda i, *_: (i, 0)),
+                pl.BlockSpec((rows, chunk * size), lambda i, *_: (0, kept // chunk + i)),
             ]
             + [ANY] * len(after),
             out_specs=[
-                pl.BlockSpec((count, 1, part, size), lambda i, *_: (0, kept + i, 0, 0)),
-                pl.BlockSpec((1, size, tokens), lambda i, *_: (i, 0, 0)),
+                pl.BlockSpec((count, chunk, part, size), lambda i, *_: (0, kept // chunk + i, 0, 0)),
+                pl.BlockSpec((chunk, size, tokens), lambda i, *_: (i, 0, 0)),
             ],
+            scratch_shapes=[pltpu.VMEM((chunk * count, size, size), F32)],
         ),
         out_shape=[
             jax.ShapeDtypeStruct((count, blocks, part, size), F32),
@@ -510,10 +618,11 @@
         ],
         compiler_params=params(),
         name="recomputed",
-        cost_estimate=cost(*received, *received, gathered, level_shape(mix_weight)),
+        cost_estimate=cost(*received, *received, act_grad_rest),
     )(
-        index, run, hidden_all, hidden_all, *received, *([mix_weight] * count), down, gathered,
-        *after,
+        index, run, others, *([others] * chunk), *received,
+        *[source for source in own_sources for _ in range(chunk)], *([mix_weight] * count),
+        act_grad_rest, own_delta, *after,
     )
 
 
@@ -584,24 +693,27 @@
     )(first[None], mixed_all, gathered, *after)
 
 
-def down_gradient_split(mixed_all, act_rest, gathered, run, share, scale, after=()):
+def down_gradient_split(
+    mixed_all, act_rest, activated, gathered, own, rest, run, share, scale, after=()
+):
     tokens, width = gathered.shape[0], gathered.shape[1] // 2
-    again, size, _ = act_rest.shape
-    kept = mixed_all.shape[1] // size
+    again, size, others = act_rest.shape
+    rows, kept = activated.shape[0], mixed_all.shape[1] // size
     count = share // size
 
-    def kernel(run_ref, mixed_ref, act_ref, right_ref, *refs):
+    def kernel(run_ref, mixed_ref, act_ref, own_act_ref, right_ref, own_ref, rest_ref, *refs):
         out_ref = refs[-1]
         block = run_ref[0] * count + pl.program_id(0)
 
         @pl.when(block < kept)
         def _():
-            activated = gelu_tanh(mixed_ref[...].astype(F32)).astype(BF16)
-            out_ref[...] = dot_tn(activated, right_ref[...]) * scale
+            act = gelu_tanh(mixed_ref[...].astype(F32)).astype(BF16)
+            out_ref[...] = dot_tn(act, right_ref[...]) * scale
 
         @pl.when(block >= kept)
         def _():
-            out_ref[...] = dot(act_ref[0], right_ref[...]) * scale
+            total = dot(act_ref[0], rest_ref[...]) + dot_tn(own_act_ref[...], own_ref[...])
+            out_ref[...] = total * scale
 
     return pl.pallas_call(
         kernel,
@@ -613,10 +725,13 @@
                     (tokens, size), lambda i, run: (0, jnp.minimum(run[0] * count + i, kept - 1))
                 ),
                 pl.BlockSpec(
-                    (1, size, tokens),
+                    (1, size, others),
                     lambda i, run: (jnp.clip(run[0] * count + i - kept, 0, again - 1), 0, 0),
                 ),
+                pl.BlockSpec((rows, size), lambda i, run: (0, run[0] * count + i)),
                 column_half(tokens, width, 1),
+                whole((rows, width)),
+                whole((others, width)),
             ]
             + [ANY] * len(after),
             out_specs=pl.BlockSpec((size, width), lambda i, *_: (i, 0)),
@@ -625,18 +740,7 @@
         compiler_params=params(),
         name="down_gradient_split",
         cost_estimate=cost(gathered, jax.ShapeDtypeStruct((share, width), F32)),
-    )(run, mixed_all, act_rest, gathered, *after)
-
-
-def exchanged(value, axis):
-    size = lax.axis_size(axis)
-    me = lax.axis_index(axis)
-    share = value.shape[1] // size
-    pieces = []
-    for s in range(size):
-        piece = lax.dynamic_slice_in_dim(value, ((me + s) % size) * share, share, 1)
-        pieces.append(rotated(piece, axis, s) if s else piece)
-    return pieces
+    )(run, mixed_all, act_rest, activated, gathered, own, rest, *after)
 
 
 def body(inputs, out_grad, up_weight, mix_weight, output_factor_matrix, partner, local_perm):
@@ -693,37 +797,44 @@
     mixed_all = lax.all_gather(mixed, "dp", axis=0, tiled=True)
     far = far_terms(delta, far_index, list(range(2, levels + 2)), mix_weight)
     far_received = [from_partner(far[lv], "mp", lv) for lv in range(levels)]
-    hidden_all, hidden_part, *sent = hidden_rows(
-        up, gathered, run[None], places, blocks, kept, part, after=far[:1]
-    )
-    sources = [from_partner(sent[lv], "mp", lv) for lv in range(levels)]
-    back = near_terms(delta, perm_here, mix_weight, after=(hidden_part,))
-    outputs, act_grad_all = down_pass(
-        activated, down, inputs, gathered, kept * size, after=(back,)
-    )
-
-    for term in far_received:
-        back = back + term.astype(F32)
-    hidden_grad = back.astype(BF16)
-    hidden_grad_pieces = exchanged(hidden_grad, "dp")
+    outputs, act_grad_all = down_first(
+        activated, down, inputs, gathered, kept * size, after=far[:1]
+    )
+    others, hidden_part, *sent = hidden_rows(
+        up, gathered, run_rows, places, blocks, kept, part, rows,
+        after=[outputs] + far_received[:1],
+    )
+    sources = [from_partner(piece, "mp", k % levels) for k, piece in enumerate(sent)]
+    part_sources, whole_sources = sources[:levels], sources[levels:]
+    run_next = ((run + jnp.arange(runs, dtype=jnp.int32)) % runs).astype(jnp.int32)
+    hidden_grad, to_send = back_pass(
+        delta, perm_here, mix_weight, far_received, run_next, after=[hidden_part] + sources[::levels]
+    )
+    hidden_grad_pieces = [to_send[0]] + [rotated(to_send[s], "dp", s) for s in range(1, runs)]
+    rest = None
+    if again:
+        outputs, *rest = down_rest(
+            activated, down, outputs, gathered, run_rows, kept * size, after=(hidden_grad,)
+        )
     input_grad = dense_added(hidden_grad, up, out_grad, True, after=(outputs,))
     made, act_rest = None, input_grad
     if again:
         made, act_rest = recomputed(
-            hidden_all, sources, again, perm_here, down, gathered, run[None], mix_weight,
-            scale, after=(input_grad,),
+            [hidden, hidden] + received, delta, others, whole_sources, index, rest[0], run[None],
+            mix_weight, scale, after=(input_grad,),
         )
     up_grad = up_gradient(
         gathered, up.shape[0], hidden_grad_pieces, run_rows, scale, after=(act_rest,)
     )
     if again:
         down_grad = down_gradient_split(
-            mixed_all, act_rest, gathered, run[None], share, scale, after=(up_grad,)
+            mixed_all, act_rest, activated, gathered, out_grad, rest[1], run[None], share,
+            scale, after=(up_grad,),
         )
     else:
         down_grad = down_gradient(mixed_all, gathered, run, share, scale, after=(up_grad,))
     mix_grad = mix_gradient(
-        mixed_all, act_grad_all, hidden_part, sources, perm_here, scale, made
+        mixed_all, act_grad_all, hidden_part, part_sources, perm_here, scale, made
     )
     return (outputs, input_grad, up_grad[None], mix_grad, down_grad[None])
 

time: 234 us -> 225 us (0.962)
  the two profiles are of different devices: /device:TPU:0 before, /device:TPU:11 now
where the time goes in v3:
time: 225 us; the launch traced here: 224 us
  Pallas kernels  153 us (68%)
  waiting for transfers between devices  35.9 us (16%)
  between operations  14.1 us (6%)
  starting transfers between devices  8.13 us (4%)
  local copies, waits for them, and re-layouts  7.48 us (3%)
  other arithmetic  5.32 us (2%)
    ppermute x3, waiting for transfers between devices, rotated(): lax.ppermute(value, axis, [(i, (i + shift) % size) for i in range(size)])  21.1 us
    pallas_call x2, Pallas kernels, dense(): pl.pallas_call(kernel, grid=(width // step,), in_specs=[whole((rows, dept...  20.2 us
    pallas_call x1, Pallas kernels, hidden_rows(): pl.pallas_call(kernel, grid_spec=pltpu.PrefetchScalarGridSpec(num_scalar_...  19.2 us
    ppermute x8, waiting for transfers between devices, from_partner(): return lax.ppermute(value, axis, pairs)  14.7 us
    pallas_call x1, Pallas kernels, down_first(): pl.pallas_call(kernel, grid=(kept // step,), in_specs=[pl.BlockSpec((rows...  14 us
    pallas_call x1, Pallas kernels, mix_gradient(): pl.pallas_call(kernel, grid_spec=pltpu.PrefetchScalarGridSpec(num_scalar_...  12 us
    pallas_call x1, Pallas kernels, recomputed(): pl.pallas_call(kernel, grid_spec=pltpu.PrefetchScalarGridSpec(num_scalar_...  11.6 us
    pallas_call x1, Pallas kernels, dense_added(): pl.pallas_call(kernel, grid=(depth // step,), in_specs=[pl.BlockSpec((row...  11 us
  transfers between devices with their start and end apart: 13, of which 5 were waited for; matrix products, arithmetic and copies ran while one was open for 2% of the time, Pallas kernels for 63%

profile of v3, /device:TPU:11, one launch (start us, length us, event | category | flops | bytes accessed | tf_op | source)
XLA Modules:
  0.0 224.1 jit_solution(8634626745757113019)
XLA Ops:
  7.2 2.1 pad_maximum_fusion
  9.4 9.0 %dense.1.refs_0_.refs_5_.refs_6_.refs_7_.refs_8_ = bf16[128,6144]{1,0:T(8,128)(2,1)} custom-call(bf16[128,1536]{1,0:T(8,128)(2,1)} %base_ref.2, bf16[1536,6144]{1,0:T(8,128)(2,1)} %bitcast.15), custom_call_target="tpu_custom_call" | custom-call | bytes 45848984 | tf_op jit(solution)/shard_map/dense/pallas_call | solution.py:267
  18.4 0.7 collective-permute-start.1
  19.1 0.3 collective-permute-start
  19.4 0.1 pad_add_fusion.2
  19.5 0.1 fusion.5
  19.5 0.1 dynamic-slice_subtract_fusion.target_ref
  19.6 0.5 pad_add_fusion.index_ref
  20.2 0.5 slice_bitcast_fusion.index_ref
  20.7 1.7 collective-permute-done.1.refs_0_.refs_1_.refs_9_.refs_10_
  22.4 1.2 copy-done
  23.5 11.2 %dense_nt.1.refs_5_.grad_ref = f32[128,6144]{1,0:T(8,128)} custom-call(bf16[128,1536]{1,0:T(8,128)(2,1)} %own_ref.3, bf16[6144,1536]{1,0:T(8,128)(2,1)} %bitcast.12, bf16[128,6144]{1,0:T(8,128)(2,1)} %copy-done), custom_call_target="tpu_custom_call" | custom-call | bytes 49309288 | tf_op jit(solution)/shard_map/dense_nt/pallas_call | solution.py:267
  34.7 9.3 %mixed_near.1.near_ref = f32[128,6144]{1,0:T(8,128)} custom-call(s32[3,24]{1,0:T(4,128)} %bitcast.20, bf16[128,6144]{1,0:T(8,128)(2,1)} %dense.1.refs_0_.refs_5_.refs_6_.refs_7_.refs_8_, bf16[128,6144]{1,0:T(8,128)(2,1)} %copy-done, bf16[4,24,256,256]{3,2,1,0:T(8,128)(2,1)} %refs_16_.1, bf16[4,24,256,256]{3,2,1,0:T(8,128)(2,1)} %refs_16_.1, ...), custom_call_target="tpu_custom_call" | custom-call | bytes 34603008 | tf_op jit(solution)/shard_map/mixed_near/pallas_call | solution.py:107
  44.0 11.3 %collective-permute-done.source_ref.refs_11_.refs_12_ = bf16[128,6144]{1,0:T(8,128)(2,1)S(1)} collective-permute-done((bf16[128,6144]{1,0:T(8,128)(2,1)}, bf16[128,6144]{1,0:T(8,128)(2,1)S(1)}, u32[]{:S(2)}, u32[]{:S(2)}) %collective-permute-start) | collective-permute-done | bytes 1572896 | tf_op jit(solution)/shard_map/ppermute | solution.py:20
  55.4 1.2 copy-done.1
  56.5 10.9 %mixed_last.1 = (bf16[128,4096]{1,0:T(8,128)(2,1)}, bf16[128,6144]{1,0:T(8,128)(2,1)}, bf16[128,6144]{1,0:T(8,128)(2,1)}) custom-call(s32[24]{0:T(128)} %slice_bitcast_fusion.index_ref, bf16[128,6144]{1,0:T(8,128)(2,1)} %copy-done.1, bf16[4,24,256,256]{3,2,1,0:T(8,128)(2,1)} %refs_16_.1, f32[128,6144]{1,0:T(8,128)} %mixed_near.1.near_ref, ...), custom_call_target="tpu_custom_call" | custom-call | bytes 31142708 | tf_op jit(solution)/shard_map/mixed_last/pallas_call | solution.py:145
  67.5 8.3 %far_terms.1 = (bf16[128,6144]{1,0:T(8,128)(2,1)}, bf16[128,6144]{1,0:T(8,128)(2,1)}) custom-call(s32[2,24]{1,0:T(2,128)} %copy-done.10, bf16[128,6144]{1,0:T(8,128)(2,1)} %get-tuple-element.29.delta_ref.refs_18_, bf16[4,24,256,256]{3,2,1,0:T(8,128)(2,1)} %refs_16_.1, bf16[4,24,256,256]{3,2,1,0:T(8,128)(2,1)} %refs_16_.1), custom_call_target="tpu_custom_call" | custom-call | bytes 24222104 | tf_op jit(solution)/shard_map/far_terms/pallas_call | solution.py:181
  75.8 0.8 collective-permute-start.2
  76.6 0.5 and_select_fusion.1.run_ref
  77.1 0.1 fusion
  77.2 0.7 select_reduce_fusion.place_ref
  77.9 0.3 collective-permute-start.3
  78.2 14.0 %down_first.1 = (f32[128,1536]{1,0:T(8,128)}, f32[512,4096]{1,0:T(8,128)}) custom-call(bf16[128,6144]{1,0:T(8,128)(2,1)} %get-tuple-element.28.act_ref.own_act_ref, bf16[6144,1536]{1,0:T(8,128)(2,1)} %bitcast.13, bf16[128,1536]{1,0:T(8,128)(2,1)} %base_ref.2, bf16[512,3072]{1,0:T(8,128)(2,1)} %all-gather.3.cloned.1.call-done.all_ref.inputs_ref.right_ref, ...), custom_call_target="tpu_custom_call" | custom-call | bytes 63438848 | tf_op jit(solution)/shard_map/down_first/pallas_call | solution.py:407
  92.2 1.1 copy-done.2
  93.4 19.2 %hidden_rows.1 = (bf16[24,256,384]{2,1,0:T(8,128)(2,1)}, bf16[24,64,512]{2,1,0:T(8,128)(2,1)}, bf16[1024,512]{1,0:T(8,128)(2,1)}, bf16[1024,512]{1,0:T(8,128)(2,...) custom-call(s32[4]{0:T(128)} %and_select_fusion.1.run_ref, s32[2,24]{1,0:T(2,128)} %select_reduce_fusion.place_ref, ...), custom_call_target="tpu_custom_call" | custom-call | bytes 55364812 | tf_op jit(solution)/shard_map/hidden_rows/pallas_call | solution.py:353
  112.6 0.4 collective-permute-start.5
  113.0 1.1 collective-permute-start.9
  114.0 0.6 collective-permute-start.4
  114.6 0.3 collective-permute-start.10
  114.9 0.6 dynamic-slice_subtract_fusion.1.perm_ref
  115.5 0.5 and_select_fusion.run_ref
  116.0 1.7 collective-permute-done.4.refs_3_.refs_0_
  117.8 1.0 copy-done.4
  118.8 0.5 copy-done.3
  119.2 10.2 %back_pass.1 = (bf16[128,6144]{1,0:T(8,128)(2,1)}, bf16[128,1536]{1,0:T(8,128)(2,1)}, bf16[128,1536]{1,0:T(8,128)(2,1)}, bf16[128,1536]{1,0:T(8,128)(2,1)}, bf16[128,1536]{1,0:T(8,128)(2,1)}) custom-call(s32[24]{0:T(128)} %dynamic-slice_subtract_fusion.1.perm_ref, s32[4]{0:T(128)} %and_select_fusion.run_ref, ...), custom_call_target="tpu_custom_call" | custom-call | bytes 24222104 | tf_op jit(solution)/shard_map/back_pass/pallas_call | solution.py:228
  129.5 1.3 collective-permute-start.6
  130.8 1.0 collective-permute-start.7
  131.8 1.4 collective-permute-start.8
  133.2 9.7 %down_rest.1 = (bf16[128,1536]{1,0:T(8,128)(2,1)}, f32[2048,384]{1,0:T(8,128)}, bf16[384,1536]{1,0:T(8,128)(2,1)}) custom-call(s32[4]{0:T(128)} %and_select_fusion.1.run_ref, bf16[128,6144]{1,0:T(8,128)(2,1)} %get-tuple-element.28.act_ref.own_act_ref, bf16[6144,1536]{1,0:T(8,128)(2,1)} %bitcast.14, f32[128,1536]{1,0:T(8,128)} %get-tuple-element.31.refs_0_.partial_ref, ...), custom_call_target="tpu_custom_call" | custom-call | bytes 17301504 | tf_op jit(solution)/shard_map/down_rest/pallas_call | solution.py:460
  142.9 11.0 %added_nt.1.refs_19_ = bf16[128,1536]{1,0:T(8,128)(2,1)} custom-call(bf16[128,6144]{1,0:T(8,128)(2,1)} %get-tuple-element.36.refs_0_.left_ref, bf16[1536,6144]{1,0:T(8,128)(2,1)} %bitcast.17, bf16[128,1536]{1,0:T(8,128)(2,1)} %own_ref.3, bf16[128,1536]{1,0:T(8,128)(2,1)} %get-tuple-element.23.refs_0_), custom_call_target="tpu_custom_call" | custom-call | bytes 45848984 | tf_op jit(solution)/shard_map/added_nt/pallas_call | solution.py:302
  153.9 1.2 copy-done.6
  155.1 11.6 %recomputed.1 = (f32[4,24,64,256]{3,2,1,0:T(8,128)}, bf16[8,256,384]{2,1,0:T(8,128)(2,1)}) custom-call(s32[4,24]{1,0:T(4,128)} %pad_add_fusion.index_ref, s32[1]{0:T(128)} %bitcast.6.run_ref, bf16[24,256,384]{2,1,0:T(8,128)(2,1)} %get-tuple-element.42.refs_0_.refs_1_.refs_2_, bf16[24,256,384]{2,1,0:T(8,128)(2,1)} %get-tuple-element.42.refs_0_.refs_1_.refs_2_, ...), custom_call_target="tpu_custom_call" | custom-call | bytes 20761804 | tf_op jit(solution)/shard_map/recomputed/pallas_call | solution.py:596
  166.8 18.5 %collective-permute-done.7.refs_2_ = bf16[128,1536]{1,0:T(8,128)(2,1)S(1)} collective-permute-done((bf16[128,1536]{1,0:T(8,128)(2,1)}, bf16[128,1536]{1,0:T(8,128)(2,1)S(1)}, u32[]{:S(2)}, u32[]{:S(2)}) %collective-permute-start.7) | collective-permute-done | bytes 393248 | tf_op jit(solution)/shard_map/ppermute | solution.py:25
  185.3 2.6 %collective-permute-done.8.refs_3_ = bf16[128,1536]{1,0:T(8,128)(2,1)S(1)} collective-permute-done((bf16[128,1536]{1,0:T(8,128)(2,1)}, bf16[128,1536]{1,0:T(8,128)(2,1)S(1)}, u32[]{:S(2)}, u32[]{:S(2)}) %collective-permute-start.8) | collective-permute-done | bytes 393248 | tf_op jit(solution)/shard_map/ppermute | solution.py:25
  187.9 0.7 copy-done.9
  188.6 7.7 %up_gradient.1.refs_0_ = f32[1536,1536]{1,0:T(8,128)} custom-call(s32[4]{0:T(128)} %and_select_fusion.1.run_ref, bf16[512,3072]{1,0:T(8,128)(2,1)} %all-gather.3.cloned.1.call-done.all_ref.inputs_ref.right_ref, bf16[128,1536]{1,0:T(8,128)(2,1)} %get-tuple-element.38.refs_0_, bf16[128,1536]{1,0:T(8,128)(2,1)} %copy-done.7, bf16[128,1536]{1,0:T(8,128)(2,1)} %copy-done.8, ...), custom_call_target="tpu_custom_call" | custom-call | bytes 27682406 | tf_op jit(solution)/shard_map/up_gradient/pallas_call | solution.py:646
  196.3 8.9 %down_gradient_split.1 = f32[1536,1536]{1,0:T(8,128)} custom-call(s32[1]{0:T(128)} %bitcast.6.run_ref, bf16[512,4096]{1,0:T(8,128)(2,1)} %all-gather.5.cloned.1.call-done.mixed_ref, bf16[8,256,384]{2,1,0:T(8,128)(2,1)} %get-tuple-element.45.refs_4_.act_ref, bf16[128,6144]{1,0:T(8,128)(2,1)} %get-tuple-element.28.act_ref.own_act_ref, ...), custom_call_target="tpu_custom_call" | custom-call | bytes 27682406 | tf_op jit(solution)/shard_map/down_gradient_split/pallas_call | solution.py:718
  205.2 12.0 %mix_gradient.1 = f32[4,24,64,256]{3,2,1,0:T(8,128)} custom-call(s32[24]{0:T(128)} %dynamic-slice_subtract_fusion.1.perm_ref, bf16[512,4096]{1,0:T(8,128)(2,1)} %all-gather.5.cloned.1.call-done.mixed_ref, f32[512,4096]{1,0:T(8,128)} %get-tuple-element.47.grad_ref, ...), custom_call_target="tpu_custom_call", output_to_operand_aliasing={{}: (6, {})} | custom-call | bytes 27682406 | tf_op jit(solution)/shard_map/mix_gradient/pallas_call | solution.py:513
  (34 shorter events, 0.2 us)
Async XLA Ops:
  7.2 71.0 %all-gather.3.cloned.1.call-start = ((), (), s32[]{:S(2)}) async-start(), calls=%async_computation | async-start | bytes 3932160 | tf_op jit(solution)/shard_map/all_gather | solution.py:784
  9.3 186.9 %all-gather.5.cloned.1.call-start = ((), (), s32[]{:S(2)}) async-start(), calls=%async_computation.1 | async-start | bytes 5242880 | tf_op jit(solution)/shard_map/all_gather | solution.py:797
  9.4 10.1 %copy-start.12 = (s32[96]{0:T(128)S(1)}, s32[96]{0:T(128)}, u32[]{:S(2)}) copy-start(s32[96]{0:T(128)} %param.13) | copy-start | bytes 1156
  9.4 10.1 %copy-start.11 = (s32[2,96]{1,0:T(2,128)S(1)}, s32[2,96]{1,0:T(2,128)}, u32[]{:S(2)}) copy-start(s32[2,96]{1,0:T(2,128)} %param.12) | copy-start | bytes 2308
  18.4 3.9 %collective-permute-start.1 = (bf16[128,6144]{1,0:T(8,128)(2,1)}, bf16[128,6144]{1,0:T(8,128)(2,1)S(1)}, u32[]{:S(2)}, u32[]{:S(2)}) collective-permute-start(bf16[128,6144]{1,0:T(8,128)(2,1)} %dense.1.refs_0_.refs_5_.refs_6_.refs_7_.refs_8_), channel_id=1, source_target_pairs={{0,4},{4,0},{8,12},{12,8},{1,5},{5,1},{9,13},{13,9},{2,6},{6,2},{1... | collective-permute-start | bytes 4718600 | tf_op jit(solution)/shard_map/ppermute | solution.py:20
  19.1 36.2 %collective-permute-start = (bf16[128,6144]{1,0:T(8,128)(2,1)}, bf16[128,6144]{1,0:T(8,128)(2,1)S(1)}, u32[]{:S(2)}, u32[]{:S(2)}) collective-permute-start(bf16[128,6144]{1,0:T(8,128)(2,1)} %dense.1.refs_0_.refs_5_.refs_6_.refs_7_.refs_8_), channel_id=1, source_target_pairs={{0,8},{4,12},{8,0},{12,4},{1,9},{5,13},{9,1},{13,5},{2,10},{6,14},... | collective-permute-start | bytes 4718600 | tf_op jit(solution)/shard_map/ppermute | solution.py:20
  19.6 15.1 %copy-start.10 = (s32[2,24]{1,0:T(2,128)}, s32[2,24]{1,0:T(2,128)S(1)}, u32[]{:S(2)}) copy-start(s32[2,24]{1,0:T(2,128)S(1)} %dynamic-slice_subtract_fusion.target_ref) | copy-start | bytes 580
  22.4 1.2 copy-start
  55.3 1.2 copy-start.1
  75.8 16.4 %collective-permute-start.2 = (bf16[128,6144]{1,0:T(8,128)(2,1)}, bf16[128,6144]{1,0:T(8,128)(2,1)S(1)}, u32[]{:S(2)}, u32[]{:S(2)}) collective-permute-start(bf16[128,6144]{1,0:T(8,128)(2,1)} %get-tuple-element.30.refs_0_), channel_id=1, source_target_pairs={{0,4},{4,0},{8,12},{12,8},{1,5},{5,1},{9,13},{13,9},{2,6},{6,2},{1... | collective-permute-start | bytes 4718600 | tf_op jit(solution)/shard_map/ppermute | solution.py:20
  77.9 38.1 %collective-permute-start.3 = (bf16[128,6144]{1,0:T(8,128)(2,1)}, bf16[128,6144]{1,0:T(8,128)(2,1)S(1)}, u32[]{:S(2)}, u32[]{:S(2)}) collective-permute-start(bf16[128,6144]{1,0:T(8,128)(2,1)} %get-tuple-element.32), channel_id=1, source_target_pairs={{0,8},{4,12},{8,0},{12,4},{1,9},{5,13},{9,1},{13,5},{2,10},{6,14},... | collective-permute-start | bytes 4718600 | tf_op jit(solution)/shard_map/ppermute | solution.py:20
  92.2 1.1 copy-start.2
  112.6 5.2 %collective-permute-start.5 = (bf16[2048,384]{1,0:T(8,128)(2,1)}, bf16[2048,384]{1,0:T(8,128)(2,1)S(1)}, u32[]{:S(2)}, u32[]{:S(2)}) collective-permute-start(bf16[2048,384]{1,0:T(8,128)(2,1)} %get-tuple-element.35), channel_id=1, source_target_pairs={{0,4},{4,0},{8,12},{12,8},{1,5},{5,1},{9,13},{13,9},{2,6},{6,2},{1... | collective-permute-start | bytes 4718600 | tf_op jit(solution)/shard_map/ppermute | solution.py:20
  113.0 40.9 %collective-permute-start.9 = (bf16[2048,384]{1,0:T(8,128)(2,1)}, bf16[2048,384]{1,0:T(8,128)(2,1)S(1)}, u32[]{:S(2)}, u32[]{:S(2)}) collective-permute-start(bf16[2048,384]{1,0:T(8,128)(2,1)} %get-tuple-element.43), channel_id=1, source_target_pairs={{0,8},{4,12},{8,0},{12,4},{1,9},{5,13},{9,1},{13,5},{2,10},{6,14},... | collective-permute-start | bytes 4718600 | tf_op jit(solution)/shard_map/ppermute | solution.py:20
  114.0 3.7 %collective-permute-start.4 = (bf16[1024,512]{1,0:T(8,128)(2,1)}, bf16[1024,512]{1,0:T(8,128)(2,1)S(1)}, u32[]{:S(2)}, u32[]{:S(2)}) collective-permute-start(bf16[1024,512]{1,0:T(8,128)(2,1)} %get-tuple-element.34), channel_id=1, source_target_pairs={{0,4},{4,0},{8,12},{12,8},{1,5},{5,1},{9,13},{13,9},{2,6},{6,2},{1... | collective-permute-start | bytes 3145736 | tf_op jit(solution)/shard_map/ppermute | solution.py:20
  114.6 90.6 %collective-permute-start.10 = (bf16[1024,512]{1,0:T(8,128)(2,1)}, bf16[1024,512]{1,0:T(8,128)(2,1)}, u32[]{:S(2)}, u32[]{:S(2)}) collective-permute-start(bf16[1024,512]{1,0:T(8,128)(2,1)} %get-tuple-element.48), channel_id=1, source_target_pairs={{0,8},{4,12},{8,0},{12,4},{1,9},{5,13},{9,1},{13,5},{2,10},{6,14},... | collective-permute-start | bytes 3145736 | tf_op jit(solution)/shard_map/ppermute | solution.py:20
  116.0 1.7 copy-start.5
  117.8 1.0 copy-start.4
  117.8 1.5 copy-start.3
  129.5 37.3 %collective-permute-start.6 = (bf16[128,1536]{1,0:T(8,128)(2,1)}, bf16[128,1536]{1,0:T(8,128)(2,1)S(1)}, u32[]{:S(2)}, u32[]{:S(2)}) collective-permute-start(bf16[128,1536]{1,0:T(8,128)(2,1)} %get-tuple-element.39), channel_id=1, source_target_pairs={{0,1},{1,2},{2,3},{3,0},{4,5},{5,6},{6,7},{7,4},{8,9},{9,10},{10,1... | collective-permute-start | bytes 1179656 | tf_op jit(solution)/shard_map/ppermute | solution.py:25
  130.8 54.5 %collective-permute-start.7 = (bf16[128,1536]{1,0:T(8,128)(2,1)}, bf16[128,1536]{1,0:T(8,128)(2,1)S(1)}, u32[]{:S(2)}, u32[]{:S(2)}) collective-permute-start(bf16[128,1536]{1,0:T(8,128)(2,1)} %get-tuple-element.40), channel_id=1, source_target_pairs={{0,2},{1,3},{2,0},{3,1},{4,6},{5,7},{6,4},{7,5},{8,10},{9,11},{10,... | collective-permute-start | bytes 1179656 | tf_op jit(solution)/shard_map/ppermute | solution.py:25
  131.8 56.1 %collective-permute-start.8 = (bf16[128,1536]{1,0:T(8,128)(2,1)}, bf16[128,1536]{1,0:T(8,128)(2,1)S(1)}, u32[]{:S(2)}, u32[]{:S(2)}) collective-permute-start(bf16[128,1536]{1,0:T(8,128)(2,1)} %get-tuple-element.41), channel_id=1, source_target_pairs={{0,3},{1,0},{2,1},{3,2},{4,7},{5,4},{6,5},{7,6},{8,11},{9,8},{10,9... | collective-permute-start | bytes 1179656 | tf_op jit(solution)/shard_map/ppermute | solution.py:25
  153.9 1.2 copy-start.6
  166.8 21.1 %copy-start.7 = (bf16[128,1536]{1,0:T(8,128)(2,1)}, bf16[128,1536]{1,0:T(8,128)(2,1)S(1)}, u32[]{:S(2)}) copy-start(bf16[128,1536]{1,0:T(8,128)(2,1)S(1)} %collective-permute-done.6.refs_1_) | copy-start | bytes 1179652
  185.3 2.6 %copy-start.8 = (bf16[128,1536]{1,0:T(8,128)(2,1)}, bf16[128,1536]{1,0:T(8,128)(2,1)S(1)}, u32[]{:S(2)}) copy-start(bf16[128,1536]{1,0:T(8,128)(2,1)S(1)} %collective-permute-done.7.refs_2_) | copy-start | bytes 1179652
  187.9 0.7 copy-start.9
Sparse Core Ops, SparseCore 0:
  9.6 62.3 all-gather.2
  73.5 106.0 all-gather.4

commit v4 on v3

--- a/solution.py
+++ b/solution.py
@@ -394,7 +394,7 @@
             total_ref[...] = base_ref[...].astype(F32)
 
         total_ref[...] += dot(act_ref[...], down_ref[...])
-        grad_ref[...] = dot_nt(all_ref[...], down_ref[...])
+        grad_ref[...] = dot_nt(all_ref[...], down_ref[...]).astype(BF16)
 
         @pl.when(here == kept // step - 1)
         def _():
@@ -402,7 +402,7 @@
 
     out_shape = [
         jax.ShapeDtypeStruct((rows, features), out_type),
-        jax.ShapeDtypeStruct((tokens, kept), F32),
+        jax.ShapeDtypeStruct((tokens, kept), BF16),
     ]
     return pl.pallas_call(
         kernel,
@@ -499,7 +499,7 @@
             here = slice(c * size, (c + 1) * size)
             block = step * chunk + c
             slope = gelu_slope(mixed_ref[:, here].astype(F32))
-            delta = (grad_ref[:, here] * slope).astype(BF16)
+            delta = (grad_ref[:, here].astype(F32) * slope).astype(BF16)
             rows = pl.ds(pl.multiple_of(block * part, part), part)
             picked = jnp.concatenate(
                 [part_ref[block], part_ref[perm_ref[block]]] + [ref[rows, :] for ref in given_refs],
@@ -743,6 +743,19 @@
     )(run, mixed_all, act_rest, activated, gathered, own, rest, *after)
 
 
+def held(values, after):
+    count = len(values)
+    return pl.pallas_call(
+        lambda *refs: None,
+        in_specs=[ANY] * (count + len(after)),
+        out_specs=[ANY] * count,
+        out_shape=[jax.ShapeDtypeStruct(v.shape, v.dtype) for v in values],
+        input_output_aliases={k: k for k in range(count)},
+        compiler_params=pltpu.CompilerParams(has_side_effects=True),
+        name="held",
+    )(*values, *after)
+
+
 def body(inputs, out_grad, up_weight, mix_weight, output_factor_matrix, partner, local_perm):
     rows = inputs.shape[0]
     blocks, size = mix_weight.shape[1], mix_weight.shape[2]
@@ -810,31 +823,32 @@
     hidden_grad, to_send = back_pass(
         delta, perm_here, mix_weight, far_received, run_next, after=[hidden_part] + sources[::levels]
     )
-    hidden_grad_pieces = [to_send[0]] + [rotated(to_send[s], "dp", s) for s in range(1, runs)]
     rest = None
     if again:
         outputs, *rest = down_rest(
             activated, down, outputs, gathered, run_rows, kept * size, after=(hidden_grad,)
         )
     input_grad = dense_added(hidden_grad, up, out_grad, True, after=(outputs,))
+    to_send = [to_send[0]] + list(held(to_send[1:], (input_grad,)))
+    hidden_grad_pieces = [to_send[0]] + [rotated(to_send[s], "dp", s) for s in range(1, runs)]
     made, act_rest = None, input_grad
     if again:
         made, act_rest = recomputed(
             [hidden, hidden] + received, delta, others, whole_sources, index, rest[0], run[None],
             mix_weight, scale, after=(input_grad,),
         )
-    up_grad = up_gradient(
-        gathered, up.shape[0], hidden_grad_pieces, run_rows, scale, after=(act_rest,)
+    mix_grad = mix_gradient(
+        mixed_all, act_grad_all, hidden_part, part_sources, perm_here, scale, made
     )
     if again:
         down_grad = down_gradient_split(
-            mixed_all, act_rest, activated, gathered, out_grad, rest[1], run[None], share,
-            scale, after=(up_grad,),
+            mixed_all, act_rest, activated, gathered, out_grad, rest[1], run[None], share, scale,
+            after=(mix_grad,),
         )
     else:
-        down_grad = down_gradient(mixed_all, gathered, run, share, scale, after=(up_grad,))
-    mix_grad = mix_gradient(
-        mixed_all, act_grad_all, hidden_part, part_sources, perm_here, scale, made
+        down_grad = down_gradient(mixed_all, gathered, run, share, scale, after=(mix_grad,))
+    up_grad = up_gradient(
+        gathered, up.shape[0], hidden_grad_pieces, run_rows, scale, after=(down_grad,)
     )
     return (outputs, input_grad, up_grad[None], mix_grad, down_grad[None])
 

time: 225 us -> 212 us (0.942)
  the two profiles are of different devices: /device:TPU:11 before, /device:TPU:0 now
where the time goes in v4:
time: 212 us; the launch traced here: 211 us
  Pallas kernels  152 us (72%)
  waiting for transfers between devices  20.2 us (10%)
  between operations  14.1 us (7%)
  starting transfers between devices  12.7 us (6%)
  local copies, waits for them, and re-layouts  6.5 us (3%)
  other arithmetic  5.31 us (3%)
    pallas_call x2, Pallas kernels, dense(): pl.pallas_call(kernel, grid=(width // step,), in_specs=[whole((rows, dept...  20.2 us
    pallas_call x1, Pallas kernels, hidden_rows(): pl.pallas_call(kernel, grid_spec=pltpu.PrefetchScalarGridSpec(num_scalar_...  19.2 us
    ppermute x8, waiting for transfers between devices, from_partner(): return lax.ppermute(value, axis, pairs)  18.8 us
    pallas_call x1, Pallas kernels, down_first(): pl.pallas_call(kernel, grid=(kept // step,), in_specs=[pl.BlockSpec((rows...  13.3 us
    pallas_call x1, Pallas kernels, recomputed(): pl.pallas_call(kernel, grid_spec=pltpu.PrefetchScalarGridSpec(num_scalar_...  11.6 us
    pallas_call x1, Pallas kernels, mix_gradient(): pl.pallas_call(kernel, grid_spec=pltpu.PrefetchScalarGridSpec(num_scalar_...  11.5 us
    pallas_call x1, Pallas kernels, dense_added(): pl.pallas_call(kernel, grid=(depth // step,), in_specs=[pl.BlockSpec((row...  11 us
    pallas_call x1, Pallas kernels, mixed_last(): pl.pallas_call(kernel, grid_spec=pltpu.PrefetchScalarGridSpec(num_scalar_...  10.9 us
  transfers between devices with their start and end apart: 13, of which 4 were waited for; matrix products, arithmetic and copies ran while one was open for 2% of the time, Pallas kernels for 68%

profile of v4, /device:TPU:0, one launch (start us, length us, event | category | flops | bytes accessed | tf_op | source)
XLA Modules:
  0.0 210.7 jit_solution(9169427919546824690)
XLA Ops:
  7.2 2.1 pad_maximum_fusion
  9.3 0.0 all-gather.5.cloned.1.call-start
  9.4 9.0 %dense.1.refs_0_.refs_5_.refs_6_.refs_7_.refs_8_ = bf16[128,6144]{1,0:T(8,128)(2,1)} custom-call(bf16[128,1536]{1,0:T(8,128)(2,1)} %base_ref.2, bf16[1536,6144]{1,0:T(8,128)(2,1)} %bitcast.15), custom_call_target="tpu_custom_call" | custom-call | bytes 45848984 | tf_op jit(solution)/shard_map/dense/pallas_call | solution.py:267
  18.4 0.5 collective-permute-start.1
  18.8 2.5 %collective-permute-start = (bf16[128,6144]{1,0:T(8,128)(2,1)}, bf16[128,6144]{1,0:T(8,128)(2,1)S(1)}, u32[]{:S(2)}, u32[]{:S(2)}) collective-permute-start(bf16[128,6144]{1,0:T(8,128)(2,1)} %dense.1.refs_0_.refs_5_.refs_6_.refs_7_.refs_8_), channel_id=1, source_target_pairs={{0,8},{4,12},{8,0},{12,4},{1,9},{5,13},{9,1},{13,5},{2,10},{6,14},... | collective-permute-start | bytes 4718600 | tf_op jit(solution)/shard_map/ppermute | solution.py:20
  21.3 0.1 pad_add_fusion.2
  21.4 0.1 fusion.5
  21.5 0.1 dynamic-slice_subtract_fusion.target_ref
  21.6 0.6 pad_add_fusion.index_ref
  22.2 0.6 slice_bitcast_fusion.index_ref
  22.8 1.1 copy-done
  23.9 11.2 %dense_nt.1.refs_5_.grad_ref = f32[128,6144]{1,0:T(8,128)} custom-call(bf16[128,1536]{1,0:T(8,128)(2,1)} %own_ref.3, bf16[6144,1536]{1,0:T(8,128)(2,1)} %bitcast.12, bf16[128,6144]{1,0:T(8,128)(2,1)} %copy-done), custom_call_target="tpu_custom_call" | custom-call | bytes 49309288 | tf_op jit(solution)/shard_map/dense_nt/pallas_call | solution.py:267
  35.0 9.3 %mixed_near.1.near_ref = f32[128,6144]{1,0:T(8,128)} custom-call(s32[3,24]{1,0:T(4,128)} %bitcast.20, bf16[128,6144]{1,0:T(8,128)(2,1)} %dense.1.refs_0_.refs_5_.refs_6_.refs_7_.refs_8_, bf16[128,6144]{1,0:T(8,128)(2,1)} %copy-done, bf16[4,24,256,256]{3,2,1,0:T(8,128)(2,1)} %refs_16_.1, bf16[4,24,256,256]{3,2,1,0:T(8,128)(2,1)} %refs_16_.1, ...), custom_call_target="tpu_custom_call" | custom-call | bytes 34603008 | tf_op jit(solution)/shard_map/mixed_near/pallas_call | solution.py:107
  44.3 12.3 %collective-permute-done.source_ref.refs_11_.refs_12_ = bf16[128,6144]{1,0:T(8,128)(2,1)S(1)} collective-permute-done((bf16[128,6144]{1,0:T(8,128)(2,1)}, bf16[128,6144]{1,0:T(8,128)(2,1)S(1)}, u32[]{:S(2)}, u32[]{:S(2)}) %collective-permute-start) | collective-permute-done | bytes 1572896 | tf_op jit(solution)/shard_map/ppermute | solution.py:20
  56.6 1.1 copy-done.1
  57.8 10.9 %mixed_last.1 = (bf16[128,4096]{1,0:T(8,128)(2,1)}, bf16[128,6144]{1,0:T(8,128)(2,1)}, bf16[128,6144]{1,0:T(8,128)(2,1)}) custom-call(s32[24]{0:T(128)} %slice_bitcast_fusion.index_ref, bf16[128,6144]{1,0:T(8,128)(2,1)} %copy-done.1, bf16[4,24,256,256]{3,2,1,0:T(8,128)(2,1)} %refs_16_.1, f32[128,6144]{1,0:T(8,128)} %mixed_near.1.near_ref, ...), custom_call_target="tpu_custom_call" | custom-call | bytes 31142708 | tf_op jit(solution)/shard_map/mixed_last/pallas_call | solution.py:145
  68.7 8.4 %far_terms.1 = (bf16[128,6144]{1,0:T(8,128)(2,1)}, bf16[128,6144]{1,0:T(8,128)(2,1)}) custom-call(s32[2,24]{1,0:T(2,128)} %copy-done.8, bf16[128,6144]{1,0:T(8,128)(2,1)} %get-tuple-element.32.delta_ref.refs_18_, bf16[4,24,256,256]{3,2,1,0:T(8,128)(2,1)} %refs_16_.1, bf16[4,24,256,256]{3,2,1,0:T(8,128)(2,1)} %refs_16_.1), custom_call_target="tpu_custom_call" | custom-call | bytes 24222104 | tf_op jit(solution)/shard_map/far_terms/pallas_call | solution.py:181
  77.0 0.0 collective-permute-start.2
  77.1 0.5 and_select_fusion.1.run_ref
  77.6 0.1 fusion
  77.7 0.7 select_reduce_fusion.place_ref
  78.4 1.7 collective-permute-start.3
  80.1 13.3 %down_first.1 = (f32[128,1536]{1,0:T(8,128)}, bf16[512,4096]{1,0:T(8,128)(2,1)}) custom-call(bf16[128,6144]{1,0:T(8,128)(2,1)} %get-tuple-element.31.act_ref.own_act_ref, bf16[6144,1536]{1,0:T(8,128)(2,1)} %bitcast.13, bf16[128,1536]{1,0:T(8,128)(2,1)} %base_ref.2, bf16[512,3072]{1,0:T(8,128)(2,1)} %all-gather.3.cloned.1.call-done.all_ref.inputs_ref.right_ref, ...), custom_call_target="tpu_custom_call" | custom-call | bytes 54211380 | tf_op jit(solution)/shard_map/down_first/pallas_call | solution.py:407
  93.4 1.1 copy-done.2
  94.5 19.2 %hidden_rows.1 = (bf16[24,256,384]{2,1,0:T(8,128)(2,1)}, bf16[24,64,512]{2,1,0:T(8,128)(2,1)}, bf16[1024,512]{1,0:T(8,128)(2,1)}, bf16[1024,512]{1,0:T(8,128)(2,...) custom-call(s32[4]{0:T(128)} %and_select_fusion.1.run_ref, s32[2,24]{1,0:T(2,128)} %select_reduce_fusion.place_ref, ...), custom_call_target="tpu_custom_call" | custom-call | bytes 55364812 | tf_op jit(solution)/shard_map/hidden_rows/pallas_call | solution.py:353
  113.8 0.3 collective-permute-start.5
  114.1 0.3 collective-permute-start.9
  114.4 1.7 collective-permute-start.10
  116.1 0.6 dynamic-slice_subtract_fusion.1.perm_ref
  116.7 0.5 and_select_fusion.run_ref
  117.3 1.7 collective-permute-done.4.refs_3_.refs_0_
  119.0 1.0 copy-done.4
  119.9 0.5 copy-done.3
  120.4 10.3 %back_pass.1 = (bf16[128,6144]{1,0:T(8,128)(2,1)}, bf16[128,1536]{1,0:T(8,128)(2,1)}, bf16[128,1536]{1,0:T(8,128)(2,1)}, bf16[128,1536]{1,0:T(8,128)(2,1)}, bf16[128,1536]{1,0:T(8,128)(2,1)}) custom-call(s32[24]{0:T(128)} %dynamic-slice_subtract_fusion.1.perm_ref, s32[4]{0:T(128)} %and_select_fusion.run_ref, ...), custom_call_target="tpu_custom_call" | custom-call | bytes 24222104 | tf_op jit(solution)/shard_map/back_pass/pallas_call | solution.py:228
  130.8 9.7 %down_rest.1 = (bf16[128,1536]{1,0:T(8,128)(2,1)}, f32[2048,384]{1,0:T(8,128)}, bf16[384,1536]{1,0:T(8,128)(2,1)}) custom-call(s32[4]{0:T(128)} %and_select_fusion.1.run_ref, bf16[128,6144]{1,0:T(8,128)(2,1)} %get-tuple-element.31.act_ref.own_act_ref, bf16[6144,1536]{1,0:T(8,128)(2,1)} %bitcast.14, f32[128,1536]{1,0:T(8,128)} %get-tuple-element.34.refs_0_.partial_ref, ...), custom_call_target="tpu_custom_call" | custom-call | bytes 17301504 | tf_op jit(solution)/shard_map/down_rest/pallas_call | solution.py:460
  140.4 11.0 %added_nt.1.refs_3_.refs_19_ = bf16[128,1536]{1,0:T(8,128)(2,1)} custom-call(bf16[128,6144]{1,0:T(8,128)(2,1)} %get-tuple-element.39.refs_0_.left_ref, bf16[1536,6144]{1,0:T(8,128)(2,1)} %bitcast.17, bf16[128,1536]{1,0:T(8,128)(2,1)} %own_ref.3, bf16[128,1536]{1,0:T(8,128)(2,1)} %get-tuple-element.26.refs_0_), custom_call_target="tpu_custom_call" | custom-call | bytes 45848984 | tf_op jit(solution)/shard_map/added_nt/pallas_call | solution.py:302
  151.5 1.6 collective-permute-start.6
  153.1 2.7 %collective-permute-start.7 = (bf16[128,1536]{1,0:T(8,128)(2,1)}, bf16[128,1536]{1,0:T(8,128)(2,1)S(1)}, u32[]{:S(2)}, u32[]{:S(2)}) collective-permute-start(bf16[128,1536]{1,0:T(8,128)(2,1)} %get-tuple-element.46), channel_id=1, source_target_pairs={{0,2},{1,3},{2,0},{3,1},{4,6},{5,7},{6,4},{7,5},{8,10},{9,11},{10,... | collective-permute-start | bytes 1179656 | tf_op jit(solution)/shard_map/ppermute | solution.py:25
  155.7 1.3 collective-permute-start.8
  157.0 11.6 %recomputed.1 = (f32[4,24,64,256]{3,2,1,0:T(8,128)}, bf16[8,256,384]{2,1,0:T(8,128)(2,1)}) custom-call(s32[4,24]{1,0:T(4,128)} %pad_add_fusion.index_ref, s32[1]{0:T(128)} %bitcast.6.run_ref, bf16[24,256,384]{2,1,0:T(8,128)(2,1)} %get-tuple-element.49.refs_0_.refs_1_.refs_2_, bf16[24,256,384]{2,1,0:T(8,128)(2,1)} %get-tuple-element.49.refs_0_.refs_1_.refs_2_, ...), custom_call_target="tpu_custom_call" | custom-call | bytes 20761804 | tf_op jit(solution)/shard_map/recomputed/pallas_call | solution.py:596
  168.6 4.9 %collective-permute-done.10.refs_1_ = bf16[1024,512]{1,0:T(8,128)(2,1)} collective-permute-done((bf16[1024,512]{1,0:T(8,128)(2,1)}, bf16[1024,512]{1,0:T(8,128)(2,1)}, u32[]{:S(2)}, u32[]{:S(2)}) %collective-permute-start.10) | collective-permute-done | bytes 1048608 | tf_op jit(solution)/shard_map/ppermute | solution.py:20
  173.4 1.3 all-gather.5.cloned.1.call-done.mixed_ref
  174.8 11.5 %mix_gradient.1.refs_0_ = f32[4,24,64,256]{3,2,1,0:T(8,128)} custom-call(s32[24]{0:T(128)} %dynamic-slice_subtract_fusion.1.perm_ref, bf16[512,4096]{1,0:T(8,128)(2,1)} %all-gather.5.cloned.1.call-done.mixed_ref, bf16[512,4096]{1,0:T(8,128)(2,1)} %get-tuple-element.54.grad_ref, ...), custom_call_target="tpu_custom_call", output_to_operand_aliasing={{}: (6, {})} | custom-call | bytes 18454936 | tf_op jit(solution)/shard_map/mix_gradient/pallas_call | solution.py:513
  186.2 8.9 %down_gradient_split.1.refs_4_ = f32[1536,1536]{1,0:T(8,128)} custom-call(s32[1]{0:T(128)} %bitcast.6.run_ref, bf16[512,4096]{1,0:T(8,128)(2,1)} %all-gather.5.cloned.1.call-done.mixed_ref, bf16[8,256,384]{2,1,0:T(8,128)(2,1)} %get-tuple-element.52.act_ref, bf16[128,6144]{1,0:T(8,128)(2,1)} %get-tuple-element.31.act_ref.own_act_ref, ...), custom_call_target="tpu_custom_call" | custom-call | bytes 27682406 | tf_op jit(solution)/shard_map/down_gradient_split/pallas_call | solution.py:718
  195.2 0.7 copy-done.5
  195.9 0.1 copy-done.6
  196.1 0.1 copy-done.7
  196.2 7.7 %up_gradient.1 = f32[1536,1536]{1,0:T(8,128)} custom-call(s32[4]{0:T(128)} %and_select_fusion.1.run_ref, bf16[512,3072]{1,0:T(8,128)(2,1)} %all-gather.3.cloned.1.call-done.all_ref.inputs_ref.right_ref, bf16[128,1536]{1,0:T(8,128)(2,1)} %get-tuple-element.41.refs_0_, bf16[128,1536]{1,0:T(8,128)(2,1)} %copy-done.5, bf16[128,1536]{1,0:T(8,128)(2,1)} %copy-done.6, ...), custom_call_target="tpu_custom_call" | custom-call | bytes 27682406 | tf_op jit(solution)/shard_map/up_gradient/pallas_call | solution.py:646
  (31 shorter events, 0.1 us)
Async XLA Ops:
  7.2 72.9 %all-gather.3.cloned.1.call-start = ((), (), s32[]{:S(2)}) async-start(), calls=%async_computation | async-start | bytes 3932160 | tf_op jit(solution)/shard_map/all_gather | solution.py:797
  9.3 165.5 %all-gather.5.cloned.1.call-start = ((), (), s32[]{:S(2)}) async-start(), calls=%async_computation.1 | async-start | bytes 5242880 | tf_op jit(solution)/shard_map/all_gather | solution.py:810
  9.3 12.1 %copy-start.10 = (s32[96]{0:T(128)S(1)}, s32[96]{0:T(128)}, u32[]{:S(2)}) copy-start(s32[96]{0:T(128)} %param.13) | copy-start | bytes 1156
  9.4 12.1 %copy-start.9 = (s32[2,96]{1,0:T(2,128)S(1)}, s32[2,96]{1,0:T(2,128)}, u32[]{:S(2)}) copy-start(s32[2,96]{1,0:T(2,128)} %param.12) | copy-start | bytes 2308
  18.4 4.4 %collective-permute-start.1 = (bf16[128,6144]{1,0:T(8,128)(2,1)}, bf16[128,6144]{1,0:T(8,128)(2,1)S(1)}, u32[]{:S(2)}, u32[]{:S(2)}) collective-permute-start(bf16[128,6144]{1,0:T(8,128)(2,1)} %dense.1.refs_0_.refs_5_.refs_6_.refs_7_.refs_8_), channel_id=1, source_target_pairs={{0,4},{4,0},{8,12},{12,8},{1,5},{5,1},{9,13},{13,9},{2,6},{6,2},{1... | collective-permute-start | bytes 4718600 | tf_op jit(solution)/shard_map/ppermute | solution.py:20
  18.8 37.8 %collective-permute-start = (bf16[128,6144]{1,0:T(8,128)(2,1)}, bf16[128,6144]{1,0:T(8,128)(2,1)S(1)}, u32[]{:S(2)}, u32[]{:S(2)}) collective-permute-start(bf16[128,6144]{1,0:T(8,128)(2,1)} %dense.1.refs_0_.refs_5_.refs_6_.refs_7_.refs_8_), channel_id=1, source_target_pairs={{0,8},{4,12},{8,0},{12,4},{1,9},{5,13},{9,1},{13,5},{2,10},{6,14},... | collective-permute-start | bytes 4718600 | tf_op jit(solution)/shard_map/ppermute | solution.py:20
  21.6 13.5 %copy-start.8 = (s32[2,24]{1,0:T(2,128)}, s32[2,24]{1,0:T(2,128)S(1)}, u32[]{:S(2)}) copy-start(s32[2,24]{1,0:T(2,128)S(1)} %dynamic-slice_subtract_fusion.target_ref) | copy-start | bytes 580
  22.8 1.1 copy-start
  56.6 1.2 copy-start.1
  77.0 16.4 %collective-permute-start.2 = (bf16[128,6144]{1,0:T(8,128)(2,1)}, bf16[128,6144]{1,0:T(8,128)(2,1)S(1)}, u32[]{:S(2)}, u32[]{:S(2)}) collective-permute-start(bf16[128,6144]{1,0:T(8,128)(2,1)} %get-tuple-element.33.refs_0_), channel_id=1, source_target_pairs={{0,4},{4,0},{8,12},{12,8},{1,5},{5,1},{9,13},{13,9},{2,6},{6,2},{1... | collective-permute-start | bytes 4718600 | tf_op jit(solution)/shard_map/ppermute | solution.py:20
  78.4 38.9 %collective-permute-start.3 = (bf16[128,6144]{1,0:T(8,128)(2,1)}, bf16[128,6144]{1,0:T(8,128)(2,1)}, u32[]{:S(2)}, u32[]{:S(2)}) collective-permute-start(bf16[128,6144]{1,0:T(8,128)(2,1)} %get-tuple-element.35), channel_id=1, source_target_pairs={{0,8},{4,12},{8,0},{12,4},{1,9},{5,13},{9,1},{13,5},{2,10},{6,14},... | collective-permute-start | bytes 4718600 | tf_op jit(solution)/shard_map/ppermute | solution.py:20
  93.4 1.1 copy-start.2
  113.8 5.2 %collective-permute-start.5 = (bf16[2048,384]{1,0:T(8,128)(2,1)}, bf16[2048,384]{1,0:T(8,128)(2,1)S(1)}, u32[]{:S(2)}, u32[]{:S(2)}) collective-permute-start(bf16[2048,384]{1,0:T(8,128)(2,1)} %get-tuple-element.38), channel_id=1, source_target_pairs={{0,4},{4,0},{8,12},{12,8},{1,5},{5,1},{9,13},{13,9},{2,6},{6,2},{1... | collective-permute-start | bytes 4718600 | tf_op jit(solution)/shard_map/ppermute | solution.py:20
  114.1 42.9 %collective-permute-start.9 = (bf16[2048,384]{1,0:T(8,128)(2,1)}, bf16[2048,384]{1,0:T(8,128)(2,1)}, u32[]{:S(2)}, u32[]{:S(2)}) collective-permute-start(bf16[2048,384]{1,0:T(8,128)(2,1)} %get-tuple-element.50), channel_id=1, source_target_pairs={{0,8},{4,12},{8,0},{12,4},{1,9},{5,13},{9,1},{13,5},{2,10},{6,14},... | collective-permute-start | bytes 4718600 | tf_op jit(solution)/shard_map/ppermute | solution.py:20
  114.4 4.5 %collective-permute-start.4 = (bf16[1024,512]{1,0:T(8,128)(2,1)}, bf16[1024,512]{1,0:T(8,128)(2,1)S(1)}, u32[]{:S(2)}, u32[]{:S(2)}) collective-permute-start(bf16[1024,512]{1,0:T(8,128)(2,1)} %get-tuple-element.37), channel_id=1, source_target_pairs={{0,4},{4,0},{8,12},{12,8},{1,5},{5,1},{9,13},{13,9},{2,6},{6,2},{1... | collective-permute-start | bytes 3145736 | tf_op jit(solution)/shard_map/ppermute | solution.py:20
  114.4 59.0 %collective-permute-start.10 = (bf16[1024,512]{1,0:T(8,128)(2,1)}, bf16[1024,512]{1,0:T(8,128)(2,1)}, u32[]{:S(2)}, u32[]{:S(2)}) collective-permute-start(bf16[1024,512]{1,0:T(8,128)(2,1)} %get-tuple-element.55), channel_id=1, source_target_pairs={{0,8},{4,12},{8,0},{12,4},{1,9},{5,13},{9,1},{13,5},{2,10},{6,14},... | collective-permute-start | bytes 3145736 | tf_op jit(solution)/shard_map/ppermute | solution.py:20
  119.0 1.0 copy-start.4
  119.0 1.5 copy-start.3
  151.5 43.7 %collective-permute-start.6 = (bf16[128,1536]{1,0:T(8,128)(2,1)}, bf16[128,1536]{1,0:T(8,128)(2,1)S(1)}, u32[]{:S(2)}, u32[]{:S(2)}) collective-permute-start(bf16[128,1536]{1,0:T(8,128)(2,1)} %get-tuple-element.45), channel_id=1, source_target_pairs={{0,1},{1,2},{2,3},{3,0},{4,5},{5,6},{6,7},{7,4},{8,9},{9,10},{10,1... | collective-permute-start | bytes 1179656 | tf_op jit(solution)/shard_map/ppermute | solution.py:25
  153.1 42.1 %collective-permute-start.7 = (bf16[128,1536]{1,0:T(8,128)(2,1)}, bf16[128,1536]{1,0:T(8,128)(2,1)S(1)}, u32[]{:S(2)}, u32[]{:S(2)}) collective-permute-start(bf16[128,1536]{1,0:T(8,128)(2,1)} %get-tuple-element.46), channel_id=1, source_target_pairs={{0,2},{1,3},{2,0},{3,1},{4,6},{5,7},{6,4},{7,5},{8,10},{9,11},{10,... | collective-permute-start | bytes 1179656 | tf_op jit(solution)/shard_map/ppermute | solution.py:25
  155.7 39.5 %collective-permute-start.8 = (bf16[128,1536]{1,0:T(8,128)(2,1)}, bf16[128,1536]{1,0:T(8,128)(2,1)S(1)}, u32[]{:S(2)}, u32[]{:S(2)}) collective-permute-start(bf16[128,1536]{1,0:T(8,128)(2,1)} %get-tuple-element.47), channel_id=1, source_target_pairs={{0,3},{1,0},{2,1},{3,2},{4,7},{5,4},{6,5},{7,6},{8,11},{9,8},{10,9... | collective-permute-start | bytes 1179656 | tf_op jit(solution)/shard_map/ppermute | solution.py:25
  195.2 0.8 copy-start.5
  195.2 0.9 copy-start.6
  195.2 1.0 copy-start.7
Sparse Core Ops, SparseCore 0:
  10.1 66.1 all-gather.2
  77.9 96.7 all-gather.4

commit v5 on v4

--- a/solution.py
+++ b/solution.py
@@ -89,7 +89,7 @@
 def mixed_near(sources, which, index, levels, mix_weight, after=()):
     rows, width = sources[0].shape
     blocks, size = mix_weight.shape[1], mix_weight.shape[2]
-    chunk = chunk_of(blocks, 4)
+    chunk = chunk_of(blocks, 8)
     count = len(levels)
     near_shape = jax.ShapeDtypeStruct((rows, width), F32)
 
@@ -124,7 +124,7 @@
 def mixed_last(source, index, level, mix_weight, near, act_grad, kept, after=()):
     rows, width = source.shape
     blocks, size = mix_weight.shape[1], mix_weight.shape[2]
-    chunk = chunk_of(math.gcd(blocks, kept), 4)
+    chunk = chunk_of(math.gcd(blocks, kept), 8)
 
     def kernel(index_ref, source_ref, weight_ref, near_ref, grad_ref, *refs):
         mixed_ref, act_ref, delta_ref = refs[-3:]
@@ -167,7 +167,7 @@
 def far_terms(delta, targets, levels, mix_weight, after=()):
     rows, width = delta.shape
     blocks, size = mix_weight.shape[1], mix_weight.shape[2]
-    chunk = chunk_of(blocks, 4)
+    chunk = chunk_of(blocks, 8)
     count = len(levels)
 
     def kernel(target_ref, delta_ref, *refs):
@@ -198,7 +198,7 @@
 def back_pass(delta, perm, mix_weight, terms, run_next, after=()):
     rows, width = delta.shape
     blocks, size = mix_weight.shape[1], mix_weight.shape[2]
-    chunk = chunk_of(blocks, 4)
+    chunk = chunk_of(blocks, 8)
     runs = run_next.shape[0]
     share = width // runs
     split = share % 128 == 0
@@ -317,7 +317,7 @@
     depth, width = up.shape
     tokens = gathered.shape[0]
     size = width // blocks
-    chunk = chunk_of(blocks, 4)
+    chunk = chunk_of(blocks, 6)
     levels = places.shape[0]
     again = blocks - kept
     others = tokens - rows
@@ -483,7 +483,7 @@
     )(run_rows, activated, down, partial, gathered, *after)
 
 
-def mix_gradient(mixed_all, act_grad_all, hidden_part, received, perm, scale, made=None):
+def mix_gradient(mixed_all, act_grad_all, hidden_part, received, perm, scale, made=None, after=()):
     tokens, width = mixed_all.shape
     blocks, part, _ = hidden_part.shape
     size = part * lax.axis_size("dp")
@@ -517,7 +517,8 @@
             grid=(kept // chunk,),
             in_specs=[columns, columns, whole(hidden_part.shape)]
             + [given] * len(received)
-            + ([] if made is None else [ANY]),
+            + ([] if made is None else [ANY])
+            + [ANY] * len(after),
             out_specs=pl.BlockSpec((count, chunk, part, size), lambda i, *_: (0, i, 0, 0)),
         ),
         out_shape=jax.ShapeDtypeStruct((count, blocks, part, size), F32),
@@ -525,7 +526,7 @@
         compiler_params=params(),
         name="mix_gradient",
         cost_estimate=cost(mixed_all, act_grad_all),
-    )(perm, mixed_all, act_grad_all, hidden_part, *received, *([] if made is None else [made]))
+    )(perm, mixed_all, act_grad_all, hidden_part, *received, *([] if made is None else [made]), *after)
 
 
 def recomputed(
@@ -829,26 +830,26 @@
             activated, down, outputs, gathered, run_rows, kept * size, after=(hidden_grad,)
         )
     input_grad = dense_added(hidden_grad, up, out_grad, True, after=(outputs,))
-    to_send = [to_send[0]] + list(held(to_send[1:], (input_grad,)))
+    to_send = [to_send[0]] + list(held(to_send[1:], (input_grad, mixed_all)))
     hidden_grad_pieces = [to_send[0]] + [rotated(to_send[s], "dp", s) for s in range(1, runs)]
     made, act_rest = None, input_grad
     if again:
         made, act_rest = recomputed(
             [hidden, hidden] + received, delta, others, whole_sources, index, rest[0], run[None],
-            mix_weight, scale, after=(input_grad,),
+            mix_weight, scale, after=to_send[1:2],
         )
-    mix_grad = mix_gradient(
-        mixed_all, act_grad_all, hidden_part, part_sources, perm_here, scale, made
-    )
     if again:
         down_grad = down_gradient_split(
             mixed_all, act_rest, activated, gathered, out_grad, rest[1], run[None], share, scale,
-            after=(mix_grad,),
         )
     else:
-        down_grad = down_gradient(mixed_all, gathered, run, share, scale, after=(mix_grad,))
+        down_grad = down_gradient(mixed_all, gathered, run, share, scale)
+    mix_grad = mix_gradient(
+        mixed_all, act_grad_all, hidden_part, part_sources, perm_here, scale, made,
+        after=(down_grad,),
+    )
     up_grad = up_gradient(
-        gathered, up.shape[0], hidden_grad_pieces, run_rows, scale, after=(down_grad,)
+        gathered, up.shape[0], hidden_grad_pieces, run_rows, scale, after=(mix_grad,)
     )
     return (outputs, input_grad, up_grad[None], mix_grad, down_grad[None])
 

time: 212 us -> 208 us (0.981)
  Pallas kernels: 152 us -> 149 us
  starting transfers between devices: 12.7 us -> 10 us
    all_gather x1, waiting for transfers between devices: 1.32 us -> 7.35 us  [body(): mixed_all = lax.all_gather(mixed, 'dp', axis=0, tiled=True)]
    ppermute x8, waiting for transfers between devices: 18.8 us -> 14.6 us  [from_partner(): return lax.ppermute(value, axis, pairs)]
    ppermute x3, starting transfers between devices: 5.52 us -> 2.97 us  [rotated(): lax.ppermute(value, axis, [(i, (i + shift) % size) for i in range(size)])]
  transfers between devices with their start and end apart: 13 -> 13, of which waited for: 4 -> 3; matrix products, arithmetic and copies ran while one was open for 2% -> 2% of each run, Pallas kernels for 68% -> 68%
where the time goes in v5:
time: 208 us; the launch traced here: 207 us
  Pallas kernels  149 us (72%)
  waiting for transfers between devices  22 us (11%)
  between operations  14.1 us (7%)
  starting transfers between devices  10 us (5%)
  local copies, waits for them, and re-layouts  6.58 us (3%)
  other arithmetic  5.37 us (3%)
    pallas_call x2, Pallas kernels, dense(): pl.pallas_call(kernel, grid=(width // step,), in_specs=[whole((rows, dept...  20.2 us
    pallas_call x1, Pallas kernels, hidden_rows(): pl.pallas_call(kernel, grid_spec=pltpu.PrefetchScalarGridSpec(num_scalar_...  19.2 us
    ppermute x8, waiting for transfers between devices, from_partner(): return lax.ppermute(value, axis, pairs)  14.6 us
    pallas_call x1, Pallas kernels, down_first(): pl.pallas_call(kernel, grid=(kept // step,), in_specs=[pl.BlockSpec((rows...  13.4 us
    pallas_call x1, Pallas kernels, recomputed(): pl.pallas_call(kernel, grid_spec=pltpu.PrefetchScalarGridSpec(num_scalar_...  11.5 us
    pallas_call x1, Pallas kernels, mix_gradient(): pl.pallas_call(kernel, grid_spec=pltpu.PrefetchScalarGridSpec(num_scalar_...  11.5 us
    pallas_call x1, Pallas kernels, dense_added(): pl.pallas_call(kernel, grid=(depth // step,), in_specs=[pl.BlockSpec((row...  11 us
    pallas_call x1, Pallas kernels, mixed_last(): pl.pallas_call(kernel, grid_spec=pltpu.PrefetchScalarGridSpec(num_scalar_...  10.6 us
  transfers between devices with their start and end apart: 13, of which 3 were waited for; matrix products, arithmetic and copies ran while one was open for 2% of the time, Pallas kernels for 68%

profile of v5, /device:TPU:0, one launch (start us, length us, event | category | flops | bytes accessed | tf_op | source)
XLA Modules:
  0.0 207.3 jit_solution(558109168124850260)
XLA Ops:
  7.2 0.0 all-gather.3.cloned.1.call-start
  7.2 2.1 pad_maximum_fusion
  9.3 0.0 all-gather.5.cloned.1.call-start
  9.4 9.0 %dense.1.refs_0_.refs_5_.refs_6_.refs_7_.refs_8_ = bf16[128,6144]{1,0:T(8,128)(2,1)} custom-call(bf16[128,1536]{1,0:T(8,128)(2,1)} %base_ref.2, bf16[1536,6144]{1,0:T(8,128)(2,1)} %bitcast.15), custom_call_target="tpu_custom_call" | custom-call | bytes 45848984 | tf_op jit(solution)/shard_map/dense/pallas_call | solution.py:267
  18.4 0.5 collective-permute-start.1
  18.8 2.5 %collective-permute-start = (bf16[128,6144]{1,0:T(8,128)(2,1)}, bf16[128,6144]{1,0:T(8,128)(2,1)S(1)}, u32[]{:S(2)}, u32[]{:S(2)}) collective-permute-start(bf16[128,6144]{1,0:T(8,128)(2,1)} %dense.1.refs_0_.refs_5_.refs_6_.refs_7_.refs_8_), channel_id=1, source_target_pairs={{0,8},{4,12},{8,0},{12,4},{1,9},{5,13},{9,1},{13,5},{2,10},{6,14},... | collective-permute-start | bytes 4718600 | tf_op jit(solution)/shard_map/ppermute | solution.py:20
  21.3 0.1 pad_add_fusion.2
  21.4 0.1 fusion.5
  21.5 0.1 dynamic-slice_subtract_fusion.target_ref
  21.6 0.6 pad_add_fusion.index_ref
  22.2 0.5 slice_bitcast_fusion.index_ref
  22.7 1.2 copy-done
  23.9 11.2 %dense_nt.1.refs_5_.grad_ref = f32[128,6144]{1,0:T(8,128)} custom-call(bf16[128,1536]{1,0:T(8,128)(2,1)} %own_ref.3, bf16[6144,1536]{1,0:T(8,128)(2,1)} %bitcast.12, bf16[128,6144]{1,0:T(8,128)(2,1)} %copy-done), custom_call_target="tpu_custom_call" | custom-call | bytes 49309288 | tf_op jit(solution)/shard_map/dense_nt/pallas_call | solution.py:267
  35.0 8.7 %mixed_near.1.near_ref = f32[128,6144]{1,0:T(8,128)} custom-call(s32[3,24]{1,0:T(4,128)} %bitcast.20, bf16[128,6144]{1,0:T(8,128)(2,1)} %dense.1.refs_0_.refs_5_.refs_6_.refs_7_.refs_8_, bf16[128,6144]{1,0:T(8,128)(2,1)} %copy-done, bf16[4,24,256,256]{3,2,1,0:T(8,128)(2,1)} %refs_16_.1, bf16[4,24,256,256]{3,2,1,0:T(8,128)(2,1)} %refs_16_.1, ...), custom_call_target="tpu_custom_call" | custom-call | bytes 34603008 | tf_op jit(solution)/shard_map/mixed_near/pallas_call | solution.py:107
  43.7 12.9 %collective-permute-done.source_ref.refs_11_.refs_12_ = bf16[128,6144]{1,0:T(8,128)(2,1)S(1)} collective-permute-done((bf16[128,6144]{1,0:T(8,128)(2,1)}, bf16[128,6144]{1,0:T(8,128)(2,1)S(1)}, u32[]{:S(2)}, u32[]{:S(2)}) %collective-permute-start) | collective-permute-done | bytes 1572896 | tf_op jit(solution)/shard_map/ppermute | solution.py:20
  56.6 1.2 copy-done.1
  57.8 10.6 %mixed_last.1 = (bf16[128,4096]{1,0:T(8,128)(2,1)}, bf16[128,6144]{1,0:T(8,128)(2,1)}, bf16[128,6144]{1,0:T(8,128)(2,1)}) custom-call(s32[24]{0:T(128)} %slice_bitcast_fusion.index_ref, bf16[128,6144]{1,0:T(8,128)(2,1)} %copy-done.1, bf16[4,24,256,256]{3,2,1,0:T(8,128)(2,1)} %refs_16_.1, f32[128,6144]{1,0:T(8,128)} %mixed_near.1.near_ref, ...), custom_call_target="tpu_custom_call" | custom-call | bytes 31142708 | tf_op jit(solution)/shard_map/mixed_last/pallas_call | solution.py:145
  68.4 7.4 %far_terms.1 = (bf16[128,6144]{1,0:T(8,128)(2,1)}, bf16[128,6144]{1,0:T(8,128)(2,1)}) custom-call(s32[2,24]{1,0:T(2,128)} %copy-done.8, bf16[128,6144]{1,0:T(8,128)(2,1)} %get-tuple-element.32.delta_ref.refs_18_, bf16[4,24,256,256]{3,2,1,0:T(8,128)(2,1)} %refs_16_.1, bf16[4,24,256,256]{3,2,1,0:T(8,128)(2,1)} %refs_16_.1), custom_call_target="tpu_custom_call" | custom-call | bytes 24222104 | tf_op jit(solution)/shard_map/far_terms/pallas_call | solution.py:181
  75.8 0.0 collective-permute-start.2
  75.9 0.6 and_select_fusion.1.run_ref
  76.4 0.1 fusion
  76.5 0.7 select_reduce_fusion.place_ref
  77.2 1.7 collective-permute-start.3
  78.9 13.4 %down_first.1 = (f32[128,1536]{1,0:T(8,128)}, bf16[512,4096]{1,0:T(8,128)(2,1)}) custom-call(bf16[128,6144]{1,0:T(8,128)(2,1)} %get-tuple-element.31.act_ref.own_act_ref, bf16[6144,1536]{1,0:T(8,128)(2,1)} %bitcast.13, bf16[128,1536]{1,0:T(8,128)(2,1)} %base_ref.2, bf16[512,3072]{1,0:T(8,128)(2,1)} %all-gather.3.cloned.1.call-done.all_ref.inputs_ref.right_ref, ...), custom_call_target="tpu_custom_call" | custom-call | bytes 54211380 | tf_op jit(solution)/shard_map/down_first/pallas_call | solution.py:407
  92.3 1.1 copy-done.2
  93.5 19.2 %hidden_rows.1 = (bf16[24,256,384]{2,1,0:T(8,128)(2,1)}, bf16[24,64,512]{2,1,0:T(8,128)(2,1)}, bf16[1024,512]{1,0:T(8,128)(2,1)}, bf16[1024,512]{1,0:T(8,128)(2,...) custom-call(s32[4]{0:T(128)} %and_select_fusion.1.run_ref, s32[2,24]{1,0:T(2,128)} %select_reduce_fusion.place_ref, ...), custom_call_target="tpu_custom_call" | custom-call | bytes 55364812 | tf_op jit(solution)/shard_map/hidden_rows/pallas_call | solution.py:353
  112.6 0.3 collective-permute-start.5
  112.9 0.4 collective-permute-start.10
  113.3 1.6 collective-permute-start.9
  115.0 0.6 dynamic-slice_subtract_fusion.1.perm_ref
  115.6 0.5 and_select_fusion.run_ref
  116.1 1.7 collective-permute-done.4.refs_3_.refs_0_
  117.8 1.0 copy-done.4
  118.8 0.6 copy-done.3
  119.4 9.3 %back_pass.1 = (bf16[128,6144]{1,0:T(8,128)(2,1)}, bf16[128,1536]{1,0:T(8,128)(2,1)}, bf16[128,1536]{1,0:T(8,128)(2,1)}, bf16[128,1536]{1,0:T(8,128)(2,1)}, bf16[128,1536]{1,0:T(8,128)(2,1)}) custom-call(s32[24]{0:T(128)} %dynamic-slice_subtract_fusion.1.perm_ref, s32[4]{0:T(128)} %and_select_fusion.run_ref, ...), custom_call_target="tpu_custom_call" | custom-call | bytes 24222104 | tf_op jit(solution)/shard_map/back_pass/pallas_call | solution.py:228
  128.7 9.7 %down_rest.1 = (bf16[128,1536]{1,0:T(8,128)(2,1)}, f32[2048,384]{1,0:T(8,128)}, bf16[384,1536]{1,0:T(8,128)(2,1)}) custom-call(s32[4]{0:T(128)} %and_select_fusion.1.run_ref, bf16[128,6144]{1,0:T(8,128)(2,1)} %get-tuple-element.31.act_ref.own_act_ref, bf16[6144,1536]{1,0:T(8,128)(2,1)} %bitcast.14, f32[128,1536]{1,0:T(8,128)} %get-tuple-element.34.refs_0_.partial_ref, ...), custom_call_target="tpu_custom_call" | custom-call | bytes 17301504 | tf_op jit(solution)/shard_map/down_rest/pallas_call | solution.py:460
  138.5 11.0 %added_nt.1.refs_3_ = bf16[128,1536]{1,0:T(8,128)(2,1)} custom-call(bf16[128,6144]{1,0:T(8,128)(2,1)} %get-tuple-element.39.refs_0_.left_ref, bf16[1536,6144]{1,0:T(8,128)(2,1)} %bitcast.17, bf16[128,1536]{1,0:T(8,128)(2,1)} %own_ref.3, bf16[128,1536]{1,0:T(8,128)(2,1)} %get-tuple-element.26.refs_0_), custom_call_target="tpu_custom_call" | custom-call | bytes 45848984 | tf_op jit(solution)/shard_map/added_nt/pallas_call | solution.py:302
  149.5 7.4 %all-gather.5.cloned.1.call-done.refs_4_.mixed_ref = bf16[512,4096]{1,0:T(8,128)(2,1)} async-done(((bf16[128,4096]{1,0:T(8,128)(2,1)}), bf16[512,4096]{1,0:T(8,128)(2,1)}) %all-gather.5.cloned.1.call-update) | async-done | bytes 4194320 | tf_op jit(solution)/shard_map/all_gather | solution.py:811
  156.8 0.9 collective-permute-start.7
  157.8 0.3 collective-permute-start.8
  158.0 1.8 collective-permute-start.6
  159.8 11.5 %recomputed.1 = (f32[4,24,64,256]{3,2,1,0:T(8,128)}, bf16[8,256,384]{2,1,0:T(8,128)(2,1)}) custom-call(s32[4,24]{1,0:T(4,128)} %pad_add_fusion.index_ref, s32[1]{0:T(128)} %bitcast.6.run_ref, bf16[24,256,384]{2,1,0:T(8,128)(2,1)} %get-tuple-element.51.refs_0_.refs_1_.refs_2_, bf16[24,256,384]{2,1,0:T(8,128)(2,1)} %get-tuple-element.51.refs_0_.refs_1_.refs_2_, ...), custom_call_target="tpu_custom_call" | custom-call | bytes 20761804 | tf_op jit(solution)/shard_map/recomputed/pallas_call | solution.py:597
  171.3 9.0 %down_gradient_split.1.refs_3_ = f32[1536,1536]{1,0:T(8,128)} custom-call(s32[1]{0:T(128)} %bitcast.6.run_ref, bf16[512,4096]{1,0:T(8,128)(2,1)} %all-gather.5.cloned.1.call-done.refs_4_.mixed_ref, bf16[8,256,384]{2,1,0:T(8,128)(2,1)} %get-tuple-element.55.act_ref, bf16[128,6144]{1,0:T(8,128)(2,1)} %get-tuple-element.31.act_ref.own_act_ref, ...), custom_call_target="tpu_custom_call" | custom-call | bytes 27682406 | tf_op jit(solution)/shard_map/down_gradient_split/pallas_call | solution.py:719
  180.3 11.5 %mix_gradient.1.refs_4_ = f32[4,24,64,256]{3,2,1,0:T(8,128)} custom-call(s32[24]{0:T(128)} %dynamic-slice_subtract_fusion.1.perm_ref, bf16[512,4096]{1,0:T(8,128)(2,1)} %all-gather.5.cloned.1.call-done.refs_4_.mixed_ref, bf16[512,4096]{1,0:T(8,128)(2,1)} %get-tuple-element.49.grad_ref, ...), custom_call_target="tpu_custom_call", output_to_operand_aliasing={{}: (6, {})} | custom-call | bytes 18454936 | tf_op jit(solution)/shard_map/mix_gradient/pallas_call | solution.py:513
  191.8 0.7 copy-done.5
  192.5 0.1 copy-done.6
  192.7 0.2 copy-done.7
  192.8 7.7 %up_gradient.1 = f32[1536,1536]{1,0:T(8,128)} custom-call(s32[4]{0:T(128)} %and_select_fusion.1.run_ref, bf16[512,3072]{1,0:T(8,128)(2,1)} %all-gather.3.cloned.1.call-done.all_ref.inputs_ref.right_ref, bf16[128,1536]{1,0:T(8,128)(2,1)} %get-tuple-element.41.refs_0_, bf16[128,1536]{1,0:T(8,128)(2,1)} %copy-done.7, bf16[128,1536]{1,0:T(8,128)(2,1)} %copy-done.5, ...), custom_call_target="tpu_custom_call" | custom-call | bytes 27682406 | tf_op jit(solution)/shard_map/up_gradient/pallas_call | solution.py:647
  (31 shorter events, 0.1 us)
Async XLA Ops:
  7.2 71.8 %all-gather.3.cloned.1.call-start = ((), (), s32[]{:S(2)}) async-start(), calls=%async_computation | async-start | bytes 3932160 | tf_op jit(solution)/shard_map/all_gather | solution.py:798
  9.3 147.5 %all-gather.5.cloned.1.call-start = ((), (), s32[]{:S(2)}) async-start(), calls=%async_computation.1 | async-start | bytes 5242880 | tf_op jit(solution)/shard_map/all_gather | solution.py:811
  9.4 12.1 %copy-start.10 = (s32[96]{0:T(128)S(1)}, s32[96]{0:T(128)}, u32[]{:S(2)}) copy-start(s32[96]{0:T(128)} %param.13) | copy-start | bytes 1156
  9.4 12.1 %copy-start.9 = (s32[2,96]{1,0:T(2,128)S(1)}, s32[2,96]{1,0:T(2,128)}, u32[]{:S(2)}) copy-start(s32[2,96]{1,0:T(2,128)} %param.12) | copy-start | bytes 2308
  18.4 4.3 %collective-permute-start.1 = (bf16[128,6144]{1,0:T(8,128)(2,1)}, bf16[128,6144]{1,0:T(8,128)(2,1)S(1)}, u32[]{:S(2)}, u32[]{:S(2)}) collective-permute-start(bf16[128,6144]{1,0:T(8,128)(2,1)} %dense.1.refs_0_.refs_5_.refs_6_.refs_7_.refs_8_), channel_id=1, source_target_pairs={{0,4},{4,0},{8,12},{12,8},{1,5},{5,1},{9,13},{13,9},{2,6},{6,2},{1... | collective-permute-start | bytes 4718600 | tf_op jit(solution)/shard_map/ppermute | solution.py:20
  18.8 37.8 %collective-permute-start = (bf16[128,6144]{1,0:T(8,128)(2,1)}, bf16[128,6144]{1,0:T(8,128)(2,1)S(1)}, u32[]{:S(2)}, u32[]{:S(2)}) collective-permute-start(bf16[128,6144]{1,0:T(8,128)(2,1)} %dense.1.refs_0_.refs_5_.refs_6_.refs_7_.refs_8_), channel_id=1, source_target_pairs={{0,8},{4,12},{8,0},{12,4},{1,9},{5,13},{9,1},{13,5},{2,10},{6,14},... | collective-permute-start | bytes 4718600 | tf_op jit(solution)/shard_map/ppermute | solution.py:20
  21.6 13.5 %copy-start.8 = (s32[2,24]{1,0:T(2,128)}, s32[2,24]{1,0:T(2,128)S(1)}, u32[]{:S(2)}) copy-start(s32[2,24]{1,0:T(2,128)S(1)} %dynamic-slice_subtract_fusion.target_ref) | copy-start | bytes 580
  22.7 1.2 copy-start
  56.6 1.2 copy-start.1
  75.8 16.5 %collective-permute-start.2 = (bf16[128,6144]{1,0:T(8,128)(2,1)}, bf16[128,6144]{1,0:T(8,128)(2,1)S(1)}, u32[]{:S(2)}, u32[]{:S(2)}) collective-permute-start(bf16[128,6144]{1,0:T(8,128)(2,1)} %get-tuple-element.33.refs_0_), channel_id=1, source_target_pairs={{0,4},{4,0},{8,12},{12,8},{1,5},{5,1},{9,13},{13,9},{2,6},{6,2},{1... | collective-permute-start | bytes 4718600 | tf_op jit(solution)/shard_map/ppermute | solution.py:20
  77.2 38.9 %collective-permute-start.3 = (bf16[128,6144]{1,0:T(8,128)(2,1)}, bf16[128,6144]{1,0:T(8,128)(2,1)}, u32[]{:S(2)}, u32[]{:S(2)}) collective-permute-start(bf16[128,6144]{1,0:T(8,128)(2,1)} %get-tuple-element.35), channel_id=1, source_target_pairs={{0,8},{4,12},{8,0},{12,4},{1,9},{5,13},{9,1},{13,5},{2,10},{6,14},... | collective-permute-start | bytes 4718600 | tf_op jit(solution)/shard_map/ppermute | solution.py:20
  92.3 1.1 copy-start.2
  112.6 5.2 %collective-permute-start.5 = (bf16[2048,384]{1,0:T(8,128)(2,1)}, bf16[2048,384]{1,0:T(8,128)(2,1)S(1)}, u32[]{:S(2)}, u32[]{:S(2)}) collective-permute-start(bf16[2048,384]{1,0:T(8,128)(2,1)} %get-tuple-element.38), channel_id=1, source_target_pairs={{0,4},{4,0},{8,12},{12,8},{1,5},{5,1},{9,13},{13,9},{2,6},{6,2},{1... | collective-permute-start | bytes 4718600 | tf_op jit(solution)/shard_map/ppermute | solution.py:20
  112.9 46.9 %collective-permute-start.10 = (bf16[2048,384]{1,0:T(8,128)(2,1)}, bf16[2048,384]{1,0:T(8,128)(2,1)}, u32[]{:S(2)}, u32[]{:S(2)}) collective-permute-start(bf16[2048,384]{1,0:T(8,128)(2,1)} %get-tuple-element.52), channel_id=1, source_target_pairs={{0,8},{4,12},{8,0},{12,4},{1,9},{5,13},{9,1},{13,5},{2,10},{6,14},... | collective-permute-start | bytes 4718600 | tf_op jit(solution)/shard_map/ppermute | solution.py:20
  113.3 4.5 %collective-permute-start.4 = (bf16[1024,512]{1,0:T(8,128)(2,1)}, bf16[1024,512]{1,0:T(8,128)(2,1)S(1)}, u32[]{:S(2)}, u32[]{:S(2)}) collective-permute-start(bf16[1024,512]{1,0:T(8,128)(2,1)} %get-tuple-element.37), channel_id=1, source_target_pairs={{0,4},{4,0},{8,12},{12,8},{1,5},{5,1},{9,13},{13,9},{2,6},{6,2},{1... | collective-permute-start | bytes 3145736 | tf_op jit(solution)/shard_map/ppermute | solution.py:20
  113.3 67.0 %collective-permute-start.9 = (bf16[1024,512]{1,0:T(8,128)(2,1)}, bf16[1024,512]{1,0:T(8,128)(2,1)}, u32[]{:S(2)}, u32[]{:S(2)}) collective-permute-start(bf16[1024,512]{1,0:T(8,128)(2,1)} %get-tuple-element.50), channel_id=1, source_target_pairs={{0,8},{4,12},{8,0},{12,4},{1,9},{5,13},{9,1},{13,5},{2,10},{6,14},... | collective-permute-start | bytes 3145736 | tf_op jit(solution)/shard_map/ppermute | solution.py:20
  117.8 1.0 copy-start.4
  117.8 1.6 copy-start.3
  156.8 34.9 %collective-permute-start.7 = (bf16[128,1536]{1,0:T(8,128)(2,1)}, bf16[128,1536]{1,0:T(8,128)(2,1)S(1)}, u32[]{:S(2)}, u32[]{:S(2)}) collective-permute-start(bf16[128,1536]{1,0:T(8,128)(2,1)} %get-tuple-element.47), channel_id=1, source_target_pairs={{0,2},{1,3},{2,0},{3,1},{4,6},{5,7},{6,4},{7,5},{8,10},{9,11},{10,... | collective-permute-start | bytes 1179656 | tf_op jit(solution)/shard_map/ppermute | solution.py:25
  157.8 34.0 %collective-permute-start.8 = (bf16[128,1536]{1,0:T(8,128)(2,1)}, bf16[128,1536]{1,0:T(8,128)(2,1)S(1)}, u32[]{:S(2)}, u32[]{:S(2)}) collective-permute-start(bf16[128,1536]{1,0:T(8,128)(2,1)} %get-tuple-element.48), channel_id=1, source_target_pairs={{0,3},{1,0},{2,1},{3,2},{4,7},{5,4},{6,5},{7,6},{8,11},{9,8},{10,9... | collective-permute-start | bytes 1179656 | tf_op jit(solution)/shard_map/ppermute | solution.py:25
  158.0 33.8 %collective-permute-start.6 = (bf16[128,1536]{1,0:T(8,128)(2,1)}, bf16[128,1536]{1,0:T(8,128)(2,1)S(1)}, u32[]{:S(2)}, u32[]{:S(2)}) collective-permute-start(bf16[128,1536]{1,0:T(8,128)(2,1)} %get-tuple-element.46.refs_19_), channel_id=1, source_target_pairs={{0,1},{1,2},{2,3},{3,0},{4,5},{5,6},{6,7},{7,4},{8,9},{9,10},{10,1... | collective-permute-start | bytes 1179656 | tf_op jit(solution)/shard_map/ppermute | solution.py:25
  191.8 0.8 copy-start.5
  191.8 0.9 copy-start.6
  191.8 1.0 copy-start.7
Sparse Core Ops, SparseCore 0:
  9.6 66.1 all-gather.2
  77.4 79.3 all-gather.4

commit v6 on v5

--- a/solution.py
+++ b/solution.py
@@ -490,7 +490,7 @@
     kept = width // size
     chunk = chunk_of(kept, 4)
     count = 2 + len(received)
-    given = whole((kept * part, tokens))
+    given = pl.BlockSpec((chunk * part, tokens), lambda i, *_: (i, 0))
 
     def kernel(perm_ref, mixed_ref, grad_ref, part_ref, *refs):
         given_refs, out_ref = refs[: len(received)], refs[-1]
@@ -500,7 +500,7 @@
             block = step * chunk + c
             slope = gelu_slope(mixed_ref[:, here].astype(F32))
             delta = (grad_ref[:, here].astype(F32) * slope).astype(BF16)
-            rows = pl.ds(pl.multiple_of(block * part, part), part)
+            rows = slice(c * part, (c + 1) * part)
             picked = jnp.concatenate(
                 [part_ref[block], part_ref[perm_ref[block]]] + [ref[rows, :] for ref in given_refs],
                 axis=0,

time: 208 us -> 208 us (level)
  no operation moved by 1% of the time
where the time goes in v6:
time: 208 us
  Pallas kernels  149 us (72%)
  waiting for transfers between devices  22.1 us (11%)
  between operations  14.1 us (7%)
  starting transfers between devices  10.1 us (5%)
  local copies, waits for them, and re-layouts  6.58 us (3%)
  other arithmetic  5.37 us (3%)
    pallas_call x2, Pallas kernels, dense(): pl.pallas_call(kernel, grid=(width // step,), in_specs=[whole((rows, dept...  20.2 us
    pallas_call x1, Pallas kernels, hidden_rows(): pl.pallas_call(kernel, grid_spec=pltpu.PrefetchScalarGridSpec(num_scalar_...  19.2 us
    ppermute x8, waiting for transfers between devices, from_partner(): return lax.ppermute(value, axis, pairs)  14.6 us
    pallas_call x1, Pallas kernels, down_first(): pl.pallas_call(kernel, grid=(kept // step,), in_specs=[pl.BlockSpec((rows...  13.4 us
    pallas_call x1, Pallas kernels, mix_gradient(): pl.pallas_call(kernel, grid_spec=pltpu.PrefetchScalarGridSpec(num_scalar_...  11.8 us
    pallas_call x1, Pallas kernels, recomputed(): pl.pallas_call(kernel, grid_spec=pltpu.PrefetchScalarGridSpec(num_scalar_...  11.5 us
    pallas_call x1, Pallas kernels, dense_added(): pl.pallas_call(kernel, grid=(depth // step,), in_specs=[pl.BlockSpec((row...  11 us
    pallas_call x1, Pallas kernels, mixed_last(): pl.pallas_call(kernel, grid_spec=pltpu.PrefetchScalarGridSpec(num_scalar_...  10.6 us
  transfers between devices with their start and end apart: 13, of which 3 were waited for; matrix products, arithmetic and copies ran while one was open for 2% of the time, Pallas kernels for 68%

profile of v6, /device:TPU:0, one launch (start us, length us, event | category | flops | bytes accessed | tf_op | source)
XLA Modules:
  0.0 207.7 jit_solution(15648783194934387769)
XLA Ops:
  7.2 0.0 all-gather.3.cloned.1.call-start
  7.2 2.1 pad_maximum_fusion
  9.3 0.0 all-gather.5.cloned.1.call-start
  9.4 9.0 %dense.1.refs_0_.refs_5_.refs_6_.refs_7_.refs_8_ = bf16[128,6144]{1,0:T(8,128)(2,1)} custom-call(bf16[128,1536]{1,0:T(8,128)(2,1)} %base_ref.2, bf16[1536,6144]{1,0:T(8,128)(2,1)} %bitcast.15), custom_call_target="tpu_custom_call" | custom-call | bytes 45848984 | tf_op jit(solution)/shard_map/dense/pallas_call | solution.py:267
  18.4 0.5 collective-permute-start.1
  18.8 2.5 %collective-permute-start = (bf16[128,6144]{1,0:T(8,128)(2,1)}, bf16[128,6144]{1,0:T(8,128)(2,1)S(1)}, u32[]{:S(2)}, u32[]{:S(2)}) collective-permute-start(bf16[128,6144]{1,0:T(8,128)(2,1)} %dense.1.refs_0_.refs_5_.refs_6_.refs_7_.refs_8_), channel_id=1, source_target_pairs={{0,8},{4,12},{8,0},{12,4},{1,9},{5,13},{9,1},{13,5},{2,10},{6,14},... | collective-permute-start | bytes 4718600 | tf_op jit(solution)/shard_map/ppermute | solution.py:20
  21.3 0.1 pad_add_fusion.2
  21.4 0.1 fusion.5
  21.5 0.1 dynamic-slice_subtract_fusion.target_ref
  21.6 0.6 pad_add_fusion.index_ref
  22.2 0.5 slice_bitcast_fusion.index_ref
  22.7 1.2 copy-done
  23.9 11.2 %dense_nt.1.refs_5_.grad_ref = f32[128,6144]{1,0:T(8,128)} custom-call(bf16[128,1536]{1,0:T(8,128)(2,1)} %own_ref.3, bf16[6144,1536]{1,0:T(8,128)(2,1)} %bitcast.12, bf16[128,6144]{1,0:T(8,128)(2,1)} %copy-done), custom_call_target="tpu_custom_call" | custom-call | bytes 49309288 | tf_op jit(solution)/shard_map/dense_nt/pallas_call | solution.py:267
  35.0 8.7 %mixed_near.1.near_ref = f32[128,6144]{1,0:T(8,128)} custom-call(s32[3,24]{1,0:T(4,128)} %bitcast.20, bf16[128,6144]{1,0:T(8,128)(2,1)} %dense.1.refs_0_.refs_5_.refs_6_.refs_7_.refs_8_, bf16[128,6144]{1,0:T(8,128)(2,1)} %copy-done, bf16[4,24,256,256]{3,2,1,0:T(8,128)(2,1)} %refs_16_.1, bf16[4,24,256,256]{3,2,1,0:T(8,128)(2,1)} %refs_16_.1, ...), custom_call_target="tpu_custom_call" | custom-call | bytes 34603008 | tf_op jit(solution)/shard_map/mixed_near/pallas_call | solution.py:107
  43.7 12.9 %collective-permute-done.source_ref.refs_11_.refs_12_ = bf16[128,6144]{1,0:T(8,128)(2,1)S(1)} collective-permute-done((bf16[128,6144]{1,0:T(8,128)(2,1)}, bf16[128,6144]{1,0:T(8,128)(2,1)S(1)}, u32[]{:S(2)}, u32[]{:S(2)}) %collective-permute-start) | collective-permute-done | bytes 1572896 | tf_op jit(solution)/shard_map/ppermute | solution.py:20
  56.6 1.2 copy-done.1
  57.8 10.6 %mixed_last.1 = (bf16[128,4096]{1,0:T(8,128)(2,1)}, bf16[128,6144]{1,0:T(8,128)(2,1)}, bf16[128,6144]{1,0:T(8,128)(2,1)}) custom-call(s32[24]{0:T(128)} %slice_bitcast_fusion.index_ref, bf16[128,6144]{1,0:T(8,128)(2,1)} %copy-done.1, bf16[4,24,256,256]{3,2,1,0:T(8,128)(2,1)} %refs_16_.1, f32[128,6144]{1,0:T(8,128)} %mixed_near.1.near_ref, ...), custom_call_target="tpu_custom_call" | custom-call | bytes 31142708 | tf_op jit(solution)/shard_map/mixed_last/pallas_call | solution.py:145
  68.4 7.4 %far_terms.1 = (bf16[128,6144]{1,0:T(8,128)(2,1)}, bf16[128,6144]{1,0:T(8,128)(2,1)}) custom-call(s32[2,24]{1,0:T(2,128)} %copy-done.8, bf16[128,6144]{1,0:T(8,128)(2,1)} %get-tuple-element.32.delta_ref.refs_18_, bf16[4,24,256,256]{3,2,1,0:T(8,128)(2,1)} %refs_16_.1, bf16[4,24,256,256]{3,2,1,0:T(8,128)(2,1)} %refs_16_.1), custom_call_target="tpu_custom_call" | custom-call | bytes 24222104 | tf_op jit(solution)/shard_map/far_terms/pallas_call | solution.py:181
  75.9 0.6 and_select_fusion.1.run_ref
  76.4 0.1 fusion
  76.5 0.7 select_reduce_fusion.place_ref
  77.2 1.7 collective-permute-start.3
  78.9 13.4 %down_first.1 = (f32[128,1536]{1,0:T(8,128)}, bf16[512,4096]{1,0:T(8,128)(2,1)}) custom-call(bf16[128,6144]{1,0:T(8,128)(2,1)} %get-tuple-element.31.act_ref.own_act_ref, bf16[6144,1536]{1,0:T(8,128)(2,1)} %bitcast.13, bf16[128,1536]{1,0:T(8,128)(2,1)} %base_ref.2, bf16[512,3072]{1,0:T(8,128)(2,1)} %all-gather.3.cloned.1.call-done.all_ref.inputs_ref.right_ref, ...), custom_call_target="tpu_custom_call" | custom-call | bytes 54211380 | tf_op jit(solution)/shard_map/down_first/pallas_call | solution.py:407
  92.3 1.1 copy-done.2
  93.4 19.2 %hidden_rows.1 = (bf16[24,256,384]{2,1,0:T(8,128)(2,1)}, bf16[24,64,512]{2,1,0:T(8,128)(2,1)}, bf16[1024,512]{1,0:T(8,128)(2,1)}, bf16[1024,512]{1,0:T(8,128)(2,...) custom-call(s32[4]{0:T(128)} %and_select_fusion.1.run_ref, s32[2,24]{1,0:T(2,128)} %select_reduce_fusion.place_ref, ...), custom_call_target="tpu_custom_call" | custom-call | bytes 55364812 | tf_op jit(solution)/shard_map/hidden_rows/pallas_call | solution.py:353
  112.6 0.3 collective-permute-start.5
  112.9 0.4 collective-permute-start.10
  113.3 0.0 collective-permute-start.4
  113.4 1.6 collective-permute-start.9
  114.9 0.6 dynamic-slice_subtract_fusion.1.perm_ref
  115.5 0.5 and_select_fusion.run_ref
  116.1 1.7 collective-permute-done.4.refs_3_.refs_0_
  117.8 1.0 copy-done.4
  118.8 0.6 copy-done.3
  119.4 9.3 %back_pass.1 = (bf16[128,6144]{1,0:T(8,128)(2,1)}, bf16[128,1536]{1,0:T(8,128)(2,1)}, bf16[128,1536]{1,0:T(8,128)(2,1)}, bf16[128,1536]{1,0:T(8,128)(2,1)}, bf16[128,1536]{1,0:T(8,128)(2,1)}) custom-call(s32[24]{0:T(128)} %dynamic-slice_subtract_fusion.1.perm_ref, s32[4]{0:T(128)} %and_select_fusion.run_ref, ...), custom_call_target="tpu_custom_call" | custom-call | bytes 24222104 | tf_op jit(solution)/shard_map/back_pass/pallas_call | solution.py:228
  128.7 9.7 %down_rest.1 = (bf16[128,1536]{1,0:T(8,128)(2,1)}, f32[2048,384]{1,0:T(8,128)}, bf16[384,1536]{1,0:T(8,128)(2,1)}) custom-call(s32[4]{0:T(128)} %and_select_fusion.1.run_ref, bf16[128,6144]{1,0:T(8,128)(2,1)} %get-tuple-element.31.act_ref.own_act_ref, bf16[6144,1536]{1,0:T(8,128)(2,1)} %bitcast.14, f32[128,1536]{1,0:T(8,128)} %get-tuple-element.34.refs_0_.partial_ref, ...), custom_call_target="tpu_custom_call" | custom-call | bytes 17301504 | tf_op jit(solution)/shard_map/down_rest/pallas_call | solution.py:460
  138.4 11.0 %added_nt.1.refs_3_ = bf16[128,1536]{1,0:T(8,128)(2,1)} custom-call(bf16[128,6144]{1,0:T(8,128)(2,1)} %get-tuple-element.39.refs_0_.left_ref, bf16[1536,6144]{1,0:T(8,128)(2,1)} %bitcast.17, bf16[128,1536]{1,0:T(8,128)(2,1)} %own_ref.3, bf16[128,1536]{1,0:T(8,128)(2,1)} %get-tuple-element.26.refs_0_), custom_call_target="tpu_custom_call" | custom-call | bytes 45848984 | tf_op jit(solution)/shard_map/added_nt/pallas_call | solution.py:302
  149.4 7.4 %all-gather.5.cloned.1.call-done.refs_4_.mixed_ref = bf16[512,4096]{1,0:T(8,128)(2,1)} async-done(((bf16[128,4096]{1,0:T(8,128)(2,1)}), bf16[512,4096]{1,0:T(8,128)(2,1)}) %all-gather.5.cloned.1.call-update) | async-done | bytes 4194320 | tf_op jit(solution)/shard_map/all_gather | solution.py:811
  156.8 0.9 collective-permute-start.7
  157.8 0.3 collective-permute-start.8
  158.0 1.8 collective-permute-start.6
  159.8 11.5 %recomputed.1 = (f32[4,24,64,256]{3,2,1,0:T(8,128)}, bf16[8,256,384]{2,1,0:T(8,128)(2,1)}) custom-call(s32[4,24]{1,0:T(4,128)} %pad_add_fusion.index_ref, s32[1]{0:T(128)} %bitcast.6.run_ref, bf16[24,256,384]{2,1,0:T(8,128)(2,1)} %get-tuple-element.51.refs_0_.refs_1_.refs_2_, bf16[24,256,384]{2,1,0:T(8,128)(2,1)} %get-tuple-element.51.refs_0_.refs_1_.refs_2_, ...), custom_call_target="tpu_custom_call" | custom-call | bytes 20761804 | tf_op jit(solution)/shard_map/recomputed/pallas_call | solution.py:597
  171.3 9.0 %down_gradient_split.1.refs_3_ = f32[1536,1536]{1,0:T(8,128)} custom-call(s32[1]{0:T(128)} %bitcast.6.run_ref, bf16[512,4096]{1,0:T(8,128)(2,1)} %all-gather.5.cloned.1.call-done.refs_4_.mixed_ref, bf16[8,256,384]{2,1,0:T(8,128)(2,1)} %get-tuple-element.55.act_ref, bf16[128,6144]{1,0:T(8,128)(2,1)} %get-tuple-element.31.act_ref.own_act_ref, ...), custom_call_target="tpu_custom_call" | custom-call | bytes 27682406 | tf_op jit(solution)/shard_map/down_gradient_split/pallas_call | solution.py:719
  180.3 11.8 %mix_gradient.1.refs_4_ = f32[4,24,64,256]{3,2,1,0:T(8,128)} custom-call(s32[24]{0:T(128)} %dynamic-slice_subtract_fusion.1.perm_ref, bf16[512,4096]{1,0:T(8,128)(2,1)} %all-gather.5.cloned.1.call-done.refs_4_.mixed_ref, bf16[512,4096]{1,0:T(8,128)(2,1)} %get-tuple-element.49.grad_ref, ...), custom_call_target="tpu_custom_call", output_to_operand_aliasing={{}: (6, {})} | custom-call | bytes 18454936 | tf_op jit(solution)/shard_map/mix_gradient/pallas_call | solution.py:513
  192.2 0.7 copy-done.5
  192.9 0.1 copy-done.6
  193.0 0.2 copy-done.7
  193.2 7.7 %up_gradient.1 = f32[1536,1536]{1,0:T(8,128)} custom-call(s32[4]{0:T(128)} %and_select_fusion.1.run_ref, bf16[512,3072]{1,0:T(8,128)(2,1)} %all-gather.3.cloned.1.call-done.all_ref.inputs_ref.right_ref, bf16[128,1536]{1,0:T(8,128)(2,1)} %get-tuple-element.41.refs_0_, bf16[128,1536]{1,0:T(8,128)(2,1)} %copy-done.7, bf16[128,1536]{1,0:T(8,128)(2,1)} %copy-done.5, ...), custom_call_target="tpu_custom_call" | custom-call | bytes 27682406 | tf_op jit(solution)/shard_map/up_gradient/pallas_call | solution.py:647
  (31 shorter events, 0.1 us)
Async XLA Ops:
  7.2 71.8 %all-gather.3.cloned.1.call-start = ((), (), s32[]{:S(2)}) async-start(), calls=%async_computation | async-start | bytes 3932160 | tf_op jit(solution)/shard_map/all_gather | solution.py:798
  9.3 147.5 %all-gather.5.cloned.1.call-start = ((), (), s32[]{:S(2)}) async-start(), calls=%async_computation.1 | async-start | bytes 5242880 | tf_op jit(solution)/shard_map/all_gather | solution.py:811
  9.4 12.1 %copy-start.10 = (s32[96]{0:T(128)S(1)}, s32[96]{0:T(128)}, u32[]{:S(2)}) copy-start(s32[96]{0:T(128)} %param.13) | copy-start | bytes 1156
  9.4 12.1 %copy-start.9 = (s32[2,96]{1,0:T(2,128)S(1)}, s32[2,96]{1,0:T(2,128)}, u32[]{:S(2)}) copy-start(s32[2,96]{1,0:T(2,128)} %param.12) | copy-start | bytes 2308
  18.4 4.3 %collective-permute-start.1 = (bf16[128,6144]{1,0:T(8,128)(2,1)}, bf16[128,6144]{1,0:T(8,128)(2,1)S(1)}, u32[]{:S(2)}, u32[]{:S(2)}) collective-permute-start(bf16[128,6144]{1,0:T(8,128)(2,1)} %dense.1.refs_0_.refs_5_.refs_6_.refs_7_.refs_8_), channel_id=1, source_target_pairs={{0,4},{4,0},{8,12},{12,8},{1,5},{5,1},{9,13},{13,9},{2,6},{6,2},{1... | collective-permute-start | bytes 4718600 | tf_op jit(solution)/shard_map/ppermute | solution.py:20
  18.8 37.8 %collective-permute-start = (bf16[128,6144]{1,0:T(8,128)(2,1)}, bf16[128,6144]{1,0:T(8,128)(2,1)S(1)}, u32[]{:S(2)}, u32[]{:S(2)}) collective-permute-start(bf16[128,6144]{1,0:T(8,128)(2,1)} %dense.1.refs_0_.refs_5_.refs_6_.refs_7_.refs_8_), channel_id=1, source_target_pairs={{0,8},{4,12},{8,0},{12,4},{1,9},{5,13},{9,1},{13,5},{2,10},{6,14},... | collective-permute-start | bytes 4718600 | tf_op jit(solution)/shard_map/ppermute | solution.py:20
  21.6 13.5 %copy-start.8 = (s32[2,24]{1,0:T(2,128)}, s32[2,24]{1,0:T(2,128)S(1)}, u32[]{:S(2)}) copy-start(s32[2,24]{1,0:T(2,128)S(1)} %dynamic-slice_subtract_fusion.target_ref) | copy-start | bytes 580
  22.7 1.2 copy-start
  56.6 1.2 copy-start.1
  75.8 16.5 %collective-permute-start.2 = (bf16[128,6144]{1,0:T(8,128)(2,1)}, bf16[128,6144]{1,0:T(8,128)(2,1)S(1)}, u32[]{:S(2)}, u32[]{:S(2)}) collective-permute-start(bf16[128,6144]{1,0:T(8,128)(2,1)} %get-tuple-element.33.refs_0_), channel_id=1, source_target_pairs={{0,4},{4,0},{8,12},{12,8},{1,5},{5,1},{9,13},{13,9},{2,6},{6,2},{1... | collective-permute-start | bytes 4718600 | tf_op jit(solution)/shard_map/ppermute | solution.py:20
  77.2 38.9 %collective-permute-start.3 = (bf16[128,6144]{1,0:T(8,128)(2,1)}, bf16[128,6144]{1,0:T(8,128)(2,1)}, u32[]{:S(2)}, u32[]{:S(2)}) collective-permute-start(bf16[128,6144]{1,0:T(8,128)(2,1)} %get-tuple-element.35), channel_id=1, source_target_pairs={{0,8},{4,12},{8,0},{12,4},{1,9},{5,13},{9,1},{13,5},{2,10},{6,14},... | collective-permute-start | bytes 4718600 | tf_op jit(solution)/shard_map/ppermute | solution.py:20
  92.3 1.1 copy-start.2
  112.6 5.2 %collective-permute-start.5 = (bf16[2048,384]{1,0:T(8,128)(2,1)}, bf16[2048,384]{1,0:T(8,128)(2,1)S(1)}, u32[]{:S(2)}, u32[]{:S(2)}) collective-permute-start(bf16[2048,384]{1,0:T(8,128)(2,1)} %get-tuple-element.38), channel_id=1, source_target_pairs={{0,4},{4,0},{8,12},{12,8},{1,5},{5,1},{9,13},{13,9},{2,6},{6,2},{1... | collective-permute-start | bytes 4718600 | tf_op jit(solution)/shard_map/ppermute | solution.py:20
  112.9 46.9 %collective-permute-start.10 = (bf16[2048,384]{1,0:T(8,128)(2,1)}, bf16[2048,384]{1,0:T(8,128)(2,1)}, u32[]{:S(2)}, u32[]{:S(2)}) collective-permute-start(bf16[2048,384]{1,0:T(8,128)(2,1)} %get-tuple-element.52), channel_id=1, source_target_pairs={{0,8},{4,12},{8,0},{12,4},{1,9},{5,13},{9,1},{13,5},{2,10},{6,14},... | collective-permute-start | bytes 4718600 | tf_op jit(solution)/shard_map/ppermute | solution.py:20
  113.3 4.5 %collective-permute-start.4 = (bf16[1024,512]{1,0:T(8,128)(2,1)}, bf16[1024,512]{1,0:T(8,128)(2,1)S(1)}, u32[]{:S(2)}, u32[]{:S(2)}) collective-permute-start(bf16[1024,512]{1,0:T(8,128)(2,1)} %get-tuple-element.37), channel_id=1, source_target_pairs={{0,4},{4,0},{8,12},{12,8},{1,5},{5,1},{9,13},{13,9},{2,6},{6,2},{1... | collective-permute-start | bytes 3145736 | tf_op jit(solution)/shard_map/ppermute | solution.py:20
  113.4 67.0 %collective-permute-start.9 = (bf16[1024,512]{1,0:T(8,128)(2,1)}, bf16[1024,512]{1,0:T(8,128)(2,1)}, u32[]{:S(2)}, u32[]{:S(2)}) collective-permute-start(bf16[1024,512]{1,0:T(8,128)(2,1)} %get-tuple-element.50), channel_id=1, source_target_pairs={{0,8},{4,12},{8,0},{12,4},{1,9},{5,13},{9,1},{13,5},{2,10},{6,14},... | collective-permute-start | bytes 3145736 | tf_op jit(solution)/shard_map/ppermute | solution.py:20
  117.8 1.0 copy-start.4
  117.8 1.6 copy-start.3
  156.8 35.3 %collective-permute-start.7 = (bf16[128,1536]{1,0:T(8,128)(2,1)}, bf16[128,1536]{1,0:T(8,128)(2,1)S(1)}, u32[]{:S(2)}, u32[]{:S(2)}) collective-permute-start(bf16[128,1536]{1,0:T(8,128)(2,1)} %get-tuple-element.47), channel_id=1, source_target_pairs={{0,2},{1,3},{2,0},{3,1},{4,6},{5,7},{6,4},{7,5},{8,10},{9,11},{10,... | collective-permute-start | bytes 1179656 | tf_op jit(solution)/shard_map/ppermute | solution.py:25
  157.8 34.4 %collective-permute-start.8 = (bf16[128,1536]{1,0:T(8,128)(2,1)}, bf16[128,1536]{1,0:T(8,128)(2,1)S(1)}, u32[]{:S(2)}, u32[]{:S(2)}) collective-permute-start(bf16[128,1536]{1,0:T(8,128)(2,1)} %get-tuple-element.48), channel_id=1, source_target_pairs={{0,3},{1,0},{2,1},{3,2},{4,7},{5,4},{6,5},{7,6},{8,11},{9,8},{10,9... | collective-permute-start | bytes 1179656 | tf_op jit(solution)/shard_map/ppermute | solution.py:25
  158.0 34.1 %collective-permute-start.6 = (bf16[128,1536]{1,0:T(8,128)(2,1)}, bf16[128,1536]{1,0:T(8,128)(2,1)S(1)}, u32[]{:S(2)}, u32[]{:S(2)}) collective-permute-start(bf16[128,1536]{1,0:T(8,128)(2,1)} %get-tuple-element.46.refs_19_), channel_id=1, source_target_pairs={{0,1},{1,2},{2,3},{3,0},{4,5},{5,6},{6,7},{7,4},{8,9},{9,10},{10,1... | collective-permute-start | bytes 1179656 | tf_op jit(solution)/shard_map/ppermute | solution.py:25
  192.1 0.8 copy-start.5
  192.1 0.9 copy-start.6
  192.2 1.0 copy-start.7
Sparse Core Ops, SparseCore 0:
  9.6 66.1 all-gather.2
  77.4 79.3 all-gather.4
